TPU v7x, 128 devices: a whole 4x4x4 slice. The times are simulated.
128 devices in a mesh: pts: 32 (over z, x, core), exp: 4 (over y).
Axes of the slice: x: 4, y: 4, z: 4, core: 2. Of those that a mesh axis runs over, the one named last changes fastest.
Arguments:
- tokens: bfloat16 [32768, 256], P('pts'), may hold values from -6 to 6
- coords: float32 [3, 32768], P(None, 'pts'), may hold values from -1 to 1
- keep: int32 [32768], P('pts'), may hold values 0 or 1
- cotangent: bfloat16 [32768, 256], P('pts'), may hold values from -6 to 6
- w_query: bfloat16 [256, 256], replicated, may hold values from -0.375 to 0.375
- w_key: bfloat16 [256, 256], replicated, may hold values from -0.375 to 0.375
- w_value: bfloat16 [256, 256], replicated, may hold values from -0.375 to 0.375
- w_geo: float32 [3, 64], replicated, may hold values from -3.5 to 3.5
- b_geo: float32 [64], replicated, may hold values from -1 to 1
- w_route: float32 [64, 8], replicated, may hold values from -0.25 to 0.25
- w_in: bfloat16 [8, 256, 1024], P('exp'), may hold values from -0.375 to 0.375
- w_out: bfloat16 [8, 1024, 256], P('exp'), may hold values from -0.1875 to 0.1875
Outputs:
- grad_x: bfloat16 [32768, 256], P('pts')
- grad_wq: float32 [256, 256], replicated
- grad_wk: float32 [256, 256], replicated
- grad_wv: float32 [256, 256], replicated
- grad_w_in: float32 [8, 256, 1024], P('exp')
- grad_w_out: float32 [8, 1024, 256], P('exp')
- grad_route: float32 [64, 8], P(None, 'exp')
All inputs are finite; a program needn't handle non-finite values. No bound on the sum of `keep` on one device may be relied on, other than what follows from the above.
Results may differ from a plain program's by a relative error of at most 0.0064.
Values may be sent and summed in bfloat16 or wider, within the bound.
No kernel may reach another device: no remote copies, remote signals or barrier semaphores. Data moves between devices by JAX's collectives and lax.ppermute only.
A program may use at most 128 MiB of HBM per device.

v0:
```python
import jax
import jax.numpy as jnp
from jax import lax
from jax.sharding import PartitionSpec as P

HEADS = 8


HIGH = lax.Precision.HIGHEST


def phi(z):
    return jnp.where(z > 0, z + 1.0, jnp.exp(jnp.minimum(z, 0.0)))


def phi_slope(z):
    return jnp.where(z > 0, 1.0, jnp.exp(jnp.minimum(z, 0.0)))


def gelu_tanh(u):
    return jax.nn.gelu(u, approximate=True)


def attend_local(tokens, keepf, w_query, w_key, w_value):
    count = tokens.shape[0]
    heads = HEADS
    head_dim = tokens.shape[1] // heads
    qpre = jnp.dot(tokens, w_query, preferred_element_type=jnp.float32)
    kpre = jnp.dot(tokens, w_key, preferred_element_type=jnp.float32)
    vpre = jnp.dot(tokens, w_value, preferred_element_type=jnp.float32)
    query = phi(qpre).astype(jnp.bfloat16).reshape(count, heads, head_dim)
    keyed = (phi(kpre) * keepf[:, None]).astype(jnp.bfloat16).reshape(count, heads, head_dim)
    value = vpre.astype(jnp.bfloat16).reshape(count, heads, head_dim)
    kv_part = jnp.einsum("thi,thj->hij", keyed, value, preferred_element_type=jnp.float32)
    ks_part = jnp.sum(keyed.astype(jnp.float32), axis=0)
    return (qpre, kpre, query, keyed, value, kv_part, ks_part)


def attend_finish(tokens, query, kv, ks):
    count = tokens.shape[0]
    qf = query.astype(jnp.float32)
    num = jnp.einsum("thi,hij->thj", qf, kv, precision=HIGH)
    den = jnp.einsum("thi,hi->th", qf, ks, precision=HIGH)
    attn = num / den[..., None]
    mid = (tokens.astype(jnp.float32) + attn.reshape(count, tokens.shape[1])).astype(jnp.bfloat16)
    return (attn, den, mid)


def attend_back_local(dmid, attn, den, query):
    count = dmid.shape[0]
    qf = query.astype(jnp.float32)
    dmh = dmid.reshape(count, HEADS, dmid.shape[1] // HEADS)
    dnum = dmh / den[..., None]
    dden = -jnp.sum(dmh * attn, axis=-1) / den
    dkv_part = jnp.einsum("thi,thj->hij", qf, dnum, precision=HIGH)
    dks_part = jnp.einsum("th,thi->hi", dden, qf, precision=HIGH)
    return (dnum, dden, dkv_part, dks_part)


def attend_back_finish(
    tokens,
    keepf,
    dmid,
    qpre,
    kpre,
    keyed,
    value,
    kv,
    ks,
    dnum,
    dden,
    dkv,
    dks,
    w_query,
    w_key,
    w_value,
):
    count = tokens.shape[0]
    width = tokens.shape[1]
    dq = jnp.einsum("thj,hij->thi", dnum, kv, precision=HIGH) + dden[..., None] * ks[None]
    dk = (
        jnp.einsum("thj,hij->thi", value.astype(jnp.float32), dkv, precision=HIGH) + dks[None]
    ) * keepf[:, None, None]
    dv = jnp.einsum("thi,hij->thj", keyed.astype(jnp.float32), dkv, precision=HIGH)
    dqp = (dq.reshape(count, width) * phi_slope(qpre)).astype(jnp.bfloat16)
    dkp = (dk.reshape(count, width) * phi_slope(kpre)).astype(jnp.bfloat16)
    dvp = dv.reshape(count, width).astype(jnp.bfloat16)
    gq = jnp.dot(tokens.T, dqp, preferred_element_type=jnp.float32)
    gk = jnp.dot(tokens.T, dkp, preferred_element_type=jnp.float32)
    gv = jnp.dot(tokens.T, dvp, preferred_element_type=jnp.float32)
    back = jnp.dot(dqp, w_query.T, preferred_element_type=jnp.float32)
    back = back + jnp.dot(dkp, w_key.T, preferred_element_type=jnp.float32)
    back = back + jnp.dot(dvp, w_value.T, preferred_element_type=jnp.float32)
    return (gq, gk, gv, (dmid + back).astype(jnp.bfloat16))


def on_device(
    tokens, coords, keep, cotangent, w_query, w_key, w_value, w_geo, b_geo, w_route, w_in, w_out
):
    rows = tokens.shape[0]
    exp_local = w_in.shape[0]
    keepf = keep.astype(jnp.float32)
    dyv = cotangent * keep[:, None].astype(jnp.bfloat16)
    dyf = dyv.astype(jnp.float32)
    hidden_geo = jnp.tanh(jnp.dot(coords.T, w_geo, precision=HIGH) + b_geo[None, :])
    expo = jnp.exp(jnp.dot(hidden_geo, w_route, precision=HIGH))
    gates_all = expo / jnp.sum(expo, axis=1, keepdims=True)
    first = lax.axis_index("exp") * exp_local
    gates = lax.dynamic_slice_in_dim(gates_all, first, exp_local, 1)
    qpre, kpre, query, keyed, value, kv_part, ks_part = attend_local(
        tokens, keepf, w_query, w_key, w_value
    )
    kv, ks = lax.psum((kv_part, ks_part), "pts")
    attn, den, mid = attend_finish(tokens, query, kv, ks)
    partial_value = jnp.zeros((rows, tokens.shape[1]), jnp.float32)
    dg_cols = []
    gw1_list = []
    gw2_list = []
    for expert in range(exp_local):
        upre = jnp.dot(mid, w_in[expert], preferred_element_type=jnp.float32)
        act, pull = jax.vjp(gelu_tanh, upre)
        act_b = act.astype(jnp.bfloat16)
        outf = jnp.dot(act_b, w_out[expert], preferred_element_type=jnp.float32)
        dg_cols.append(jnp.sum(dyf * outf, axis=1))
        dfe = (gates[:, expert : expert + 1] * dyf).astype(jnp.bfloat16)
        gw2_list.append(jnp.dot(act_b.T, dfe, preferred_element_type=jnp.float32))
        dact = jnp.dot(dfe, w_out[expert].T, preferred_element_type=jnp.float32)
        due = pull(dact)[0].astype(jnp.bfloat16)
        gw1_list.append(jnp.dot(mid.T, due, preferred_element_type=jnp.float32))
        partial_value = partial_value + jnp.dot(
            due, w_in[expert].T, preferred_element_type=jnp.float32
        )
    dgate = jnp.stack(dg_cols, axis=1)
    gate_part = jnp.sum(gates * dgate, axis=1)
    mixed, gsum = lax.psum((partial_value, gate_part), "exp")
    dmid = mixed + dyf
    dlogit = gates * (dgate - gsum[:, None])
    route_part = jnp.dot(hidden_geo.T, dlogit, precision=HIGH)
    grad_w_in, grad_w_out, grad_route = lax.psum(
        (jnp.stack(gw1_list), jnp.stack(gw2_list), route_part), "pts"
    )
    dnum, dden, dkv_part, dks_part = attend_back_local(dmid, attn, den, query)
    dkv, dks = lax.psum((dkv_part, dks_part), "pts")
    gq, gk, gv, dx_att = attend_back_finish(
        tokens,
        keepf,
        dmid,
        qpre,
        kpre,
        keyed,
        value,
        kv,
        ks,
        dnum,
        dden,
        dkv,
        dks,
        w_query,
        w_key,
        w_value,
    )
    grad_wq, grad_wk, grad_wv = lax.psum((gq, gk, gv), "pts")
    return (dx_att, grad_wq, grad_wk, grad_wv, grad_w_in, grad_w_out, grad_route)


def solution(mesh):
    in_specs = (
        P("pts", None),
        P(None, "pts"),
        P("pts"),
        P("pts", None),
        P(),
        P(),
        P(),
        P(),
        P(),
        P(),
        P("exp", None, None),
        P("exp", None, None),
    )
    out_specs = (
        P("pts", None),
        P(),
        P(),
        P(),
        P("exp", None, None),
        P("exp", None, None),
        P(None, "exp"),
    )
    return jax.shard_map(
        on_device, mesh=mesh, in_specs=in_specs, out_specs=out_specs, check_vma=False
    )
```

profile of v0, /device:TPU:1, one launch (start us, length us, event | category | flops | bytes accessed | tf_op | source)
XLA Modules:
  0.0 491.2 jit_solution(5247567044801425763)
XLA Ops:
  9.4 2.7 convert_reduce_fusion
  12.2 2.6 select_convert_fusion
  15.1 126.8 %all-reduce.1 = (f32[8,32,32]{2,1,0:T(8,128)S(1)}, f32[8,32]{1,0:T(8,128)S(1)}) all-reduce(f32[8,32,32]{2,1,0:T(8,128)S(1)} %fusion.60, f32[8,32]{1,0:T(8,128)S(1)} %reduce_sum.58), channel_id=1, replica_groups=mesh['pts'=32,'exp'=4] {'pts'}, use_global_device_ids=true, to_apply=%region_1.2 | all-reduce | flops 8448 | bytes 67584 | tf_op jit(solution)/shard_map/psum | solution.py:113
  144.0 4.5 multiply_convert_fusion.1
  148.5 3.4 multiply_convert_fusion
  156.1 5.4 %fusion.6 = bf16[1024,1024]{1,0:T(8,128)(2,1)S(1)} fusion(f32[1024,1024]{1,0:T(8,128)} %get-tuple-element.38, bf16[2,1024,256]{2,1,0:T(8,128)(2,1)} %param.23, f32[1024]{0:T(1024)S(1)} %bitcast.153, bf16[1024,256]{1,0:T(8,128)(2,1)} %param.15, bf16[1024]{0:T(1024)(128)(2,1)S(1)} %get-tuple-element.30), kind=kOutput, calls=%fused_computation.10 | convolution fusion | flops 558891008 | bytes 7346176 | tf_op jit(solution)/shard_map/dot_general | solution.py:127
  164.9 3.8 fusion.13
  168.7 1.7 convolution_add_fusion.3
  170.7 3.9 convolution_bitcast_fusion
  174.6 2.1 convolution_bitcast_fusion.1
  176.7 9.7 %psum.94 = f32[1024]{0:T(1024)S(1)} all-reduce(f32[1024]{0:T(1024)} %get-tuple-element.24), channel_id=1, replica_groups=mesh['pts'=32,'exp'=4] {'exp'}, use_global_device_ids=true, to_apply=%region_16.17 | all-reduce | flops 1024 | bytes 8192 | tf_op jit(solution)/shard_map/psum | solution.py:135
  186.4 3.2 pad_maximum_fusion.1
  193.4 23.1 %all-reduce.6.cloned.1.call-done = f32[1024,256]{1,0:T(8,128)} async-done(((f32[1024,256]{1,0:T(8,128)}), f32[1024,256]{1,0:T(8,128)}) %all-reduce.6.cloned.1.call-update) | async-done | bytes 1048592 | tf_op jit(solution)/shard_map/psum | solution.py:135
  216.5 1.6 convert_add_fusion
  221.0 1.9 fusion.45
  223.0 2.0 fusion.16
  225.5 125.3 %all-reduce = (f32[8,32,32]{2,1,0:T(8,128)S(1)}, f32[8,32]{1,0:T(8,128)S(1)}, f32[64,2]{0,1:T(2,128)}) all-reduce(f32[8,32,32]{2,1,0:T(8,128)S(1)} %fusion.45, f32[8,32]{1,0:T(8,128)S(1)} %bitcast.152, f32[64,2]{0,1:T(2,128)S(1)} %copy-done.33), channel_id=1, replica_groups=mesh['pts'=32,'exp'=4] {'pts'}, use_global_device_ids=true, to_apply=%region_6.7 | all-reduce | flops 8576 | bytes 68608 | tf_op jit(solution)/shard_map/psum | solution.py:143
  350.8 1.7 convolution_convert_fusion
  356.6 1.8 fusion.25
  361.4 112.9 %all-reduce.8.cloned.1.call-done = (f32[256,256]{0,1:T(8,128)}, f32[256,256]{0,1:T(8,128)}, f32[256,256]{0,1:T(8,128)}, f32[2,256,1024]{2,1,0:T(8,128)}, f32[2,1024,256]{2,1,0:T(8,128)}) async-done(((f32[256,256]{0,1:T(8,128)}, f32[256,256]{0,1:T(8,128)}, f32[256,256]{0,1:T(8,128)}, f32[2,256,1024]{2,1,0:T(8,128)}, f32[2,1024,256]{2,1,0:T(8,128)}), (f32[256,256]{0,1:T(8,128)}, f32[256,256]{0,1:T(8,128)}, ...) | async-done | bytes 4980752 | tf_op jit(solution)/shard_map/psum | solution.py:162
  474.3 1.9 copy.25
  476.3 1.8 copy.26
  478.1 1.8 copy.27
  479.8 3.2 copy.48
  (131 shorter events, 27.9 us)
Async XLA Ops:
  7.2 209.3 %all-reduce.6.cloned.1.call-start = ((), (), s32[]{:S(2)}) async-start(), calls=%async_computation | async-start | bytes 2097152 | tf_op jit(solution)/shard_map/psum | solution.py:135
  8.0 166.6 %copy-start.29 = (bf16[1024]{0:T(1024)(128)(2,1)}, bf16[1024]{0:T(1024)(128)(2,1)S(1)}, u32[]{:S(2)}) copy-start(bf16[1024]{0:T(1024)(128)(2,1)S(1)} %get-tuple-element.30) | copy-start | bytes 6148
  9.4 134.1 %copy-start.2 = (bf16[1024,256]{0,1:T(8,128)(2,1)}, bf16[1024,256]{0,1:T(8,128)(2,1)S(1)}, u32[]{:S(2)}) copy-start(bf16[1024,256]{0,1:T(8,128)(2,1)S(1)} %convolution_convert_fusion.1) | copy-start | bytes 1572868
  12.1 130.1 %copy-start.12 = (bf16[1024,256]{0,1:T(8,128)(2,1)}, bf16[1024,256]{0,1:T(8,128)(2,1)S(1)}, u32[]{:S(2)}) copy-start(bf16[1024,256]{0,1:T(8,128)(2,1)S(1)} %get-tuple-element.27) | copy-start | bytes 1572868
  14.8 128.7 %copy-start.9 = (bf16[1024,256]{0,1:T(8,128)(2,1)}, bf16[1024,256]{0,1:T(8,128)(2,1)S(1)}, u32[]{:S(2)}) copy-start(bf16[1024,256]{0,1:T(8,128)(2,1)S(1)} %get-tuple-element.33) | copy-start | bytes 1572868
  14.8 129.1 %copy-start.1 = (bf16[1024,256]{1,0:T(8,128)(2,1)S(1)}, bf16[1024,256]{1,0:T(8,128)(2,1)}, u32[]{:S(2)}) copy-start(bf16[1024,256]{1,0:T(8,128)(2,1)} %param.12) | copy-start | bytes 1572868
  143.5 5.0 %copy-start.4 = (f32[1024,8,32]{0,2,1:T(8,128)}, f32[1024,8,32]{0,2,1:T(8,128)S(1)}, u32[]{:S(2)}) copy-start(f32[1024,8,32]{0,2,1:T(8,128)S(1)} %fusion.17) | copy-start | bytes 3145732
  144.0 4.5 copy-start.20
  155.5 7.3 %copy-start.36 = (f32[1024,1]{0,1:T(1,128)}, f32[1024,1]{0,1:T(1,128)S(1)}, u32[]{:S(2)}) copy-start(f32[1024,1]{0,1:T(1,128)S(1)} %get-tuple-element.28) | copy-start | bytes 12292
  156.1 5.4 %copy-start.21 = (bf16[2,256,1024]{2,1,0:T(8,128)(2,1)S(1)}, bf16[2,256,1024]{2,1,0:T(8,128)(2,1)}, u32[]{:S(2)}) copy-start(bf16[2,256,1024]{2,1,0:T(8,128)(2,1)} %param.22) | copy-start | bytes 3145732
  170.4 303.9 %all-reduce.8.cloned.1.call-start = ((), (), s32[]{:S(2)}) async-start(), calls=%async_computation.1 | async-start | bytes 9961472 | tf_op jit(solution)/shard_map/psum | solution.py:162
  170.7 3.9 copy-start.16
  170.7 3.9 copy-start.35
  170.7 3.9 copy-start.44
  186.4 3.9 copy-start.8
  191.0 28.4 %copy-start.5 = (f32[1024,8,32]{0,2,1:T(8,128)S(1)}, f32[1024,8,32]{0,2,1:T(8,128)}, u32[]{:S(2)}) copy-start(f32[1024,8,32]{0,2,1:T(8,128)} %copy-done.4) | copy-start | bytes 3145732
  192.5 28.5 %copy-start.10 = (bf16[1024,256]{0,1:T(8,128)(2,1)S(1)}, bf16[1024,256]{0,1:T(8,128)(2,1)}, u32[]{:S(2)}) copy-start(bf16[1024,256]{0,1:T(8,128)(2,1)} %copy-done.9) | copy-start | bytes 1572868
  193.4 27.6 %copy-start.23 = (f32[8,1,1024]{2,0,1:T(8,128)S(1)}, f32[8,1,1024]{2,0,1:T(8,128)}, u32[]{:S(2)}) copy-start(f32[8,1,1024]{2,0,1:T(8,128)} %copy-done.22) | copy-start | bytes 98308
  218.1 4.9 copy-start.19
  218.1 4.9 copy-start.32
  218.1 4.9 copy-start.42
  221.0 4.5 copy-start.33
  222.9 130.5 %copy-start.3 = (bf16[1024,256]{0,1:T(8,128)(2,1)S(1)}, bf16[1024,256]{0,1:T(8,128)(2,1)}, u32[]{:S(2)}) copy-start(bf16[1024,256]{0,1:T(8,128)(2,1)} %copy-done.2) | copy-start | bytes 1572868
  474.3 8.7 %copy-start.11 = (f32[2,1024,256]{2,1,0:T(8,128)S(1)}, f32[2,1024,256]{2,1,0:T(8,128)}, u32[]{:S(2)}) copy-start(f32[2,1024,256]{2,1,0:T(8,128)} %get-tuple-element.46) | copy-start | bytes 6291460
  (25 other events, 47.8 us)
Sparse Core Ops, SparseCore 0:
  170.6 45.8 all-reduce.5
  359.5 114.7 all-reduce.7
where the time goes:
time: 492 us; the launch traced here: 491 us
  blocking collectives  262 us (53%)
  waiting for transfers between devices  136 us (28%)
  matrix products  49.6 us (10%)
  local copies, waits for them, and re-layouts  16.3 us (3%)
  between operations  14.7 us (3%)
  other arithmetic  12.6 us (3%)
    psum x1, blocking collectives, on_device(): kv, ks = lax.psum((kv_part, ks_part), 'pts')  127 us
    psum x1, blocking collectives, on_device(): dkv, dks = lax.psum((dkv_part, dks_part), 'pts')  125 us
    psum x1, waiting for transfers between devices, on_device(): grad_wq, grad_wk, grad_wv = lax.psum((gq, gk, gv), 'pts')  113 us
    psum x1, waiting for transfers between devices, on_device(): mixed, gsum = lax.psum((partial_value, gate_part), 'exp')  23.1 us
    unnamed x99, local copies, waits for them, and re-layouts  14.5 us
  transfers between devices with their start and end apart: 2, of which 2 were waited for; matrix products, arithmetic and copies ran while one was open for 3% of the time, Pallas kernels for 0%

commit v1 on v0

v1 whole, which is shorter than its diff:
```python
import functools

import jax
import jax.numpy as jnp
from jax import lax
from jax.experimental import pallas as pl
from jax.experimental.pallas import tpu as pltpu
from jax.sharding import PartitionSpec as P


D = 256
HD = 32
FH = 1024
N1 = 1024
N2 = 2048
TB = 512
HC = 256
F32 = jnp.float32
BF = jnp.bfloat16
VMEM_LIMIT = 60 * 1024 * 1024


def mm(a, b):
    return jnp.dot(a, b, preferred_element_type=F32)


def mm_nt(a, b):
    return lax.dot_general(a, b, (((1,), (1,)), ((), ())), preferred_element_type=F32)


def split2(x):
    hi = x.astype(BF)
    return hi, (x - hi.astype(F32)).astype(BF)


def flip(x):
    return x.astype(F32).T


def head_mask(rows, cols):
    r = lax.broadcasted_iota(jnp.int32, (rows, cols), 0) // HD
    c = lax.broadcasted_iota(jnp.int32, (rows, cols), 1) // HD
    return r == c


def pack_heads(full):
    full = jnp.where(head_mask(D, D), full, 0.0)
    parts = []
    for g in range(2):
        cols = full[:, 128 * g : 128 * g + 128]
        parts.append(sum(cols[128 * g + HD * h : 128 * g + HD * h + HD] for h in range(4)))
    return parts


def unpack_heads(packed):
    mask = head_mask(128, 128)
    zero = jnp.zeros((128, 128), F32)
    blocks = []
    for g in range(2):
        piece = packed[HD * g : HD * g + HD]
        blocks.append(jnp.where(mask, jnp.concatenate([piece] * 4, axis=0), 0.0))
    top = jnp.concatenate([blocks[0], zero], axis=1)
    low = jnp.concatenate([zero, blocks[1]], axis=1)
    return jnp.concatenate([top, low], axis=0)


def row_of(packed, first):
    return jnp.concatenate([packed[first : first + 8], packed[first + 8 : first + 16]], axis=1)


def as_column(row):
    r = lax.broadcasted_iota(jnp.int32, (D, D), 0)
    c = lax.broadcasted_iota(jnp.int32, (D, D), 1)
    return jnp.sum(jnp.where(r == c, row, 0.0), axis=1, keepdims=True)


def params():
    return pltpu.CompilerParams(vmem_limit_bytes=VMEM_LIMIT)


def cost(flops, nbytes):
    return pl.CostEstimate(flops=int(flops), bytes_accessed=int(nbytes), transcendentals=0)


def keys_kernel(tok_ref, keep_ref, wk_ref, wv_ref, km_ref, v_ref, slope_ref, msg_ref):
    tok = tok_ref[...]
    kpre = mm_nt(flip(wk_ref[...]).astype(BF), tok)
    val = mm_nt(flip(wv_ref[...]).astype(BF), tok).astype(BF)
    keep = keep_ref[...].astype(F32)
    low = jnp.exp(jnp.minimum(kpre, 0.0))
    km = (keep * jnp.where(kpre > 0, kpre + 1.0, low)).astype(BF)
    km_ref[...] = km
    v_ref[...] = val
    slope_ref[...] = keep * jnp.where(kpre > 0, 1.0, low)
    parts = pack_heads(mm_nt(val, km))
    msg_ref[0:32, :] = parts[0]
    msg_ref[32:64, :] = parts[1]
    ks = mm_nt(jnp.ones((8, N1), BF), km)
    msg_ref[64:72, :] = ks[:, :128]
    msg_ref[72:80, :] = ks[:, 128:]


def keys_call(tokens, keep_row, wk, wv):
    return pl.pallas_call(
        keys_kernel,
        out_shape=(
            jax.ShapeDtypeStruct((D, N1), BF),
            jax.ShapeDtypeStruct((D, N1), BF),
            jax.ShapeDtypeStruct((D, N1), F32),
            jax.ShapeDtypeStruct((80, 128), F32),
        ),
        compiler_params=params(),
        cost_estimate=cost(4e8, 3e6),
        name="keys",
    )(tokens, keep_row, wk, wv)


def query_kernel(tok_ref, oth_ref, wq_ref, tokt_ref, q_ref):
    wqt = flip(wq_ref[...]).astype(BF)
    for half, ref in enumerate((tok_ref, oth_ref)):
        tok = ref[...]
        cols = slice(N1 * half, N1 * half + N1)
        tokt_ref[:, cols] = flip(tok).astype(BF)
        pre = mm_nt(wqt, tok)
        phi = jnp.where(pre > 0, pre + 1.0, jnp.exp(jnp.minimum(pre, 0.0)))
        q_ref[:, cols] = phi.astype(BF)


def query_call(tokens, tokens_o, wq):
    return pl.pallas_call(
        query_kernel,
        out_shape=(jax.ShapeDtypeStruct((D, N2), BF), jax.ShapeDtypeStruct((D, N2), BF)),
        compiler_params=params(),
        cost_estimate=cost(4e8, 3e6),
        name="queries",
    )(tokens, tokens_o, wq)


def back_kernel(at_ref, cot_ref, oth_ref, ck_ref, cko_ref, win_ref, wout_ref, dyt_ref, back_ref, wint_ref):
    for half, (ref, keep_ref) in enumerate(((cot_ref, ck_ref), (oth_ref, cko_ref))):
        cot = ref[...]
        keep = keep_ref[3:4, :]
        cols = slice(N1 * half, N1 * half + N1)
        dyt_ref[:, cols] = (flip(cot) * keep).astype(BF)
        for j in range(0, FH, HC):
            back_ref[j : j + HC, cols] = (mm_nt(wout_ref[0, j : j + HC, :], cot) * keep).astype(BF)
    wint_ref[...] = flip(win_ref[0]).astype(BF)


def back_call(at, cot, cot_o, ck, ck_o, w_in, w_out):
    whole = lambda shape: pl.BlockSpec(shape, lambda i, at: (0,) * len(shape))
    return pl.pallas_call(
        back_kernel,
        grid_spec=pltpu.PrefetchScalarGridSpec(
            num_scalar_prefetch=1,
            grid=(1,),
            in_specs=[
                whole((N1, D)),
                whole((N1, D)),
                whole((4, N1)),
                whole((4, N1)),
                pl.BlockSpec((1, D, FH), lambda i, at: (at[0], 0, 0)),
                pl.BlockSpec((1, FH, D), lambda i, at: (at[0], 0, 0)),
            ],
            out_specs=[whole((D, N2)), whole((FH, N2)), whole((FH, D))],
        ),
        out_shape=(
            jax.ShapeDtypeStruct((D, N2), BF),
            jax.ShapeDtypeStruct((FH, N2), BF),
            jax.ShapeDtypeStruct((FH, D), BF),
        ),
        compiler_params=params(),
        cost_estimate=cost(11e8, 8e6),
        name="cotangent_back",
    )(at, cot, cot_o, ck, ck_o, w_in, w_out)


def gate_kernel(ck_ref, cko_ref, wgeo_ref, bgeo_ref, wroute_ref, r_ref, g_ref):
    for half, ref in enumerate((ck_ref, cko_ref)):
        cols = slice(N1 * half, N1 * half + N1)
        pre = bgeo_ref[...]
        for k in range(3):
            pre = pre + wgeo_ref[:, k : k + 1] * ref[k : k + 1, :]
        r = jnp.tanh(pre)
        r_ref[:, cols] = r
        logit = jnp.dot(wroute_ref[...], r, precision=lax.Precision.HIGHEST, preferred_element_type=F32)
        expo = jnp.exp(logit)
        g_ref[:, cols] = expo / jnp.sum(expo, axis=0, keepdims=True)


def gate_call(ck, ck_o, wgeo_t, bgeo, wroute_t):
    return pl.pallas_call(
        gate_kernel,
        out_shape=(jax.ShapeDtypeStruct((64, N2), F32), jax.ShapeDtypeStruct((8, N2), F32)),
        compiler_params=params(),
        cost_estimate=cost(1e7, 1e6),
        name="gate",
    )(ck, ck_o, wgeo_t, bgeo, wroute_t)


GELU_A = 0.7978845608028654
GELU_B = 0.7978845608028654 * 0.044715


def expert_kernel(
    at_ref, msg_ref, tokt_ref, q_ref, dyt_ref, back_ref, g_ref, r_ref, win_ref, wint_ref,
    own_ref, oth_ref, msg2_ref, p0_ref, p1_ref, p2_ref, p3_ref,
    kvh, kvl, ksh, ksl, gw1, gw2, dkv, dks, route,
):
    step = pl.program_id(0)
    expert = at_ref[1]

    @pl.when(step == 0)
    def _():
        hi, lo = split2(unpack_heads(msg_ref[0:64, :]))
        kvh[...] = hi
        kvl[...] = lo
        ks = row_of(msg_ref, 64)[0:1]
        hi, lo = split2(jnp.where(head_mask(D, D), ks, 0.0))
        ksh[...] = hi
        ksl[...] = lo
        gw1[...] = jnp.zeros_like(gw1)
        gw2[...] = jnp.zeros_like(gw2)
        dkv[...] = jnp.zeros_like(dkv)
        dks[...] = jnp.zeros_like(dks)
        route[...] = jnp.zeros_like(route)

    q = q_ref[...]
    num = mm(kvh[...], q) + mm(kvl[...], q)
    rden = 1.0 / (mm(ksh[...], q) + mm(ksl[...], q))
    attn = num * rden
    mid = (tokt_ref[...].astype(F32) + attn).astype(BF)
    gates = g_ref[...]
    mine = lax.broadcasted_iota(jnp.int32, gates.shape, 0) == expert
    gate = jnp.sum(jnp.where(mine, gates, 0.0), axis=0, keepdims=True)
    dyt = dyt_ref[...].astype(F32)
    df = (dyt * gate).astype(BF)
    first = jnp.logical_and(at_ref[2] == 0, step < N1 // TB)
    dmid = dyt * jnp.where(first, 1.0, 0.0)
    stat = jnp.zeros((1, TB), F32)
    for j in range(0, FH, HC):
        rows = slice(j, j + HC)
        u = mm(wint_ref[rows, :], mid)
        u2 = u * u
        t = jnp.tanh(u * (GELU_A + GELU_B * u2))
        half = 0.5 + 0.5 * t
        act = (u * half).astype(BF)
        slope = half + 0.5 * u * (1.0 - t * t) * (GELU_A + 3.0 * GELU_B * u2)
        back = back_ref[rows, :].astype(F32)
        stat = stat + jnp.sum(act.astype(F32) * back, axis=0, keepdims=True)
        du = (back * gate * slope).astype(BF)
        gw2[rows, :] += mm_nt(act, df)
        gw1[rows, :] += mm_nt(du, mid)
        dmid = dmid + mm(win_ref[0, :, rows], du)
    stat = stat * gate
    turn = (jnp.where(mine, 1.0, 0.0) - gates) * stat
    route[...] += lax.dot_general(
        turn, r_ref[...], (((1,), (1,)), ((), ())), precision=lax.Precision.HIGHEST, preferred_element_type=F32
    )
    dnum = dmid * rden
    dden = -jnp.sum((dnum * attn).reshape(8, HD, TB), axis=1)
    hi, lo = split2(dnum)
    dkv[...] += mm_nt(q, hi) + mm_nt(q, lo)
    hi, lo = split2(dden)
    dks[...] += mm_nt(hi, q) + mm_nt(lo, q)

    @pl.when(step < N1 // TB)
    def _():
        own_ref[...] = dmid.astype(BF)

    @pl.when(step >= N1 // TB)
    def _():
        oth_ref[...] = dmid.astype(BF)

    @pl.when(step == N2 // TB - 1)
    def _():
        x, z = at_ref[3], at_ref[4]
        for d, ref in enumerate((p0_ref, p1_ref, p2_ref, p3_ref)):
            for e in range(4):
                piece = lax.rem(x + d, 4) * 4 + lax.rem(z + e, 4)
                rows = pl.ds(pl.multiple_of(piece * 64, 64), 64)
                ref[e, 0:64, :] = gw1[rows, :].astype(BF)
                ref[e, 64:128, :] = gw2[rows, :].astype(BF)
        parts = pack_heads(dkv[...])
        msg2_ref[0:32, :] = parts[0]
        msg2_ref[32:64, :] = parts[1]
        r = lax.broadcasted_iota(jnp.int32, (8, D), 0)
        c = lax.broadcasted_iota(jnp.int32, (8, D), 1) // HD
        sums = jnp.where(r == c, dks[...], 0.0)
        msg2_ref[64:72, :] = sums[:, :128]
        msg2_ref[72:80, :] = sums[:, 128:]
        msg2_ref[80:88, :] = jnp.concatenate([route[...], jnp.zeros((8, 64), F32)], axis=1)


def expert_call(at, msg, tokt, q, dyt, back, g, r, w_in, wint):
    steps, own = N2 // TB, N1 // TB
    whole = lambda shape: pl.BlockSpec(shape, lambda i, at: (0,) * len(shape))
    by_points = lambda rows: pl.BlockSpec((rows, TB), lambda i, at: (0, i))
    return pl.pallas_call(
        expert_kernel,
        grid_spec=pltpu.PrefetchScalarGridSpec(
            num_scalar_prefetch=1,
            grid=(steps,),
            in_specs=[
                whole((80, 128)),
                by_points(D),
                by_points(D),
                by_points(D),
                by_points(FH),
                by_points(8),
                by_points(64),
                pl.BlockSpec((1, D, FH), lambda i, at: (at[0], 0, 0)),
                whole((FH, D)),
            ],
            out_specs=[
                pl.BlockSpec((D, TB), lambda i, at: (0, jnp.minimum(i, own - 1))),
                pl.BlockSpec((D, TB), lambda i, at: (0, jnp.maximum(i - own, 0))),
                whole((88, 128)),
            ]
            + [whole((4, 128, D))] * 4,
            scratch_shapes=[pltpu.VMEM((D, D), BF)] * 4
            + [
                pltpu.VMEM((FH, D), F32),
                pltpu.VMEM((FH, D), F32),
                pltpu.VMEM((D, D), F32),
                pltpu.VMEM((8, D), F32),
                pltpu.VMEM((8, 64), F32),
            ],
        ),
        out_shape=(
            jax.ShapeDtypeStruct((D, N1), BF),
            jax.ShapeDtypeStruct((D, N1), BF),
            jax.ShapeDtypeStruct((88, 128), F32),
        )
        + (jax.ShapeDtypeStruct((4, 128, D), BF),) * 4,
        compiler_params=params(),
        cost_estimate=cost(6e9, 12e6),
        name="expert",
    )(at, msg, tokt, q, dyt, back, g, r, w_in, wint)


def back_query_kernel(at_ref, d0, d1, d2, d3, msg_ref, tokt_ref, q_ref, wq_ref, gx_ref, gq_ref):
    dmid = (d0[...].astype(F32) + d1[...].astype(F32)) + (d2[...].astype(F32) + d3[...].astype(F32))
    q = q_ref[...]
    tokt = tokt_ref[...]
    kvt = unpack_heads(msg_ref[0:64, :])
    kvth, kvtl = split2(kvt)
    kvh, kvl = split2(kvt.T)
    ks = row_of(msg_ref, 64)[0:1]
    mask = head_mask(D, D)
    ksh, ksl = split2(jnp.where(mask, ks, 0.0))
    kch, kcl = split2(jnp.where(mask, as_column(ks), 0.0))
    num = mm(kvth, q) + mm(kvtl, q)
    rden = 1.0 / (mm(ksh, q) + mm(ksl, q))
    attn = num * rden
    dnum = dmid * rden
    nh, nl = split2(dnum)
    zh, zl = split2(dnum * attn)
    dq = (mm(kvh, nh) - mm(kch, zh)) + (mm(kvl, nh) - mm(kcl, zh)) + (mm(kvh, nl) - mm(kch, zl))
    wq = wq_ref[...]
    pre = mm(flip(wq).astype(BF), tokt)
    dqp = (dq * jnp.where(pre > 0, 1.0, jnp.exp(jnp.minimum(pre, 0.0)))).astype(BF)
    gx_ref[...] = dmid + mm(wq, dqp)
    rows = pl.ds(pl.multiple_of(at_ref[2] * 64, 64), 64)
    gq_ref[...] = mm_nt(tokt_ref[rows, :], dqp)


def back_query_call(at, dm, msg, tokt, q, wq):
    whole = lambda shape: pl.BlockSpec(shape, lambda i, at: (0,) * len(shape))
    return pl.pallas_call(
        back_query_kernel,
        grid_spec=pltpu.PrefetchScalarGridSpec(
            num_scalar_prefetch=1,
            grid=(1,),
            in_specs=[whole((D, N1))] * 4
            + [whole((80, 128)), whole((D, N1)), whole((D, N1)), whole((D, D))],
            out_specs=[whole((D, N1)), whole((64, D))],
        ),
        out_shape=(jax.ShapeDtypeStruct((D, N1), F32), jax.ShapeDtypeStruct((64, D), F32)),
        compiler_params=params(),
        cost_estimate=cost(2e9, 5e6),
        name="back_query",
    )(at, *dm, msg, tokt, q, wq)


def back_keys_kernel(at_ref, msg_ref, km_ref, v_ref, slope_ref, tokt_ref, gq_ref, dk_ref, dv_ref, keep_ref, send_ref):
    dkv = unpack_heads(msg_ref[0:64, :])
    dks = jnp.sum(row_of(msg_ref, 64), axis=0, keepdims=True)
    hi, lo = split2(dkv)
    v = v_ref[...]
    dk = mm(hi, v) + mm(lo, v) + as_column(dks)
    dk = (dk * slope_ref[...]).astype(BF)
    hi, lo = split2(dkv.T)
    km = km_ref[...]
    dv = (mm(hi, km) + mm(lo, km)).astype(BF)
    dk_ref[...] = dk
    dv_ref[...] = dv
    core, y = at_ref[0], at_ref[2]
    for ref, part in ((keep_ref, core), (send_ref, 1 - core)):
        tok = tokt_ref[pl.ds(pl.multiple_of(y * 64 + part * 32, 32), 32), :]
        ref[:, 0:D] = gq_ref[pl.ds(pl.multiple_of(part * 32, 32), 32), :].astype(BF)
        ref[:, D : 2 * D] = mm_nt(tok, dk).astype(BF)
        ref[:, 2 * D : 3 * D] = mm_nt(tok, dv).astype(BF)


def back_keys_call(at, msg, km, v, slope, tokt, gq):
    whole = lambda shape: pl.BlockSpec(shape, lambda i, at: (0,) * len(shape))
    return pl.pallas_call(
        back_keys_kernel,
        grid_spec=pltpu.PrefetchScalarGridSpec(
            num_scalar_prefetch=1,
            grid=(1,),
            in_specs=[whole((88, 128))] + [whole((D, N1))] * 4 + [whole((64, D))],
            out_specs=[whole((D, N1)), whole((D, N1)), whole((32, 3 * D)), whole((32, 3 * D))],
        ),
        out_shape=(
            jax.ShapeDtypeStruct((D, N1), BF),
            jax.ShapeDtypeStruct((D, N1), BF),
            jax.ShapeDtypeStruct((32, 3 * D), BF),
            jax.ShapeDtypeStruct((32, 3 * D), BF),
        ),
        compiler_params=params(),
        cost_estimate=cost(1e9, 4e6),
        name="back_keys",
    )(at, msg, km, v, slope, tokt, gq)


def grad_x_kernel(gx_ref, dk_ref, dv_ref, wk_ref, wv_ref, out_ref):
    total = gx_ref[...] + mm(wk_ref[...], dk_ref[...]) + mm(wv_ref[...], dv_ref[...])
    out_ref[...] = total.T.astype(BF)


def grad_x_call(gx, dk, dv, wk, wv):
    return pl.pallas_call(
        grad_x_kernel,
        out_shape=jax.ShapeDtypeStruct((N1, D), BF),
        compiler_params=params(),
        cost_estimate=cost(3e8, 3e6),
        name="grad_x",
    )(gx, dk, dv, wk, wv)


def place_kernel(at_ref, *refs):
    ins, (gin_ref, gout_ref, buf) = refs[:8], refs[8:]
    core, x, z = at_ref[0], at_ref[3], at_ref[4]
    for side in range(2):
        expert = core if side == 0 else 1 - core
        for d in range(4):
            ref = ins[4 * side + d]
            for e in range(4):
                piece = lax.rem(x + 4 - d, 4) * 4 + lax.rem(z + 4 - e, 4)
                rows = pl.ds(pl.multiple_of(piece * 64, 64), 64)
                buf[rows, :] = ref[e, 0:64, :].astype(F32)
                gout_ref[expert, rows, :] = ref[e, 64:128, :].astype(F32)
        gin_ref[expert] = buf[...].T


def place_call(at, pieces):
    whole = lambda shape: pl.BlockSpec(shape, lambda i, at: (0,) * len(shape))
    return pl.pallas_call(
        place_kernel,
        grid_spec=pltpu.PrefetchScalarGridSpec(
            num_scalar_prefetch=1,
            grid=(1,),
            in_specs=[whole((4, 128, D))] * 8,
            out_specs=[whole((2, D, FH)), whole((2, FH, D))],
            scratch_shapes=[pltpu.VMEM((FH, D), F32)],
        ),
        out_shape=(jax.ShapeDtypeStruct((2, D, FH), F32), jax.ShapeDtypeStruct((2, FH, D), F32)),
        compiler_params=params(),
        cost_estimate=cost(1e6, 7e6),
        name="place_experts",
    )(at, *pieces)


def place_proj_kernel(at_ref, *refs):
    ins, outs = refs[:4], refs[4:]
    core, y = at_ref[0], at_ref[2]
    for d, ref in enumerate(ins):
        for side in range(2):
            part = core if side == 0 else 1 - core
            rows = pl.ds(pl.multiple_of(lax.rem(y + 4 - d, 4) * 64 + part * 32, 32), 32)
            for k, out in enumerate(outs):
                out[rows, :] = ref[side, :, D * k : D * k + D].astype(F32)


def place_proj_call(at, pieces):
    whole = lambda shape: pl.BlockSpec(shape, lambda i, at: (0,) * len(shape))
    return pl.pallas_call(
        place_proj_kernel,
        grid_spec=pltpu.PrefetchScalarGridSpec(
            num_scalar_prefetch=1,
            grid=(1,),
            in_specs=[whole((2, 32, 3 * D))] * 4,
            out_specs=[whole((D, D))] * 3,
        ),
        out_shape=(jax.ShapeDtypeStruct((D, D), F32),) * 3,
        compiler_params=params(),
        cost_estimate=cost(1e6, 1e6),
        name="place_projections",
    )(at, *pieces)


def swap_core(v):
    return lax.ppermute(v, "pts", [(i, i ^ 1) for i in range(32)])


def to_x(v, d):
    return lax.ppermute(v, "pts", [(i, (i & ~6) | ((i + 2 * d) & 6)) for i in range(32)])


def to_z(v, d):
    return lax.ppermute(v, "pts", [(i, (i + 8 * d) % 32) for i in range(32)])


def to_y(v, d):
    return lax.ppermute(v, "exp", [(i, (i + d) % 4) for i in range(4)])


def star(v, to):
    return [to(v, d) for d in (1, 2, 3)]


def star_sum(v, to):
    a, b, c = star(v, to)
    if v.dtype == BF:
        return ((v.astype(F32) + a.astype(F32)) + (b.astype(F32) + c.astype(F32))).astype(BF)
    return (v + a) + (b + c)


def on_device(
    tokens, coords, keep, cotangent, w_query, w_key, w_value, w_geo, b_geo, w_route, w_in, w_out
):
    pts = lax.axis_index("pts")
    y = lax.axis_index("exp")
    core, x, z = pts % 2, (pts // 2) % 4, pts // 8
    at = jnp.stack([core, 2 * y + core, y, x, z]).astype(jnp.int32)
    keep_row = keep[None, :]
    ck = jnp.concatenate([coords, keep_row.astype(F32)], axis=0)

    km, v, slope, msg = keys_call(tokens, keep_row, w_key, w_value)
    tokens_o, cot_o, ck_o = swap_core(tokens), swap_core(cotangent), swap_core(ck)

    msg = msg + swap_core(msg)
    msg = star_sum(msg, to_x)
    msg = star_sum(msg, to_z)

    tokt, q = query_call(tokens, tokens_o, w_query)
    dyt, back, wint = back_call(at, cotangent, cot_o, ck, ck_o, w_in, w_out)
    r, g = gate_call(ck, ck_o, w_geo.T, b_geo[:, None], w_route.T)

    own, oth, msg2, p0, p1, p2, p3 = expert_call(at, msg, tokt, q, dyt, back, g, r, w_in, wint)

    msg2 = msg2 + swap_core(msg2)
    msg2 = star_sum(msg2, to_y)
    msg2 = star_sum(msg2, to_z)
    msg2 = star_sum(msg2, to_x)

    a, b, c = to_x(p1, 1), to_x(p2, 2), to_x(p3, 3)
    s = (p0.astype(F32) + a.astype(F32)) + (b.astype(F32) + c.astype(F32))
    s = [s[e].astype(BF) for e in range(4)]
    a, b, c = to_z(s[1], 1), to_z(s[2], 2), to_z(s[3], 3)
    s = ((s[0].astype(F32) + a.astype(F32)) + (b.astype(F32) + c.astype(F32))).astype(BF)

    own = (own.astype(F32) + swap_core(oth).astype(F32)).astype(BF)
    dm = [own] + star(own, to_y)

    gx, gq = back_query_call(at, dm, msg, tokt, q, w_query)
    dk, dv, part, away = back_keys_call(at, msg2, km, v, slope, tokt, gq)

    s = jnp.stack([s] + star(s, to_z))
    pieces = [s] + star(s, to_x)
    pieces = pieces + [swap_core(piece) for piece in pieces]
    grad_w_in, grad_w_out = place_call(at, pieces)

    part = (part.astype(F32) + swap_core(away).astype(F32)).astype(BF)
    part = star_sum(part, to_x)
    part = star_sum(part, to_z)
    part = jnp.stack([part, swap_core(part)])
    grad_wq, grad_wk, grad_wv = place_proj_call(at, [part] + star(part, to_y))

    grad_x = grad_x_call(gx, dk, dv, w_key, w_value)
    grad_route = lax.dynamic_slice_in_dim(msg2[80:88, :64], 2 * y, 2, 0).T
    return (grad_x, grad_wq, grad_wk, grad_wv, grad_w_in, grad_w_out, grad_route)


def solution(mesh):
    in_specs = (
        P("pts", None),
        P(None, "pts"),
        P("pts"),
        P("pts", None),
        P(),
        P(),
        P(),
        P(),
        P(),
        P(),
        P("exp", None, None),
        P("exp", None, None),
    )
    out_specs = (
        P("pts", None),
        P(),
        P(),
        P(),
        P("exp", None, None),
        P("exp", None, None),
        P(None, "exp"),
    )
    return jax.shard_map(
        on_device, mesh=mesh, in_specs=in_specs, out_specs=out_specs, check_vma=False
    )
```

time: 492 us -> 174 us (0.35)
  blocking collectives: 262 us -> 0 us
  waiting for transfers between devices: 136 us -> 37.4 us
  starting transfers between devices: 0.26 us -> 65.6 us
  Pallas kernels: 0 us -> 53.5 us
  matrix products: 49.6 us -> 0 us
  between operations: 14.7 us -> 0.91 us
  local copies, waits for them, and re-layouts: 16.3 us -> 9.64 us
  other arithmetic: 12.6 us -> 6.62 us
    psum x3 -> x0, blocking collectives: 262 us -> none  [the longest x1 127 us: on_device(): kv, ks = lax.psum((kv_part, ks_part), 'pts')]
    psum x2 -> x0, waiting for transfers between devices: 136 us -> none  [the longest x1 113 us: on_device(): grad_wq, grad_wk, grad_wv = lax.psum((gq, gk, gv), 'pts')]
    ppermute x0 -> x51, starting transfers between devices: none -> 65.6 us  [the longest x12 22.1 us: swap_core(): return lax.ppermute(v, 'pts', [(i, i ^ 1) for i in range(32)])]
    pallas_call x0 -> x10, Pallas kernels: none -> 53.5 us  [the longest x1 18.6 us: expert_call(): pl.pallas_call(expert_kernel, grid_spec=pltpu.PrefetchScalarGridSpec(num_...]
    dot_general x32 -> x0, matrix products: 49.6 us -> none  [the longest x2 9.14 us: on_device(): dact = jnp.dot(dfe, w_out[expert].T, preferred_element_type=jnp.float32)]
    ppermute x0 -> x51, waiting for transfers between devices: none -> 37.4 us  [the longest x9 22.8 us: to_y(): return lax.ppermute(v, 'exp', [(i, (i + d) % 4) for i in range(4)])]
    unnamed x99 -> x43, local copies, waits for them, and re-layouts: 14.5 us -> 6.45 us
  transfers between devices with their start and end apart: 2 -> 51, of which waited for: 2 -> 15; matrix products, arithmetic and copies ran while one was open for 3% -> 6% of each run, Pallas kernels for 0% -> 13%
where the time goes in v1:
time: 174 us
  starting transfers between devices  65.6 us (38%)
  Pallas kernels  53.5 us (31%)
  waiting for transfers between devices  37.4 us (21%)
  local copies, waits for them, and re-layouts  9.64 us (6%)
  other arithmetic  6.62 us (4%)
    ppermute x9, waiting for transfers between devices, to_y(): return lax.ppermute(v, 'exp', [(i, (i + d) % 4) for i in range(4)])  22.8 us
    ppermute x12, starting transfers between devices, swap_core(): return lax.ppermute(v, 'pts', [(i, i ^ 1) for i in range(32)])  22.1 us
    pallas_call x1, Pallas kernels, expert_call(): pl.pallas_call(expert_kernel, grid_spec=pltpu.PrefetchScalarGridSpec(num_...  18.6 us
    ppermute x15, starting transfers between devices, to_x(): lax.ppermute(v, 'pts', [(i, i & ~6 | i + 2 * d & 6) for i in range(32)])  17.9 us
    ppermute x15, starting transfers between devices, to_z(): return lax.ppermute(v, 'pts', [(i, (i + 8 * d) % 32) for i in range(32)])  17.7 us
    ppermute x15, waiting for transfers between devices, to_x(): lax.ppermute(v, 'pts', [(i, i & ~6 | i + 2 * d & 6) for i in range(32)])  8.9 us
    ppermute x9, starting transfers between devices, to_y(): return lax.ppermute(v, 'exp', [(i, (i + d) % 4) for i in range(4)])  7.93 us
    unnamed x43, local copies, waits for them, and re-layouts  6.45 us
  transfers between devices with their start and end apart: 51, of which 15 were waited for; matrix products, arithmetic and copies ran while one was open for 6% of the time, Pallas kernels for 13%

profile of v1, /device:TPU:1, one launch (start us, length us, event | category | flops | bytes accessed | tf_op | source)
XLA Modules:
  0.0 173.6 jit_solution(15008344813053948053)
XLA Ops:
  0.6 3.1 %keys.1 = (bf16[256,1024]{1,0:T(8,128)(2,1)}, bf16[256,1024]{1,0:T(8,128)(2,1)}, f32[256,1024]{1,0:T(8,128)}, f32[80,128]{1,0:T(8,128)}) custom-call(bf16[1024,256]{1,0:T(8,128)(2,1)} %tok_ref.3, s32[1,1024]{1,0:T(1,128)} %bitcast.38, bf16[256,256]{1,0:T(8,128)(2,1)} %wk_ref.3, bf16[256,256]{1,0:T(8,128)(2,1)} %wv_ref.3), custom_call_target="tpu_custom_call" | custom-call | flops 400000000 | bytes 3000000 | tf_op jit(solution)/shard_map/keys/pallas_call | solution.py:104
  7.0 2.6 %collective-permute-start.3 = (f32[80,128]{1,0:T(8,128)S(1)}, f32[80,128]{1,0:T(8,128)S(1)}, u32[]{:S(2)}, u32[]{:S(2)}) collective-permute-start(f32[80,128]{1,0:T(8,128)S(1)} %add.111), channel_id=1, source_target_pairs={{0,24},{4,28},{8,0},{12,4},{16,8},{20,12},{24,16},{28,20},{32,56},... | collective-permute-start | bytes 122888 | tf_op jit(solution)/shard_map/ppermute | solution.py:509
  14.4 3.8 %collective-permute-start.6 = (f32[80,128]{1,0:T(8,128)S(1)}, f32[80,128]{1,0:T(8,128)S(1)}, u32[]{:S(2)}, u32[]{:S(2)}) collective-permute-start(f32[80,128]{1,0:T(8,128)S(1)} %add_add_fusion.4), channel_id=1, source_target_pairs={{0,96},{4,100},{8,104},{12,108},{16,112},{20,116},{24,120},{28,124... | collective-permute-start | bytes 122888 | tf_op jit(solution)/shard_map/ppermute | solution.py:513
  25.7 3.4 %queries.1 = (bf16[256,2048]{1,0:T(8,128)(2,1)}, bf16[256,2048]{1,0:T(8,128)(2,1)}) custom-call(bf16[1024,256]{1,0:T(8,128)(2,1)} %tok_ref.3, bf16[1024,256]{1,0:T(8,128)(2,1)} %copy-done.16, bf16[256,256]{1,0:T(8,128)(2,1)} %wq_ref.3), custom_call_target="tpu_custom_call" | custom-call | flops 400000000 | bytes 3000000 | tf_op jit(solution)/shard_map/queries/pallas_call | solution.py:130
  29.9 6.0 %cotangent_back.1 = (bf16[256,2048]{1,0:T(8,128)(2,1)}, bf16[1024,2048]{1,0:T(8,128)(2,1)}, bf16[1024,256]{1,0:T(8,128)(2,1)}) custom-call(s32[5]{0:T(128)} %stack.47.at_ref, bf16[1024,256]{1,0:T(8,128)(2,1)} %cot_ref.1, bf16[1024,256]{1,0:T(8,128)(2,1)} %copy-done.17, f32[4,1024]{1,0:T(4,128)} %copy-done.14, f32[4,1024]{1,0:T(4,128)} %copy-done.15, ...), custom_call_target="tpu_custom_call" | custom-call | flops 1100000000 | bytes 8000000 | tf_op jit(solution)/shard_map/cotangent_back/pallas_call | solution.py:152
  35.9 18.6 %expert.1 = (bf16[256,1024]{1,0:T(8,128)(2,1)}, bf16[256,1024]{1,0:T(8,128)(2,1)}, f32[88,128]{1,0:T(8,128)}, bf16[4,128,256]{2,1,0:T(8,128)(2,1)}, bf16[4,128,2...) custom-call(s32[5]{0:T(128)} %stack.47.at_ref, f32[80,128]{1,0:T(8,128)} %add_add_fusion.3.msg_ref, ...), custom_call_target="tpu_custom_call" | custom-call | flops 6000000000 | bytes 12000000 | tf_op jit(solution)/shard_map/expert/pallas_call | solution.py:299
  54.5 2.8 %collective-permute-start.14 = (f32[88,128]{1,0:T(8,128)}, f32[88,128]{1,0:T(8,128)S(1)}, u32[]{:S(2)}, u32[]{:S(2)}) collective-permute-start(f32[88,128]{1,0:T(8,128)} %get-tuple-element.47), channel_id=1, source_target_pairs={{0,4},{4,0},{8,12},{12,8},{16,20},{20,16},{24,28},{28,24},{32,36},... | collective-permute-start | bytes 135176 | tf_op jit(solution)/shard_map/ppermute | solution.py:505
  59.1 2.7 %collective-permute-start.17 = (f32[88,128]{1,0:T(8,128)S(1)}, f32[88,128]{1,0:T(8,128)S(1)}, u32[]{:S(2)}, u32[]{:S(2)}) collective-permute-start(f32[88,128]{1,0:T(8,128)S(1)} %add.119), channel_id=1, source_target_pairs={{0,3},{1,0},{2,1},{3,2},{4,7},{5,4},{6,5},{7,6},{8,11},{9,8},{10,9... | collective-permute-start | bytes 135176 | tf_op jit(solution)/shard_map/ppermute | solution.py:517
  64.1 2.2 %collective-permute-done.16 = f32[88,128]{1,0:T(8,128)S(1)} collective-permute-done((f32[88,128]{1,0:T(8,128)S(1)}, f32[88,128]{1,0:T(8,128)S(1)}, u32[]{:S(2)}, u32[]{:S(2)}) %collective-permute-start.16) | collective-permute-done | bytes 45088 | tf_op jit(solution)/shard_map/ppermute | solution.py:517
  70.6 2.4 %collective-permute-done.19 = f32[88,128]{1,0:T(8,128)S(1)} collective-permute-done((f32[88,128]{1,0:T(8,128)S(1)}, f32[88,128]{1,0:T(8,128)S(1)}, u32[]{:S(2)}, u32[]{:S(2)}) %collective-permute-start.19) | collective-permute-done | bytes 45088 | tf_op jit(solution)/shard_map/ppermute | solution.py:513
  81.3 5.3 %collective-permute-done.22 = f32[88,128]{1,0:T(8,128)S(1)} collective-permute-done((f32[88,128]{1,0:T(8,128)S(1)}, f32[88,128]{1,0:T(8,128)S(1)}, u32[]{:S(2)}, u32[]{:S(2)}) %collective-permute-start.22) | collective-permute-done | bytes 45088 | tf_op jit(solution)/shard_map/ppermute | solution.py:509
  90.1 2.6 %collective-permute-start.40 = (bf16[128,256]{1,0:T(8,128)(2,1)S(1)}, bf16[128,256]{1,0:T(8,128)(2,1)S(1)}, u32[]{:S(2)}, u32[]{:S(2)}) collective-permute-start(bf16[128,256]{1,0:T(8,128)(2,1)S(1)} %get-tuple-element.66), channel_id=1, source_target_pairs={{0,96},{4,100},{8,104},{12,108},{16,112},{20,116},{24,120},{28,124... | collective-permute-start | bytes 196616 | tf_op jit(solution)/shard_map/ppermute | solution.py:513
  95.0 2.2 %collective-permute-done.12.d2 = bf16[256,1024]{1,0:T(8,128)(2,1)S(1)} collective-permute-done((bf16[256,1024]{1,0:T(8,128)(2,1)S(1)}, bf16[256,1024]{1,0:T(8,128)(2,1)S(1)}, u32[]{:S(2)}, u32[]{:S(2)}) %collective-permute-start.12) | collective-permute-done | bytes 524320 | tf_op jit(solution)/shard_map/ppermute | solution.py:517
  97.2 16.0 %collective-permute-done.11.d1 = bf16[256,1024]{1,0:T(8,128)(2,1)S(1)} collective-permute-done((bf16[256,1024]{1,0:T(8,128)(2,1)S(1)}, bf16[256,1024]{1,0:T(8,128)(2,1)S(1)}, u32[]{:S(2)}, u32[]{:S(2)}) %collective-permute-start.11) | collective-permute-done | bytes 524320 | tf_op jit(solution)/shard_map/ppermute | solution.py:517
  114.0 5.8 %back_query.1 = (f32[256,1024]{1,0:T(8,128)}, f32[64,256]{1,0:T(8,128)}) custom-call(s32[5]{0:T(128)} %stack.47.at_ref, bf16[256,1024]{1,0:T(8,128)(2,1)} %copy-done.1, bf16[256,1024]{1,0:T(8,128)(2,1)} %copy-done.20, bf16[256,1024]{1,0:T(8,128)(2,1)} %copy-done.19, bf16[256,1024]{1,0:T(8,128)(2,1)} %copy-done.18, f32[80,128]{1,0:T(8,128)} %add_add_fusion.3.msg_ref, ...), custom_call_target="tpu_custom_call" | custom-call | flops 2000000000 | bytes 5000000 | tf_op jit(solution)/shard_map/back_query/pallas_call | solution.py:370
  119.7 4.2 %back_keys.1 = (bf16[256,1024]{1,0:T(8,128)(2,1)}, bf16[256,1024]{1,0:T(8,128)(2,1)}, bf16[32,768]{1,0:T(8,128)(2,1)}, bf16[32,768]{1,0:T(8,128)(2,1)}) custom-call(s32[5]{0:T(128)} %stack.47.at_ref, f32[88,128]{1,0:T(8,128)} %add_add_fusion.msg_ref, bf16[256,1024]{1,0:T(8,128)(2,1)} %get-tuple-element.48.km_ref, bf16[256,1024]{1,0:T(8,128)(2,1)} %get-tuple-element.49.v_ref, ...), custom_call_target="tpu_custom_call" | custom-call | flops 1000000000 | bytes 4000000 | tf_op jit(solution)/shard_map/back_keys/pallas_call | solution.py:408
  128.1 4.1 %collective-permute-start.27 = (bf16[32,768]{1,0:T(8,128)(2,1)S(1)}, bf16[32,768]{1,0:T(8,128)(2,1)S(1)}, u32[]{:S(2)}, u32[]{:S(2)}) collective-permute-start(bf16[32,768]{1,0:T(8,128)(2,1)S(1)} %add_convert_fusion.4), channel_id=1, source_target_pairs={{0,24},{4,28},{8,0},{12,4},{16,8},{20,12},{24,16},{28,20},{32,56},... | collective-permute-start | bytes 147464 | tf_op jit(solution)/shard_map/ppermute | solution.py:509
  133.0 2.9 %collective-permute-start.46 = (bf16[4,128,256]{2,1,0:T(8,128)(2,1)S(1)}, bf16[4,128,256]{2,1,0:T(8,128)(2,1)S(1)}, u32[]{:S(2)}, u32[]{:S(2)}) collective-permute-start(bf16[4,128,256]{2,1,0:T(8,128)(2,1)S(1)} %pad_maximum_fusion.refs_0_), channel_id=1, source_target_pairs={{0,24},{4,28},{8,0},{12,4},{16,8},{20,12},{24,16},{28,20},{32,56},... | collective-permute-start | bytes 786440 | tf_op jit(solution)/shard_map/ppermute | solution.py:509
  137.2 3.0 %collective-permute-start.30 = (bf16[32,768]{1,0:T(8,128)(2,1)S(1)}, bf16[32,768]{1,0:T(8,128)(2,1)S(1)}, u32[]{:S(2)}, u32[]{:S(2)}) collective-permute-start(bf16[32,768]{1,0:T(8,128)(2,1)S(1)} %add_convert_fusion.3), channel_id=1, source_target_pairs={{0,96},{4,100},{8,104},{12,108},{16,112},{20,116},{24,120},{28,124... | collective-permute-start | bytes 147464 | tf_op jit(solution)/shard_map/ppermute | solution.py:513
  142.8 3.6 %collective-permute-start.47 = (bf16[4,128,256]{2,1,0:T(8,128)(2,1)S(1)}, bf16[4,128,256]{2,1,0:T(8,128)(2,1)S(1)}, u32[]{:S(2)}, u32[]{:S(2)}) collective-permute-start(bf16[4,128,256]{2,1,0:T(8,128)(2,1)S(1)} %pad_maximum_fusion.refs_0_), channel_id=1, source_target_pairs={{0,4},{4,0},{8,12},{12,8},{16,20},{20,16},{24,28},{28,24},{32,36},... | collective-permute-start | bytes 786440 | tf_op jit(solution)/shard_map/ppermute | solution.py:505
  149.0 5.7 %collective-permute-start.49 = (bf16[4,128,256]{2,1,0:T(8,128)(2,1)S(1)}, bf16[4,128,256]{2,1,0:T(8,128)(2,1)S(1)}, u32[]{:S(2)}, u32[]{:S(2)}) collective-permute-start(bf16[4,128,256]{2,1,0:T(8,128)(2,1)S(1)} %collective-permute-done.45.refs_2_), channel_id=1, source_target_pairs={{0,4},{4,0},{8,12},{12,8},{16,20},{20,16},{24,28},{28,24},{32,36},... | collective-permute-start | bytes 786440 | tf_op jit(solution)/shard_map/ppermute | solution.py:505
  161.8 4.9 %place_experts.1 = (f32[2,256,1024]{2,1,0:T(8,128)}, f32[2,1024,256]{2,1,0:T(8,128)}) custom-call(s32[5]{0:T(128)} %stack.47.at_ref, bf16[4,128,256]{2,1,0:T(8,128)(2,1)} %copy-done, bf16[4,128,256]{2,1,0:T(8,128)(2,1)} %copy-done.6, bf16[4,128,256]{2,1,0:T(8,128)(2,1)} %copy-done.5, bf16[4,128,256]{2,1,0:T(8,128)(2,1)} %copy-done.4, ...), custom_call_target="tpu_custom_call" | custom-call | flops 1000000 | bytes 7000000 | tf_op jit(solution)/shard_map/place_experts/pallas_call | solution.py:460
  166.8 2.9 %grad_x.1 = bf16[1024,256]{1,0:T(8,128)(2,1)} custom-call(f32[256,1024]{1,0:T(8,128)} %get-tuple-element.46.gx_ref, bf16[256,1024]{1,0:T(8,128)(2,1)} %get-tuple-element.52.dk_ref, bf16[256,1024]{1,0:T(8,128)(2,1)} %get-tuple-element.53.dv_ref, bf16[256,256]{1,0:T(8,128)(2,1)} %wk_ref.3, bf16[256,256]{1,0:T(8,128)(2,1)} %wv_ref.3), custom_call_target="tpu_custom_call" | custom-call | flops 300000000 | bytes 3000000 | tf_op jit(solution)/shard_map/grad_x/pallas_call | solution.py:434
  171.0 2.6 %place_projections.1 = (f32[256,256]{1,0:T(8,128)}, f32[256,256]{1,0:T(8,128)}, f32[256,256]{1,0:T(8,128)}) custom-call(s32[5]{0:T(128)} %stack.47.at_ref, bf16[2,32,768]{2,1,0:T(8,128)(2,1)} %copy-done.2, bf16[2,32,768]{2,1,0:T(8,128)(2,1)} %copy-done.13, bf16[2,32,768]{2,1,0:T(8,128)(2,1)} %copy-done.12, bf16[2,32,768]{2,1,0:T(8,128)(2,1)} %copy-done.11), custom_call_target="tpu_custom_call" | custom-call | flops 1000000 | bytes 1000000 | tf_op jit(solution)/shard_map/place_projections/pallas_call | solution.py:489
  (153 shorter events, 59.3 us)
Async XLA Ops:
  5.2 19.7 %collective-permute-start.7 = (bf16[1024,256]{1,0:T(8,128)(2,1)}, bf16[1024,256]{1,0:T(8,128)(2,1)S(1)}, u32[]{:S(2)}, u32[]{:S(2)}) collective-permute-start(bf16[1024,256]{1,0:T(8,128)(2,1)} %tok_ref.3), channel_id=1, source_target_pairs={{0,4},{4,0},{8,12},{12,8},{16,20},{20,16},{24,28},{28,24},{32,36},... | collective-permute-start | bytes 1572872 | tf_op jit(solution)/shard_map/ppermute | solution.py:505
  12.7 16.4 %collective-permute-start.8 = (bf16[1024,256]{1,0:T(8,128)(2,1)}, bf16[1024,256]{1,0:T(8,128)(2,1)S(1)}, u32[]{:S(2)}, u32[]{:S(2)}) collective-permute-start(bf16[1024,256]{1,0:T(8,128)(2,1)} %cot_ref.1), channel_id=1, source_target_pairs={{0,4},{4,0},{8,12},{12,8},{16,20},{20,16},{24,28},{28,24},{32,36},... | collective-permute-start | bytes 1572872 | tf_op jit(solution)/shard_map/ppermute | solution.py:505
  14.4 9.8 %collective-permute-start.6 = (f32[80,128]{1,0:T(8,128)S(1)}, f32[80,128]{1,0:T(8,128)S(1)}, u32[]{:S(2)}, u32[]{:S(2)}) collective-permute-start(f32[80,128]{1,0:T(8,128)S(1)} %add_add_fusion.4), channel_id=1, source_target_pairs={{0,96},{4,100},{8,104},{12,108},{16,112},{20,116},{24,120},{28,124... | collective-permute-start | bytes 122888 | tf_op jit(solution)/shard_map/ppermute | solution.py:513
  62.9 17.1 %collective-permute-start.10 = (bf16[256,1024]{1,0:T(8,128)(2,1)}, bf16[256,1024]{1,0:T(8,128)(2,1)S(1)}, u32[]{:S(2)}, u32[]{:S(2)}) collective-permute-start(bf16[256,1024]{1,0:T(8,128)(2,1)} %get-tuple-element.45), channel_id=1, source_target_pairs={{0,4},{4,0},{8,12},{12,8},{16,20},{20,16},{24,28},{28,24},{32,36},... | collective-permute-start | bytes 1572872 | tf_op jit(solution)/shard_map/ppermute | solution.py:505
  75.0 13.3 %collective-permute-start.35 = (bf16[4,128,256]{2,1,0:T(8,128)(2,1)}, bf16[4,128,256]{2,1,0:T(8,128)(2,1)S(1)}, u32[]{:S(2)}, u32[]{:S(2)}) collective-permute-start(bf16[4,128,256]{2,1,0:T(8,128)(2,1)} %get-tuple-element.60), channel_id=1, source_target_pairs={{0,8},{4,12},{8,16},{12,20},{16,24},{20,28},{24,0},{28,4},{32,40},... | collective-permute-start | bytes 786440 | tf_op jit(solution)/shard_map/ppermute | solution.py:509
  76.2 13.5 %collective-permute-start.36 = (bf16[4,128,256]{2,1,0:T(8,128)(2,1)}, bf16[4,128,256]{2,1,0:T(8,128)(2,1)S(1)}, u32[]{:S(2)}, u32[]{:S(2)}) collective-permute-start(bf16[4,128,256]{2,1,0:T(8,128)(2,1)} %get-tuple-element.61), channel_id=1, source_target_pairs={{0,16},{4,20},{8,24},{12,28},{16,0},{20,4},{24,8},{28,12},{32,48},... | collective-permute-start | bytes 786440 | tf_op jit(solution)/shard_map/ppermute | solution.py:509
  77.5 12.3 %collective-permute-start.37 = (bf16[4,128,256]{2,1,0:T(8,128)(2,1)}, bf16[4,128,256]{2,1,0:T(8,128)(2,1)S(1)}, u32[]{:S(2)}, u32[]{:S(2)}) collective-permute-start(bf16[4,128,256]{2,1,0:T(8,128)(2,1)} %get-tuple-element.62), channel_id=1, source_target_pairs={{0,24},{4,28},{8,0},{12,4},{16,8},{20,12},{24,16},{28,20},{32,56},... | collective-permute-start | bytes 786440 | tf_op jit(solution)/shard_map/ppermute | solution.py:509
  78.6 8.0 %collective-permute-start.22 = (f32[88,128]{1,0:T(8,128)S(1)}, f32[88,128]{1,0:T(8,128)S(1)}, u32[]{:S(2)}, u32[]{:S(2)}) collective-permute-start(f32[88,128]{1,0:T(8,128)S(1)} %add_add_fusion.1), channel_id=1, source_target_pairs={{0,16},{4,20},{8,24},{12,28},{16,0},{20,4},{24,8},{28,12},{32,48},... | collective-permute-start | bytes 135176 | tf_op jit(solution)/shard_map/ppermute | solution.py:509
  86.6 8.0 %collective-permute-start.13 = (bf16[256,1024]{1,0:T(8,128)(2,1)S(1)}, bf16[256,1024]{1,0:T(8,128)(2,1)S(1)}, u32[]{:S(2)}, u32[]{:S(2)}) collective-permute-start(bf16[256,1024]{1,0:T(8,128)(2,1)S(1)} %add_convert_fusion.d0), channel_id=1, source_target_pairs={{0,3},{1,0},{2,1},{3,2},{4,7},{5,4},{6,5},{7,6},{8,11},{9,8},{10,9... | collective-permute-start | bytes 1572872 | tf_op jit(solution)/shard_map/ppermute | solution.py:517
  87.5 9.6 %collective-permute-start.12 = (bf16[256,1024]{1,0:T(8,128)(2,1)S(1)}, bf16[256,1024]{1,0:T(8,128)(2,1)S(1)}, u32[]{:S(2)}, u32[]{:S(2)}) collective-permute-start(bf16[256,1024]{1,0:T(8,128)(2,1)S(1)} %add_convert_fusion.d0), channel_id=1, source_target_pairs={{0,2},{1,3},{2,0},{3,1},{4,6},{5,7},{6,4},{7,5},{8,10},{9,11},{10,... | collective-permute-start | bytes 1572872 | tf_op jit(solution)/shard_map/ppermute | solution.py:517
  88.3 24.9 %collective-permute-start.11 = (bf16[256,1024]{1,0:T(8,128)(2,1)S(1)}, bf16[256,1024]{1,0:T(8,128)(2,1)S(1)}, u32[]{:S(2)}, u32[]{:S(2)}) collective-permute-start(bf16[256,1024]{1,0:T(8,128)(2,1)S(1)} %add_convert_fusion.d0), channel_id=1, source_target_pairs={{0,1},{1,2},{2,3},{3,0},{4,5},{5,6},{6,7},{7,4},{8,9},{9,10},{10,1... | collective-permute-start | bytes 1572872 | tf_op jit(solution)/shard_map/ppermute | solution.py:517
  89.9 35.4 %collective-permute-start.38 = (bf16[128,256]{1,0:T(8,128)(2,1)S(1)}, bf16[128,256]{1,0:T(8,128)(2,1)S(1)}, u32[]{:S(2)}, u32[]{:S(2)}) collective-permute-start(bf16[128,256]{1,0:T(8,128)(2,1)S(1)} %get-tuple-element.65), channel_id=1, source_target_pairs={{0,32},{4,36},{8,40},{12,44},{16,48},{20,52},{24,56},{28,60},{32,6... | collective-permute-start | bytes 196616 | tf_op jit(solution)/shard_map/ppermute | solution.py:513
  90.1 35.3 %collective-permute-start.40 = (bf16[128,256]{1,0:T(8,128)(2,1)S(1)}, bf16[128,256]{1,0:T(8,128)(2,1)S(1)}, u32[]{:S(2)}, u32[]{:S(2)}) collective-permute-start(bf16[128,256]{1,0:T(8,128)(2,1)S(1)} %get-tuple-element.66), channel_id=1, source_target_pairs={{0,96},{4,100},{8,104},{12,108},{16,112},{20,116},{24,120},{28,124... | collective-permute-start | bytes 196616 | tf_op jit(solution)/shard_map/ppermute | solution.py:513
  94.7 30.7 %collective-permute-start.39 = (bf16[128,256]{1,0:T(8,128)(2,1)S(1)}, bf16[128,256]{1,0:T(8,128)(2,1)S(1)}, u32[]{:S(2)}, u32[]{:S(2)}) collective-permute-start(bf16[128,256]{1,0:T(8,128)(2,1)S(1)} %get-tuple-element.67), channel_id=1, source_target_pairs={{0,64},{4,68},{8,72},{12,76},{16,80},{20,84},{24,88},{28,92},{32,9... | collective-permute-start | bytes 196616 | tf_op jit(solution)/shard_map/ppermute | solution.py:513
  128.1 7.8 %collective-permute-start.27 = (bf16[32,768]{1,0:T(8,128)(2,1)S(1)}, bf16[32,768]{1,0:T(8,128)(2,1)S(1)}, u32[]{:S(2)}, u32[]{:S(2)}) collective-permute-start(bf16[32,768]{1,0:T(8,128)(2,1)S(1)} %add_convert_fusion.4), channel_id=1, source_target_pairs={{0,24},{4,28},{8,0},{12,4},{16,8},{20,12},{24,16},{28,20},{32,56},... | collective-permute-start | bytes 147464 | tf_op jit(solution)/shard_map/ppermute | solution.py:509
  133.0 9.6 %collective-permute-start.46 = (bf16[4,128,256]{2,1,0:T(8,128)(2,1)S(1)}, bf16[4,128,256]{2,1,0:T(8,128)(2,1)S(1)}, u32[]{:S(2)}, u32[]{:S(2)}) collective-permute-start(bf16[4,128,256]{2,1,0:T(8,128)(2,1)S(1)} %pad_maximum_fusion.refs_0_), channel_id=1, source_target_pairs={{0,24},{4,28},{8,0},{12,4},{16,8},{20,12},{24,16},{28,20},{32,56},... | collective-permute-start | bytes 786440 | tf_op jit(solution)/shard_map/ppermute | solution.py:509
  142.6 12.9 %collective-permute-start.44 = (bf16[4,128,256]{2,1,0:T(8,128)(2,1)S(1)}, bf16[4,128,256]{2,1,0:T(8,128)(2,1)S(1)}, u32[]{:S(2)}, u32[]{:S(2)}) collective-permute-start(bf16[4,128,256]{2,1,0:T(8,128)(2,1)S(1)} %pad_maximum_fusion.refs_0_), channel_id=1, source_target_pairs={{0,8},{4,12},{8,16},{12,20},{16,24},{20,28},{24,0},{28,4},{32,40},... | collective-permute-start | bytes 786440 | tf_op jit(solution)/shard_map/ppermute | solution.py:509
  142.8 16.3 %collective-permute-start.47 = (bf16[4,128,256]{2,1,0:T(8,128)(2,1)S(1)}, bf16[4,128,256]{2,1,0:T(8,128)(2,1)S(1)}, u32[]{:S(2)}, u32[]{:S(2)}) collective-permute-start(bf16[4,128,256]{2,1,0:T(8,128)(2,1)S(1)} %pad_maximum_fusion.refs_0_), channel_id=1, source_target_pairs={{0,4},{4,0},{8,12},{12,8},{16,20},{20,16},{24,28},{28,24},{32,36},... | collective-permute-start | bytes 786440 | tf_op jit(solution)/shard_map/ppermute | solution.py:505
  146.4 13.1 %collective-permute-start.50 = (bf16[4,128,256]{2,1,0:T(8,128)(2,1)S(1)}, bf16[4,128,256]{2,1,0:T(8,128)(2,1)S(1)}, u32[]{:S(2)}, u32[]{:S(2)}) collective-permute-start(bf16[4,128,256]{2,1,0:T(8,128)(2,1)S(1)} %collective-permute-done.46.refs_3_), channel_id=1, source_target_pairs={{0,4},{4,0},{8,12},{12,8},{16,20},{20,16},{24,28},{28,24},{32,36},... | collective-permute-start | bytes 786440 | tf_op jit(solution)/shard_map/ppermute | solution.py:505
  148.4 9.8 %collective-permute-start.31 = (bf16[32,768]{1,0:T(8,128)(2,1)S(1)}, bf16[32,768]{1,0:T(8,128)(2,1)S(1)}, u32[]{:S(2)}, u32[]{:S(2)}) collective-permute-start(bf16[32,768]{1,0:T(8,128)(2,1)S(1)} %add_convert_fusion.2), channel_id=1, source_target_pairs={{0,4},{4,0},{8,12},{12,8},{16,20},{20,16},{24,28},{28,24},{32,36},... | collective-permute-start | bytes 147464 | tf_op jit(solution)/shard_map/ppermute | solution.py:505
  149.0 11.4 %collective-permute-start.49 = (bf16[4,128,256]{2,1,0:T(8,128)(2,1)S(1)}, bf16[4,128,256]{2,1,0:T(8,128)(2,1)S(1)}, u32[]{:S(2)}, u32[]{:S(2)}) collective-permute-start(bf16[4,128,256]{2,1,0:T(8,128)(2,1)S(1)} %collective-permute-done.45.refs_2_), channel_id=1, source_target_pairs={{0,4},{4,0},{8,12},{12,8},{16,20},{20,16},{24,28},{28,24},{32,36},... | collective-permute-start | bytes 786440 | tf_op jit(solution)/shard_map/ppermute | solution.py:505
  158.2 11.5 %collective-permute-start.34 = (bf16[2,32,768]{2,1,0:T(8,128)(2,1)S(1)}, bf16[2,32,768]{2,1,0:T(8,128)(2,1)S(1)}, u32[]{:S(2)}, u32[]{:S(2)}) collective-permute-start(bf16[2,32,768]{2,1,0:T(8,128)(2,1)S(1)} %pad_maximum_fusion.1.refs_0_), channel_id=1, source_target_pairs={{0,3},{1,0},{2,1},{3,2},{4,7},{5,4},{6,5},{7,6},{8,11},{9,8},{10,9... | collective-permute-start | bytes 294920 | tf_op jit(solution)/shard_map/ppermute | solution.py:517
  159.1 10.6 %collective-permute-start.33 = (bf16[2,32,768]{2,1,0:T(8,128)(2,1)S(1)}, bf16[2,32,768]{2,1,0:T(8,128)(2,1)S(1)}, u32[]{:S(2)}, u32[]{:S(2)}) collective-permute-start(bf16[2,32,768]{2,1,0:T(8,128)(2,1)S(1)} %pad_maximum_fusion.1.refs_0_), channel_id=1, source_target_pairs={{0,2},{1,3},{2,0},{3,1},{4,6},{5,7},{6,4},{7,5},{8,10},{9,11},{10,... | collective-permute-start | bytes 294920 | tf_op jit(solution)/shard_map/ppermute | solution.py:517
  159.5 10.2 %collective-permute-start.32 = (bf16[2,32,768]{2,1,0:T(8,128)(2,1)S(1)}, bf16[2,32,768]{2,1,0:T(8,128)(2,1)S(1)}, u32[]{:S(2)}, u32[]{:S(2)}) collective-permute-start(bf16[2,32,768]{2,1,0:T(8,128)(2,1)S(1)} %pad_maximum_fusion.1.refs_0_), channel_id=1, source_target_pairs={{0,1},{1,2},{2,3},{3,0},{4,5},{5,6},{6,7},{7,4},{8,9},{9,10},{10,1... | collective-permute-start | bytes 294920 | tf_op jit(solution)/shard_map/ppermute | solution.py:517
  (48 other events, 339.3 us)

commit v2 on v1

v2 whole, which is shorter than its diff:
```python
import functools

import jax
import jax.numpy as jnp
from jax import lax
from jax.experimental import pallas as pl
from jax.experimental.pallas import tpu as pltpu
from jax.sharding import PartitionSpec as P


D = 256
HD = 32
FH = 1024
N1 = 1024
N2 = 2048
TB = 512
HC = 256
F32 = jnp.float32
BF = jnp.bfloat16
VMEM_LIMIT = 60 * 1024 * 1024


def mm(a, b):
    return jnp.dot(a, b, preferred_element_type=F32)


def mm_nt(a, b):
    return lax.dot_general(a, b, (((1,), (1,)), ((), ())), preferred_element_type=F32)


def split2(x):
    hi = x.astype(BF)
    return hi, (x - hi.astype(F32)).astype(BF)


def flip(x):
    return x.astype(F32).T


def head_mask(rows, cols):
    r = lax.broadcasted_iota(jnp.int32, (rows, cols), 0) // HD
    c = lax.broadcasted_iota(jnp.int32, (rows, cols), 1) // HD
    return r == c


def pack_heads(full):
    full = jnp.where(head_mask(D, D), full, 0.0)
    parts = []
    for g in range(2):
        cols = full[:, 128 * g : 128 * g + 128]
        parts.append(sum(cols[128 * g + HD * h : 128 * g + HD * h + HD] for h in range(4)))
    return parts


def unpack_heads(packed):
    mask = head_mask(128, 128)
    zero = jnp.zeros((128, 128), F32)
    blocks = []
    for g in range(2):
        piece = packed[HD * g : HD * g + HD]
        blocks.append(jnp.where(mask, jnp.concatenate([piece] * 4, axis=0), 0.0))
    top = jnp.concatenate([blocks[0], zero], axis=1)
    low = jnp.concatenate([zero, blocks[1]], axis=1)
    return jnp.concatenate([top, low], axis=0)


def ordered(core, own, other):
    first = core == 0
    return jnp.where(first, own, other), jnp.where(first, other, own)


def row_of(halves):
    return jnp.concatenate([half[HD : HD + 8] for half in halves], axis=1)


def heads_of(halves):
    return unpack_heads(jnp.concatenate([half[:HD] for half in halves], axis=0))


def column_of(row):
    n = row.shape[1]
    r = lax.broadcasted_iota(jnp.int32, (n, n), 0)
    c = lax.broadcasted_iota(jnp.int32, (n, n), 1)
    return jnp.sum(jnp.where(r == c, row, 0.0), axis=1, keepdims=True)


def whole(*shape):
    return pl.BlockSpec(shape, lambda i, at: (0,) * len(shape))


def call(kernel, grid, in_specs, out_specs, out_shape, flops, nbytes, name, scratch=()):
    return pl.pallas_call(
        kernel,
        grid_spec=pltpu.PrefetchScalarGridSpec(
            num_scalar_prefetch=1,
            grid=grid,
            in_specs=in_specs,
            out_specs=out_specs,
            scratch_shapes=list(scratch),
        ),
        out_shape=out_shape,
        compiler_params=pltpu.CompilerParams(vmem_limit_bytes=VMEM_LIMIT),
        cost_estimate=pl.CostEstimate(flops=int(flops), bytes_accessed=int(nbytes), transcendentals=0),
        name=name,
    )


def struct(shape, dtype):
    return jax.ShapeDtypeStruct(shape, dtype)


def keys_kernel(at_ref, tok_ref, keep_ref, coords_ref, wk_ref, wv_ref, km_ref, v_ref, slope_ref, ck_ref, keep_msg, send_msg, keep_m, send_m):
    core = at_ref[0]
    tok = tok_ref[...]
    tokt = flip(tok).astype(BF)
    kpre = mm(flip(wk_ref[...]).astype(BF), tokt)
    val = mm(flip(wv_ref[...]).astype(BF), tokt).astype(BF)
    keep = keep_ref[...].astype(F32)
    ck_ref[0:3, :] = coords_ref[...]
    ck_ref[3:4, :] = keep
    low = jnp.exp(jnp.minimum(kpre, 0.0))
    km = (keep * jnp.where(kpre > 0, kpre + 1.0, low)).astype(BF)
    km_ref[...] = km
    v_ref[...] = val
    slope_ref[...] = keep * jnp.where(kpre > 0, 1.0, low)
    parts = pack_heads(mm_nt(val, km))
    ks = mm_nt(jnp.ones((8, N1), BF), km)
    halves = [jnp.concatenate([parts[g], ks[:, 128 * g : 128 * g + 128]], axis=0) for g in range(2)]
    keep_msg[...], send_msg[...] = ordered(core, *halves)
    for ref, half in ((keep_m, core), (send_m, 1 - core)):
        rows = pl.ds(pl.multiple_of(half * 128, 128), 128)
        ref[...] = mm_nt(tokt, km_ref[rows, :]).astype(BF)


def keys_call(at, tokens, keep_row, coords, wk, wv):
    return call(
        keys_kernel,
        (1,),
        [whole(N1, D), whole(1, N1), whole(3, N1), whole(D, D), whole(D, D)],
        [whole(D, N1), whole(D, N1), whole(D, N1), whole(4, N1), whole(40, 128), whole(40, 128), whole(D, 128), whole(D, 128)],
        (
            struct((D, N1), BF), struct((D, N1), BF), struct((D, N1), F32), struct((4, N1), F32),
            struct((40, 128), F32), struct((40, 128), F32), struct((D, 128), BF), struct((D, 128), BF),
        ),
        4e8, 3e6, "keys",
    )(at, tokens, keep_row, coords, wk, wv)


def query_kernel(at_ref, tok_ref, oth_ref, wq_ref, tokt_ref, q_ref):
    wqt = flip(wq_ref[...]).astype(BF)
    for half, ref in enumerate((tok_ref, oth_ref)):
        tokt = flip(ref[...]).astype(BF)
        cols = slice(N1 * half, N1 * half + N1)
        tokt_ref[:, cols] = tokt
        pre = mm(wqt, tokt)
        q_ref[:, cols] = jnp.where(pre > 0, pre + 1.0, jnp.exp(jnp.minimum(pre, 0.0))).astype(BF)


def query_call(at, tokens, tokens_o, wq):
    return call(
        query_kernel, (1,), [whole(N1, D), whole(N1, D), whole(D, D)], [whole(D, N2), whole(D, N2)],
        (struct((D, N2), BF), struct((D, N2), BF)), 4e8, 3e6, "queries",
    )(at, tokens, tokens_o, wq)


def gate_kernel(at_ref, ck_ref, cko_ref, wgeo_ref, bgeo_ref, wroute_ref, r_ref, g_ref):
    geo = [column_of(wgeo_ref[k : k + 1, :]) for k in range(3)]
    bias = column_of(bgeo_ref[...])
    for half, ref in enumerate((ck_ref, cko_ref)):
        cols = slice(N1 * half, N1 * half + N1)
        pre = bias
        for k in range(3):
            pre = pre + geo[k] * ref[k : k + 1, :]
        r = jnp.tanh(pre)
        r_ref[:, cols] = r
        logit = lax.dot_general(
            wroute_ref[...], r, (((0,), (0,)), ((), ())), precision=lax.Precision.HIGHEST, preferred_element_type=F32
        )
        expo = jnp.exp(logit)
        g_ref[:, cols] = expo / jnp.sum(expo, axis=0, keepdims=True)


def gate_call(at, ck, ck_o, wgeo, bgeo, wroute):
    return call(
        gate_kernel, (1,), [whole(4, N1), whole(4, N1), whole(3, 64), whole(1, 64), whole(64, 8)],
        [whole(64, N2), whole(8, N2)], (struct((64, N2), F32), struct((8, N2), F32)), 1e8, 1e6, "gate",
    )(at, ck, ck_o, wgeo, bgeo, wroute)


def back_kernel(at_ref, cot_ref, oth_ref, ck_ref, cko_ref, win_ref, wout_ref, dyt_ref, back_ref, wint_ref):
    for half, (ref, keep_ref) in enumerate(((cot_ref, ck_ref), (oth_ref, cko_ref))):
        cot = ref[...]
        keep = keep_ref[3:4, :]
        cols = slice(N1 * half, N1 * half + N1)
        dyt_ref[:, cols] = (flip(cot) * keep).astype(BF)
        for j in range(0, FH, HC):
            back_ref[j : j + HC, cols] = (mm_nt(wout_ref[0, j : j + HC, :], cot) * keep).astype(BF)
    wint_ref[...] = flip(win_ref[0]).astype(BF)


def back_call(at, cot, cot_o, ck, ck_o, w_in, w_out):
    return call(
        back_kernel, (1,),
        [
            whole(N1, D), whole(N1, D), whole(4, N1), whole(4, N1),
            pl.BlockSpec((1, D, FH), lambda i, at: (at[0], 0, 0)),
            pl.BlockSpec((1, FH, D), lambda i, at: (at[0], 0, 0)),
        ],
        [whole(D, N2), whole(FH, N2), whole(FH, D)],
        (struct((D, N2), BF), struct((FH, N2), BF), struct((FH, D), BF)), 11e8, 8e6, "cotangent_back",
    )(at, cot, cot_o, ck, ck_o, w_in, w_out)


GELU_A = 0.7978845608028654
GELU_B = 0.7978845608028654 * 0.044715


def expert_kernel(
    at_ref, msg_ref, msgo_ref, m_ref, mo_ref, tokt_ref, q_ref, dyt_ref, back_ref, g_ref, r_ref, win_ref, wint_ref,
    own_ref, oth_ref, keep_msg, send_msg, pieces_ref,
    kvh, kvl, ksh, ksl, gw1, gw2, dkv, dks, route,
):
    step = pl.program_id(0)
    core, expert = at_ref[0], at_ref[1]

    @pl.when(step == 0)
    def _():
        halves = ordered(core, msg_ref[...], msgo_ref[...])
        hi, lo = split2(heads_of(halves))
        kvh[...] = hi
        kvl[...] = lo
        hi, lo = split2(jnp.where(head_mask(D, D), row_of(halves)[0:1], 0.0))
        ksh[...] = hi
        ksl[...] = lo
        gw1[...] = jnp.zeros_like(gw1)
        gw2[...] = jnp.zeros_like(gw2)
        dkv[...] = jnp.zeros_like(dkv)
        dks[...] = jnp.zeros_like(dks)
        route[...] = jnp.zeros_like(route)

    q = q_ref[...]
    num = mm(kvh[...], q) + mm(kvl[...], q)
    rden = 1.0 / (mm(ksh[...], q) + mm(ksl[...], q))
    attn = num * rden
    mid = (tokt_ref[...].astype(F32) + attn).astype(BF)
    gates = g_ref[...]
    mine = lax.broadcasted_iota(jnp.int32, gates.shape, 0) == expert
    gate = jnp.sum(jnp.where(mine, gates, 0.0), axis=0, keepdims=True)
    dyt = dyt_ref[...].astype(F32)
    df = (dyt * gate).astype(BF)
    first = jnp.logical_and(at_ref[2] == 0, step < N1 // TB)
    dmid = dyt * jnp.where(first, 1.0, 0.0)
    stat = jnp.zeros((1, TB), F32)
    for j in range(0, FH, HC):
        rows = slice(j, j + HC)
        u = mm(wint_ref[rows, :], mid)
        u2 = u * u
        t = jnp.tanh(u * (GELU_A + GELU_B * u2))
        half = 0.5 + 0.5 * t
        act = (u * half).astype(BF)
        slope = half + 0.5 * u * (1.0 - t * t) * (GELU_A + 3.0 * GELU_B * u2)
        back = back_ref[rows, :].astype(F32)
        stat = stat + jnp.sum(act.astype(F32) * back, axis=0, keepdims=True)
        du = (back * gate * slope).astype(BF)
        gw2[rows, :] += mm_nt(act, df)
        gw1[rows, :] += mm_nt(du, mid)
        dmid = dmid + mm(win_ref[0, :, rows], du)
    stat = stat * gate
    turn = (jnp.where(mine, 1.0, 0.0) - gates) * stat
    route[...] += lax.dot_general(
        turn, r_ref[...], (((1,), (1,)), ((), ())), precision=lax.Precision.HIGHEST, preferred_element_type=F32
    )
    dnum = dmid * rden
    dden = -jnp.sum((dnum * attn).reshape(8, HD, TB), axis=1)
    hi, lo = split2(dnum)
    dkv[...] += mm_nt(q, hi) + mm_nt(q, lo)
    hi, lo = split2(dden)
    dks[...] += mm_nt(hi, q) + mm_nt(lo, q)

    @pl.when(step < N1 // TB)
    def _():
        own_ref[...] = dmid.astype(BF)

    @pl.when(step >= N1 // TB)
    def _():
        oth_ref[...] = dmid.astype(BF)

    @pl.when(step == N2 // TB - 1)
    def _():
        m = (m_ref[...].astype(F32) + mo_ref[...].astype(F32)).astype(BF)
        for k in range(16):
            rows = slice(64 * k, 64 * k + 64)
            pieces_ref[k, 0:64, :] = gw1[rows, :].astype(BF)
            pieces_ref[k, 64:128, :] = gw2[rows, :].astype(BF)
            pieces_ref[k, 128:144, 0:128] = m[16 * k : 16 * k + 16]
            pieces_ref[k, 128:144, 128:256] = jnp.zeros((16, 128), BF)
        parts = pack_heads(dkv[...])
        r = lax.broadcasted_iota(jnp.int32, (8, D), 0)
        c = lax.broadcasted_iota(jnp.int32, (8, D), 1) // HD
        sums = jnp.where(r == c, dks[...], 0.0)
        last = [jnp.concatenate([route[...], jnp.zeros((8, 64), F32)], axis=1), jnp.zeros((8, 128), F32)]
        halves = [jnp.concatenate([parts[g], sums[:, 128 * g : 128 * g + 128], last[g]], axis=0) for g in range(2)]
        keep_msg[...], send_msg[...] = ordered(core, *halves)


def expert_call(at, msg, msg_o, m, m_o, tokt, q, dyt, back, g, r, w_in, wint):
    steps, own = N2 // TB, N1 // TB
    by_points = lambda rows: pl.BlockSpec((rows, TB), lambda i, at: (0, i))
    return call(
        expert_kernel, (steps,),
        [whole(40, 128), whole(40, 128), whole(D, 128), whole(D, 128)]
        + [by_points(rows) for rows in (D, D, D, FH, 8, 64)]
        + [pl.BlockSpec((1, D, FH), lambda i, at: (at[0], 0, 0)), whole(FH, D)],
        [
            pl.BlockSpec((D, TB), lambda i, at: (0, jnp.minimum(i, own - 1))),
            pl.BlockSpec((D, TB), lambda i, at: (0, jnp.maximum(i - own, 0))),
            whole(48, 128), whole(48, 128), whole(16, 144, D),
        ],
        (
            struct((D, N1), BF), struct((D, N1), BF), struct((48, 128), F32), struct((48, 128), F32),
            struct((16, 144, D), BF),
        ),
        6e9, 12e6, "expert",
        [pltpu.VMEM((D, D), BF)] * 4
        + [pltpu.VMEM((FH, D), F32)] * 2
        + [pltpu.VMEM((D, D), F32), pltpu.VMEM((8, D), F32), pltpu.VMEM((8, 64), F32)],
    )(at, msg, msg_o, m, m_o, tokt, q, dyt, back, g, r, w_in, wint)


def back_query_kernel(at_ref, d0, d1, d2, d3, msg_ref, msgo_ref, tokt_ref, q_ref, wq_ref, gx_ref, gq_ref):
    dmid = (d0[...].astype(F32) + d1[...].astype(F32)) + (d2[...].astype(F32) + d3[...].astype(F32))
    q = q_ref[...]
    tokt = tokt_ref[...]
    halves = ordered(at_ref[0], msg_ref[...], msgo_ref[...])
    kvt = heads_of(halves)
    kvth, kvtl = split2(kvt)
    kvh, kvl = split2(kvt.T)
    ks = row_of(halves)[0:1]
    mask = head_mask(D, D)
    ksh, ksl = split2(jnp.where(mask, ks, 0.0))
    kch, kcl = split2(jnp.where(mask, column_of(ks), 0.0))
    num = mm(kvth, q) + mm(kvtl, q)
    rden = 1.0 / (mm(ksh, q) + mm(ksl, q))
    attn = num * rden
    dnum = dmid * rden
    nh, nl = split2(dnum)
    zh, zl = split2(dnum * attn)
    dq = (mm(kvh, nh) - mm(kch, zh)) + (mm(kvl, nh) - mm(kcl, zh)) + (mm(kvh, nl) - mm(kch, zl))
    wq = wq_ref[...]
    pre = mm(flip(wq).astype(BF), tokt)
    dqp = (dq * jnp.where(pre > 0, 1.0, jnp.exp(jnp.minimum(pre, 0.0)))).astype(BF)
    gx_ref[...] = dmid + mm(wq, dqp)
    gq_ref[...] = mm_nt(tokt, dqp)


def back_query_call(at, dm, msg, msg_o, tokt, q, wq):
    return call(
        back_query_kernel, (1,),
        [whole(D, N1)] * 4 + [whole(40, 128), whole(40, 128), whole(D, N1), whole(D, N1), whole(D, D)],
        [whole(D, N1), whole(D, D)], (struct((D, N1), F32), struct((D, D), F32)), 2e9, 5e6, "back_query",
    )(at, *dm, msg, msg_o, tokt, q, wq)


def back_keys_kernel(at_ref, msg_ref, msgo_ref, km_ref, v_ref, slope_ref, tokt_ref, gq_ref, dk_ref, dv_ref, keep_ref, send_ref):
    core = at_ref[0]
    halves = ordered(core, msg_ref[...], msgo_ref[...])
    dkv = heads_of(halves)
    dks = jnp.sum(row_of(halves), axis=0, keepdims=True)
    hi, lo = split2(dkv)
    v = v_ref[...]
    dk = mm(hi, v) + mm(lo, v) + column_of(dks)
    dk = (dk * slope_ref[...]).astype(BF)
    hi, lo = split2(dkv.T)
    km = km_ref[...]
    dk_ref[...] = dk
    dv_ref[...] = (mm(hi, km) + mm(lo, km)).astype(BF)
    for ref, part in ((keep_ref, core), (send_ref, 1 - core)):
        rows = pl.ds(pl.multiple_of(part * 128, 128), 128)
        ref[:, 0:D] = gq_ref[rows, :].astype(BF)
        ref[:, D : 2 * D] = mm_nt(tokt_ref[rows, :], dk).astype(BF)


def back_keys_call(at, msg, msg_o, km, v, slope, tokt, gq):
    return call(
        back_keys_kernel, (1,), [whole(48, 128)] * 2 + [whole(D, N1)] * 4 + [whole(D, D)],
        [whole(D, N1), whole(D, N1), whole(128, 2 * D), whole(128, 2 * D)],
        (struct((D, N1), BF), struct((D, N1), BF), struct((128, 2 * D), BF), struct((128, 2 * D), BF)),
        1e9, 4e6, "back_keys",
    )(at, msg, msg_o, km, v, slope, tokt, gq)


def grad_x_kernel(at_ref, gx_ref, dk_ref, dv_ref, wk_ref, wv_ref, out_ref):
    total = gx_ref[...] + mm(wk_ref[...], dk_ref[...]) + mm(wv_ref[...], dv_ref[...])
    out_ref[...] = total.T.astype(BF)


def grad_x_call(at, gx, dk, dv, wk, wv):
    return call(
        grad_x_kernel, (1,), [whole(D, N1)] * 3 + [whole(D, D)] * 2, [whole(N1, D)], (struct((N1, D), BF),),
        3e8, 3e6, "grad_x",
    )(at, gx, dk, dv, wk, wv)[0]


def place_kernel(at_ref, own_ref, oth_ref, gin_ref, gout_ref):
    def put(ref):
        parts = [ref[k, 0:64, :].astype(F32) for k in range(4)]
        gin_ref[0] = jnp.concatenate(parts, axis=0).T
        for k in range(4):
            gout_ref[0, 64 * k : 64 * k + 64, :] = ref[k, 64:128, :].astype(F32)

    step = pl.program_id(0)
    pl.when(step < 4)(lambda: put(own_ref))
    pl.when(step >= 4)(lambda: put(oth_ref))


def place_call(at, own, oth):
    expert = lambda i, at: jnp.where(i < 4, at[0], 1 - at[0])
    return call(
        place_kernel, (8,),
        [
            pl.BlockSpec((4, 144, D), lambda i, at: (jnp.minimum(i, 3), 0, 0)),
            pl.BlockSpec((4, 144, D), lambda i, at: (jnp.maximum(i - 4, 0), 0, 0)),
        ],
        [
            pl.BlockSpec((1, D, 256), lambda i, at: (expert(i, at), 0, lax.rem(i, 4))),
            pl.BlockSpec((1, 256, D), lambda i, at: (expert(i, at), lax.rem(i, 4), 0)),
        ],
        (struct((2, D, FH), F32), struct((2, FH, D), F32)), 1e6, 7e6, "place_experts",
    )(at, own, oth)


def place_m_kernel(at_ref, msg_ref, msgo_ref, own_ref, oth_ref, gv_ref, route_ref):
    core, y = at_ref[0], at_ref[2]
    halves = ordered(core, msg_ref[...], msgo_ref[...])
    hi, lo = split2(heads_of(halves))
    own = jnp.concatenate([own_ref[k, :, 0:128].astype(F32) for k in range(16)], axis=0)
    oth = jnp.concatenate([oth_ref[k, :, 0:128].astype(F32) for k in range(16)], axis=0)
    m = jnp.concatenate(ordered(core, own, oth), axis=1).astype(BF)
    gv_ref[...] = mm(m, hi) + mm(m, lo)
    sums = halves[0][40:48, 0:64]
    at_row = lax.broadcasted_iota(jnp.int32, sums.shape, 0)
    cols = [column_of(jnp.sum(jnp.where(at_row == 2 * y + e, sums, 0.0), axis=0, keepdims=True)) for e in range(2)]
    route_ref[...] = jnp.concatenate(cols, axis=1)


def place_m_call(at, msg, msg_o, own, oth):
    last = pl.BlockSpec((16, 16, D), lambda i, at: (0, 8, 0))
    return call(
        place_m_kernel, (1,), [whole(48, 128)] * 2 + [last] * 2, [whole(D, D), whole(64, 2)],
        (struct((D, D), F32), struct((64, 2), F32)), 1e8, 1e6, "grad_wv",
    )(at, msg, msg_o, own, oth)


def place_proj_kernel(at_ref, own_ref, oth_ref, gq_ref, gk_ref):
    core = at_ref[0]
    for ref, part in ((own_ref, core), (oth_ref, 1 - core)):
        rows = pl.ds(pl.multiple_of(part * 128, 128), 128)
        gq_ref[rows, :] = ref[:, 0:D].astype(F32)
        gk_ref[rows, :] = ref[:, D : 2 * D].astype(F32)


def place_proj_call(at, own, oth):
    return call(
        place_proj_kernel, (1,), [whole(128, 2 * D)] * 2, [whole(D, D)] * 2, (struct((D, D), F32),) * 2,
        1e6, 1e6, "place_projections",
    )(at, own, oth)


def swap_core(v):
    return lax.ppermute(v, "pts", [(i, i ^ 1) for i in range(32)])


def to_x(v, d):
    return lax.ppermute(v, "pts", [(i, (i & ~6) | ((i + 2 * d) & 6)) for i in range(32)])


def to_z(v, d):
    return lax.ppermute(v, "pts", [(i, (i + 8 * d) % 32) for i in range(32)])


def to_y(v, d):
    return lax.ppermute(v, "exp", [(i, (i + d) % 4) for i in range(4)])


def star(v, to):
    return [to(v, d) for d in (1, 2, 3)]


def star_sum(v, to):
    a, b, c = star(v, to)
    if v.dtype == BF:
        return ((v.astype(F32) + a.astype(F32)) + (b.astype(F32) + c.astype(F32))).astype(BF)
    return (v + a) + (b + c)


CHIPS = [[2 * k + core for k in range(16)] for core in range(2)]


def exchange(v):
    return lax.all_to_all(v, "pts", 0, 0, axis_index_groups=CHIPS)


def chips_sum(v):
    every = exchange(jnp.broadcast_to(v[None], (16,) + v.shape))
    return jnp.sum(every.astype(F32), axis=0)


def on_device(
    tokens, coords, keep, cotangent, w_query, w_key, w_value, w_geo, b_geo, w_route, w_in, w_out
):
    pts = lax.axis_index("pts")
    y = lax.axis_index("exp")
    core = pts % 2
    at = jnp.stack([core, 2 * y + core, y]).astype(jnp.int32)

    tokens_o, cot_o = swap_core(tokens), swap_core(cotangent)
    km, v, slope, ck, msg, msg_away, m, m_away = keys_call(at, tokens, keep[None, :], coords, w_key, w_value)
    msg = msg + swap_core(msg_away)
    msg = chips_sum(msg)
    msg_o = swap_core(msg)
    ck_o, m_o = swap_core(ck), swap_core(m_away)

    tokt, q = query_call(at, tokens, tokens_o, w_query)
    dyt, back, wint = back_call(at, cotangent, cot_o, ck, ck_o, w_in, w_out)
    r, g = gate_call(at, ck, ck_o, w_geo, b_geo[None, :], w_route)

    own, oth, msg2, msg2_away, pieces = expert_call(
        at, msg, msg_o, m, m_o, tokt, q, dyt, back, g, r, w_in, wint
    )

    pieces = exchange(pieces)
    pieces = jnp.sum(pieces.astype(F32), axis=0).astype(BF)

    msg2 = msg2 + swap_core(msg2_away)
    msg2 = star_sum(msg2, to_y)
    msg2 = chips_sum(msg2)
    msg2_o = swap_core(msg2)

    own = (own.astype(F32) + swap_core(oth).astype(F32)).astype(BF)
    dm = [own] + star(own, to_y)

    gx, gq = back_query_call(at, dm, msg, msg_o, tokt, q, w_query)
    dk, dv, part, away = back_keys_call(at, msg2, msg2_o, km, v, slope, tokt, gq)

    pieces = exchange(jnp.broadcast_to(pieces[None], (16,) + pieces.shape))
    pieces_o = swap_core(pieces)
    grad_w_in, grad_w_out = place_call(at, pieces, pieces_o)
    grad_wv, grad_route = place_m_call(at, msg2, msg2_o, pieces, pieces_o)

    part = (part.astype(F32) + swap_core(away).astype(F32)).astype(BF)
    part = star_sum(part, to_x)
    part = star_sum(part, to_z)
    grad_wq, grad_wk = place_proj_call(at, part, swap_core(part))

    grad_x = grad_x_call(at, gx, dk, dv, w_key, w_value)
    return (grad_x, grad_wq, grad_wk, grad_wv, grad_w_in, grad_w_out, grad_route)


def solution(mesh):
    in_specs = (
        P("pts", None),
        P(None, "pts"),
        P("pts"),
        P("pts", None),
        P(),
        P(),
        P(),
        P(),
        P(),
        P(),
        P("exp", None, None),
        P("exp", None, None),
    )
    out_specs = (
        P("pts", None),
        P(),
        P(),
        P(),
        P("exp", None, None),
        P("exp", None, None),
        P(None, "exp"),
    )
    return jax.shard_map(
        on_device, mesh=mesh, in_specs=in_specs, out_specs=out_specs, check_vma=False
    )
```

time: 174 us -> 191 us (1.098)
  waiting for transfers between devices: 37.4 us -> 71.6 us
  starting transfers between devices: 65.6 us -> 43.4 us
  Pallas kernels: 53.5 us -> 60.9 us
  other arithmetic: 6.62 us -> 2.78 us
    all_to_all x0 -> x4, waiting for transfers between devices: none -> 25.1 us  [exchange(): return lax.all_to_all(v, 'pts', 0, 0, axis_index_groups=CHIPS)]
    all_to_all x0 -> x4, starting transfers between devices: none -> 19.1 us  [exchange(): return lax.all_to_all(v, 'pts', 0, 0, axis_index_groups=CHIPS)]
    ppermute x15 -> x3, starting transfers between devices: 17.9 us -> 3.68 us  [to_x(): lax.ppermute(v, 'pts', [(i, i & ~6 | i + 2 * d & 6) for i in range(32)])]
    ppermute x15 -> x3, starting transfers between devices: 17.7 us -> 3.67 us  [to_z(): return lax.ppermute(v, 'pts', [(i, (i + 8 * d) % 32) for i in range(32)])]
    ppermute x12, starting transfers between devices: 22.1 us -> 9.25 us  [swap_core(): return lax.ppermute(v, 'pts', [(i, i ^ 1) for i in range(32)])]
    pallas_call x10 -> x11, Pallas kernels: 53.5 us -> 60.9 us  [the longest x1 18.8 us: expert_call(): call(expert_kernel, (steps,), [whole(40, 128), whole(40, 128), whole(D, 1...]
    ppermute x15 -> x3, waiting for transfers between devices: 4.13 us -> 8.59 us  [to_z(): return lax.ppermute(v, 'pts', [(i, (i + 8 * d) % 32) for i in range(32)])]
    ppermute x9 -> x6, waiting for transfers between devices: 22.8 us -> 25.7 us  [to_y(): return lax.ppermute(v, 'exp', [(i, (i + d) % 4) for i in range(4)])]
  transfers between devices with their start and end apart: 51 -> 28, of which waited for: 15 -> 18; matrix products, arithmetic and copies ran while one was open for 6% -> 3% of each run, Pallas kernels for 13% -> 17%
where the time goes in v2:
time: 191 us; the launch traced here: 189 us
  waiting for transfers between devices  71.6 us (37%)
  Pallas kernels  60.9 us (32%)
  starting transfers between devices  43.4 us (23%)
  local copies, waits for them, and re-layouts  9.83 us (5%)
  other arithmetic  2.78 us (1%)
    ppermute x6, waiting for transfers between devices, to_y(): return lax.ppermute(v, 'exp', [(i, (i + d) % 4) for i in range(4)])  25.7 us
    all_to_all x4, waiting for transfers between devices, exchange(): return lax.all_to_all(v, 'pts', 0, 0, axis_index_groups=CHIPS)  25.1 us
    all_to_all x4, starting transfers between devices, exchange(): return lax.all_to_all(v, 'pts', 0, 0, axis_index_groups=CHIPS)  19.1 us
    pallas_call x1, Pallas kernels, expert_call(): call(expert_kernel, (steps,), [whole(40, 128), whole(40, 128), whole(D, 1...  18.8 us
    ppermute x12, starting transfers between devices, swap_core(): return lax.ppermute(v, 'pts', [(i, i ^ 1) for i in range(32)])  9.25 us
    ppermute x3, waiting for transfers between devices, to_z(): return lax.ppermute(v, 'pts', [(i, (i + 8 * d) % 32) for i in range(32)])  8.59 us
    ppermute x3, waiting for transfers between devices, to_x(): lax.ppermute(v, 'pts', [(i, i & ~6 | i + 2 * d & 6) for i in range(32)])  8.58 us
    ppermute x6, starting transfers between devices, to_y(): return lax.ppermute(v, 'exp', [(i, (i + d) % 4) for i in range(4)])  7.76 us
  transfers between devices with their start and end apart: 28, of which 18 were waited for; matrix products, arithmetic and copies ran while one was open for 3% of the time, Pallas kernels for 17%

profile of v2, /device:TPU:1, one launch (start us, length us, event | category | flops | bytes accessed | tf_op | source)
XLA Modules:
  0.0 189.4 jit_solution(10733273519866361310)
XLA Ops:
  2.8 4.0 %keys.1 = (bf16[256,1024]{1,0:T(8,128)(2,1)}, bf16[256,1024]{1,0:T(8,128)(2,1)}, f32[256,1024]{1,0:T(8,128)}, f32[4,1024]{1,0:T(4,128)}, f32[40,128]{1,0:T(8,128...) custom-call(s32[3]{0:T(128)} %pad_add_fusion.at_ref, bf16[1024,256]{1,0:T(8,128)(2,1)} %tok_ref.3, ...), custom_call_target="tpu_custom_call" | custom-call | flops 400000000 | bytes 3000000 | tf_op jit(solution)/shard_map/keys/pallas_call | solution.py:136
  9.8 7.7 %all-to-all-start = ((f32[16,40,128]{2,1,0:T(8,128)}), f32[16,40,128]{2,1,0:T(8,128)S(1)}, u32[]{:S(2)}, u32[]{:S(2)}) async-start(f32[16,40,128]{2,1,0:T(8,128)} %broadcast_in_dim.11), calls=%async_computation | async-start | bytes 655360 | tf_op jit(solution)/shard_map/all_to_all | solution.py:500
  19.8 2.7 %gate.1 = (f32[64,2048]{1,0:T(8,128)}, f32[8,2048]{1,0:T(8,128)}) custom-call(s32[3]{0:T(128)} %pad_add_fusion.at_ref, f32[4,1024]{1,0:T(4,128)} %get-tuple-element.45.ck_ref, f32[4,1024]{1,0:T(4,128)} %copy-done.18, f32[3,64]{1,0:T(4,128)} %wgeo_ref.1, f32[1,64]{1,0:T(1,128)} %bitcast.6, f32[64,8]{1,0:T(8,128)} %copy.21.wroute_ref), custom_call_target="tpu_custom_call" | custom-call | flops 100000000 | bytes 1000000 | tf_op jit(solution)/shard_map/gate/pallas_call | solution.py:184
  22.5 3.8 %all-to-all-done = f32[16,40,128]{2,1,0:T(8,128)S(1)} async-done(((f32[16,40,128]{2,1,0:T(8,128)}), f32[16,40,128]{2,1,0:T(8,128)S(1)}, u32[]{:S(2)}, u32[]{:S(2)}) %all-to-all-start) | async-done | bytes 327712 | tf_op jit(solution)/shard_map/all_to_all | solution.py:500
  28.7 6.0 %cotangent_back.1 = (bf16[256,2048]{1,0:T(8,128)(2,1)}, bf16[1024,2048]{1,0:T(8,128)(2,1)}, bf16[1024,256]{1,0:T(8,128)(2,1)}) custom-call(s32[3]{0:T(128)} %pad_add_fusion.at_ref, bf16[1024,256]{1,0:T(8,128)(2,1)} %cot_ref.1, bf16[1024,256]{1,0:T(8,128)(2,1)} %copy-done.12, f32[4,1024]{1,0:T(4,128)} %get-tuple-element.45.ck_ref, f32[4,1024]{1,0:T(4,128)} %copy-done.18, ...), custom_call_target="tpu_custom_call" | custom-call | flops 1100000000 | bytes 8000000 | tf_op jit(solution)/shard_map/cotangent_back/pallas_call | solution.py:202
  35.5 3.8 %queries.1 = (bf16[256,2048]{1,0:T(8,128)(2,1)}, bf16[256,2048]{1,0:T(8,128)(2,1)}) custom-call(s32[3]{0:T(128)} %pad_add_fusion.at_ref, bf16[1024,256]{1,0:T(8,128)(2,1)} %tok_ref.3, bf16[1024,256]{1,0:T(8,128)(2,1)} %copy-done.11, bf16[256,256]{1,0:T(8,128)(2,1)} %wq_ref.3), custom_call_target="tpu_custom_call" | custom-call | flops 400000000 | bytes 3000000 | tf_op jit(solution)/shard_map/queries/pallas_call | solution.py:160
  39.9 18.8 %expert.1 = (bf16[256,1024]{1,0:T(8,128)(2,1)}, bf16[256,1024]{1,0:T(8,128)(2,1)}, f32[48,128]{1,0:T(8,128)}, f32[48,128]{1,0:T(8,128)}, bf16[16,144,256]{2,1,0:T(8,128)(2,1)}) custom-call(s32[3]{0:T(128)} %pad_add_fusion.at_ref, f32[40,128]{1,0:T(8,128)} %copy-done.9, f32[40,128]{1,0:T(8,128)} %copy-done.17, bf16[256,128]{1,0:T(8,128)(2,1)} %get-tuple-element.41.m_ref, ...), custom_call_target="tpu_custom_call" | custom-call | flops 6000000000 | bytes 12000000 | tf_op jit(solution)/shard_map/expert/pallas_call | solution.py:309
  58.7 3.8 %all-to-all-start.2 = ((bf16[16,144,256]{2,1,0:T(8,128)(2,1)}), bf16[16,144,256]{2,1,0:T(8,128)(2,1)S(1)}, u32[]{:S(2)}, u32[]{:S(2)}) async-start(bf16[16,144,256]{2,1,0:T(8,128)(2,1)} %get-tuple-element.66), calls=%async_computation.2 | async-start | bytes 2359296 | tf_op jit(solution)/shard_map/all_to_all | solution.py:500
  63.8 2.8 %collective-permute-start.13 = (f32[48,128]{1,0:T(8,128)S(1)}, f32[48,128]{1,0:T(8,128)S(1)}, u32[]{:S(2)}, u32[]{:S(2)}) collective-permute-start(f32[48,128]{1,0:T(8,128)S(1)} %add.50), channel_id=1, source_target_pairs={{0,3},{1,0},{2,1},{3,2},{4,7},{5,4},{6,5},{7,6},{8,11},{9,8},{10,9... | collective-permute-start | bytes 73736 | tf_op jit(solution)/shard_map/ppermute | solution.py:482
  71.4 12.3 %all-to-all-done.2 = bf16[16,144,256]{2,1,0:T(8,128)(2,1)S(1)} async-done(((bf16[16,144,256]{2,1,0:T(8,128)(2,1)}), bf16[16,144,256]{2,1,0:T(8,128)(2,1)S(1)}, u32[]{:S(2)}, u32[]{:S(2)}) %all-to-all-start.2) | async-done | bytes 1179680 | tf_op jit(solution)/shard_map/all_to_all | solution.py:500
  84.5 3.7 %all-to-all-start.1 = ((f32[16,48,128]{2,1,0:T(8,128)}), f32[16,48,128]{2,1,0:T(8,128)S(1)}, u32[]{:S(2)}, u32[]{:S(2)}) async-start(f32[16,48,128]{2,1,0:T(8,128)} %broadcast_in_dim.13), calls=%async_computation.1 | async-start | bytes 786432 | tf_op jit(solution)/shard_map/all_to_all | solution.py:500
  88.4 9.0 %all-to-all-done.1 = f32[16,48,128]{2,1,0:T(8,128)S(1)} async-done(((f32[16,48,128]{2,1,0:T(8,128)}), f32[16,48,128]{2,1,0:T(8,128)S(1)}, u32[]{:S(2)}, u32[]{:S(2)}) %all-to-all-start.1) | async-done | bytes 393248 | tf_op jit(solution)/shard_map/all_to_all | solution.py:500
  98.4 3.8 %all-to-all-start.3 = ((bf16[16,144,256]{2,1,0:T(8,128)(2,1)}), bf16[16,144,256]{2,1,0:T(8,128)(2,1)S(1)}, u32[]{:S(2)}, u32[]{:S(2)}) async-start(bf16[16,144,256]{2,1,0:T(8,128)(2,1)} %broadcast_in_dim.28), calls=%async_computation.3 | async-start | bytes 2359296 | tf_op jit(solution)/shard_map/all_to_all | solution.py:500
  102.5 2.9 %collective-permute-start.9 = (bf16[256,1024]{1,0:T(8,128)(2,1)S(1)}, bf16[256,1024]{1,0:T(8,128)(2,1)S(1)}, u32[]{:S(2)}, u32[]{:S(2)}) collective-permute-start(bf16[256,1024]{1,0:T(8,128)(2,1)S(1)} %add_convert_fusion.d0), channel_id=1, source_target_pairs={{0,3},{1,0},{2,1},{3,2},{4,7},{5,4},{6,5},{7,6},{8,11},{9,8},{10,9... | collective-permute-start | bytes 1572872 | tf_op jit(solution)/shard_map/ppermute | solution.py:482
  109.1 7.0 %collective-permute-done.9.d3 = bf16[256,1024]{1,0:T(8,128)(2,1)S(1)} collective-permute-done((bf16[256,1024]{1,0:T(8,128)(2,1)S(1)}, bf16[256,1024]{1,0:T(8,128)(2,1)S(1)}, u32[]{:S(2)}, u32[]{:S(2)}) %collective-permute-start.9) | collective-permute-done | bytes 524320 | tf_op jit(solution)/shard_map/ppermute | solution.py:482
  118.5 13.5 %collective-permute-done.7.d1 = bf16[256,1024]{1,0:T(8,128)(2,1)} collective-permute-done((bf16[256,1024]{1,0:T(8,128)(2,1)S(1)}, bf16[256,1024]{1,0:T(8,128)(2,1)}, u32[]{:S(2)}, u32[]{:S(2)}) %collective-permute-start.7) | collective-permute-done | bytes 524320 | tf_op jit(solution)/shard_map/ppermute | solution.py:482
  132.1 5.8 %back_query.1 = (f32[256,1024]{1,0:T(8,128)}, f32[256,256]{1,0:T(8,128)}) custom-call(s32[3]{0:T(128)} %pad_add_fusion.at_ref, bf16[256,1024]{1,0:T(8,128)(2,1)} %copy-done.3, bf16[256,1024]{1,0:T(8,128)(2,1)} %collective-permute-done.7.d1, bf16[256,1024]{1,0:T(8,128)(2,1)} %collective-permute-done.8.d2, bf16[256,1024]{1,0:T(8,128)(2,1)} %copy-done.14, ...), custom_call_target="tpu_custom_call" | custom-call | flops 2000000000 | bytes 5000000 | tf_op jit(solution)/shard_map/back_query/pallas_call | solution.py:357
  138.5 4.1 %back_keys.1 = (bf16[256,1024]{1,0:T(8,128)(2,1)}, bf16[256,1024]{1,0:T(8,128)(2,1)}, bf16[128,512]{1,0:T(8,128)(2,1)}, bf16[128,512]{1,0:T(8,128)(2,1)}) custom-call(s32[3]{0:T(128)} %pad_add_fusion.at_ref, f32[48,128]{1,0:T(8,128)} %copy-done.6, f32[48,128]{1,0:T(8,128)} %copy-done.7, bf16[256,1024]{1,0:T(8,128)(2,1)} %get-tuple-element.56.km_ref, ...), custom_call_target="tpu_custom_call" | custom-call | flops 1000000000 | bytes 4000000 | tf_op jit(solution)/shard_map/back_keys/pallas_call | solution.py:384
  149.0 4.0 %collective-permute-done.18 = bf16[128,512]{1,0:T(8,128)(2,1)S(1)} collective-permute-done((bf16[128,512]{1,0:T(8,128)(2,1)S(1)}, bf16[128,512]{1,0:T(8,128)(2,1)S(1)}, u32[]{:S(2)}, u32[]{:S(2)}) %collective-permute-start.18) | collective-permute-done | bytes 131104 | tf_op jit(solution)/shard_map/ppermute | solution.py:474
  153.8 3.8 %collective-permute-done.16 = bf16[128,512]{1,0:T(8,128)(2,1)S(1)} collective-permute-done((bf16[128,512]{1,0:T(8,128)(2,1)S(1)}, bf16[128,512]{1,0:T(8,128)(2,1)S(1)}, u32[]{:S(2)}, u32[]{:S(2)}) %collective-permute-start.16) | collective-permute-done | bytes 131104 | tf_op jit(solution)/shard_map/ppermute | solution.py:474
  163.1 2.8 %collective-permute-done.20 = bf16[128,512]{1,0:T(8,128)(2,1)S(1)} collective-permute-done((bf16[128,512]{1,0:T(8,128)(2,1)S(1)}, bf16[128,512]{1,0:T(8,128)(2,1)S(1)}, u32[]{:S(2)}, u32[]{:S(2)}) %collective-permute-start.20) | collective-permute-done | bytes 131104 | tf_op jit(solution)/shard_map/ppermute | solution.py:478
  165.9 4.0 %collective-permute-done.19 = bf16[128,512]{1,0:T(8,128)(2,1)S(1)} collective-permute-done((bf16[128,512]{1,0:T(8,128)(2,1)S(1)}, bf16[128,512]{1,0:T(8,128)(2,1)S(1)}, u32[]{:S(2)}, u32[]{:S(2)}) %collective-permute-start.19) | collective-permute-done | bytes 131104 | tf_op jit(solution)/shard_map/ppermute | solution.py:478
  170.6 3.5 %grad_x.1 = bf16[1024,256]{1,0:T(8,128)(2,1)} custom-call(s32[3]{0:T(128)} %pad_add_fusion.at_ref, f32[256,1024]{1,0:T(8,128)} %get-tuple-element.53.gx_ref, bf16[256,1024]{1,0:T(8,128)(2,1)} %get-tuple-element.60.dk_ref, bf16[256,1024]{1,0:T(8,128)(2,1)} %get-tuple-element.61.dv_ref, bf16[256,256]{1,0:T(8,128)(2,1)} %wk_ref.3, bf16[256,256]{1,0:T(8,128)(2,1)} %wv_ref.3), custom_call_target="tpu_custom_call" | custom-call | flops 300000000 | bytes 3000000 | tf_op jit(solution)/shard_map/grad_x/pallas_call | solution.py:398
  182.3 7.1 %place_experts.1 = (f32[2,256,1024]{2,1,0:T(8,128)}, f32[2,1024,256]{2,1,0:T(8,128)}) custom-call(s32[3]{0:T(128)} %pad_add_fusion.at_ref, bf16[16,144,256]{2,1,0:T(8,128)(2,1)} %copy-done, bf16[16,144,256]{2,1,0:T(8,128)(2,1)} %copy-done.1), custom_call_target="tpu_custom_call" | custom-call | flops 1000000 | bytes 7000000 | tf_op jit(solution)/shard_map/place_experts/pallas_call | solution.py:418
  (97 shorter events, 47.7 us)
Async XLA Ops:
  0.6 27.3 %collective-permute-start.4 = (bf16[1024,256]{1,0:T(8,128)(2,1)}, bf16[1024,256]{1,0:T(8,128)(2,1)S(1)}, u32[]{:S(2)}, u32[]{:S(2)}) collective-permute-start(bf16[1024,256]{1,0:T(8,128)(2,1)} %cot_ref.1), channel_id=1, source_target_pairs={{0,4},{4,0},{8,12},{12,8},{16,20},{20,16},{24,28},{28,24},{32,36},... | collective-permute-start | bytes 1572872 | tf_op jit(solution)/shard_map/ppermute | solution.py:470
  2.1 32.5 %collective-permute-start.3 = (bf16[1024,256]{1,0:T(8,128)(2,1)}, bf16[1024,256]{1,0:T(8,128)(2,1)S(1)}, u32[]{:S(2)}, u32[]{:S(2)}) collective-permute-start(bf16[1024,256]{1,0:T(8,128)(2,1)} %tok_ref.3), channel_id=1, source_target_pairs={{0,4},{4,0},{8,12},{12,8},{16,20},{20,16},{24,28},{28,24},{32,36},... | collective-permute-start | bytes 1572872 | tf_op jit(solution)/shard_map/ppermute | solution.py:470
  9.8 16.5 %all-to-all-start = ((f32[16,40,128]{2,1,0:T(8,128)}), f32[16,40,128]{2,1,0:T(8,128)S(1)}, u32[]{:S(2)}, u32[]{:S(2)}) async-start(f32[16,40,128]{2,1,0:T(8,128)} %broadcast_in_dim.11), calls=%async_computation | async-start | bytes 655360 | tf_op jit(solution)/shard_map/all_to_all | solution.py:500
  18.2 21.1 %collective-permute-start.2 = (bf16[256,128]{1,0:T(8,128)(2,1)}, bf16[256,128]{1,0:T(8,128)(2,1)S(1)}, u32[]{:S(2)}, u32[]{:S(2)}) collective-permute-start(bf16[256,128]{1,0:T(8,128)(2,1)} %get-tuple-element.42), channel_id=1, source_target_pairs={{0,4},{4,0},{8,12},{12,8},{16,20},{20,16},{24,28},{28,24},{32,36},... | collective-permute-start | bytes 196616 | tf_op jit(solution)/shard_map/ppermute | solution.py:470
  26.3 12.9 %collective-permute-start.1 = (f32[40,128]{1,0:T(8,128)S(1)}, f32[40,128]{1,0:T(8,128)S(1)}, u32[]{:S(2)}, u32[]{:S(2)}) collective-permute-start(f32[40,128]{1,0:T(8,128)S(1)} %reduce_sum.30.msg_ref), channel_id=1, source_target_pairs={{0,4},{4,0},{8,12},{12,8},{16,20},{20,16},{24,28},{28,24},{32,36},... | collective-permute-start | bytes 61448 | tf_op jit(solution)/shard_map/ppermute | solution.py:470
  58.7 25.0 %all-to-all-start.2 = ((bf16[16,144,256]{2,1,0:T(8,128)(2,1)}), bf16[16,144,256]{2,1,0:T(8,128)(2,1)S(1)}, u32[]{:S(2)}, u32[]{:S(2)}) async-start(bf16[16,144,256]{2,1,0:T(8,128)(2,1)} %get-tuple-element.66), calls=%async_computation.2 | async-start | bytes 2359296 | tf_op jit(solution)/shard_map/all_to_all | solution.py:500
  63.8 4.8 %collective-permute-start.13 = (f32[48,128]{1,0:T(8,128)S(1)}, f32[48,128]{1,0:T(8,128)S(1)}, u32[]{:S(2)}, u32[]{:S(2)}) collective-permute-start(f32[48,128]{1,0:T(8,128)S(1)} %add.50), channel_id=1, source_target_pairs={{0,3},{1,0},{2,1},{3,2},{4,7},{5,4},{6,5},{7,6},{8,11},{9,8},{10,9... | collective-permute-start | bytes 73736 | tf_op jit(solution)/shard_map/ppermute | solution.py:482
  66.6 4.5 %collective-permute-start.12 = (f32[48,128]{1,0:T(8,128)S(1)}, f32[48,128]{1,0:T(8,128)S(1)}, u32[]{:S(2)}, u32[]{:S(2)}) collective-permute-start(f32[48,128]{1,0:T(8,128)S(1)} %add.50), channel_id=1, source_target_pairs={{0,2},{1,3},{2,0},{3,1},{4,6},{5,7},{6,4},{7,5},{8,10},{9,11},{10,... | collective-permute-start | bytes 73736 | tf_op jit(solution)/shard_map/ppermute | solution.py:482
  67.0 4.4 %collective-permute-start.11 = (f32[48,128]{1,0:T(8,128)S(1)}, f32[48,128]{1,0:T(8,128)S(1)}, u32[]{:S(2)}, u32[]{:S(2)}) collective-permute-start(f32[48,128]{1,0:T(8,128)S(1)} %add.50), channel_id=1, source_target_pairs={{0,1},{1,2},{2,3},{3,0},{4,5},{5,6},{6,7},{7,4},{8,9},{9,10},{10,1... | collective-permute-start | bytes 73736 | tf_op jit(solution)/shard_map/ppermute | solution.py:482
  67.7 34.6 %collective-permute-start.6 = (bf16[256,1024]{1,0:T(8,128)(2,1)S(1)}, bf16[256,1024]{1,0:T(8,128)(2,1)S(1)}, u32[]{:S(2)}, u32[]{:S(2)}) collective-permute-start(bf16[256,1024]{1,0:T(8,128)(2,1)S(1)} %copy-done.13), channel_id=1, source_target_pairs={{0,4},{4,0},{8,12},{12,8},{16,20},{20,16},{24,28},{28,24},{32,36},... | collective-permute-start | bytes 1572872 | tf_op jit(solution)/shard_map/ppermute | solution.py:470
  84.5 12.9 %all-to-all-start.1 = ((f32[16,48,128]{2,1,0:T(8,128)}), f32[16,48,128]{2,1,0:T(8,128)S(1)}, u32[]{:S(2)}, u32[]{:S(2)}) async-start(f32[16,48,128]{2,1,0:T(8,128)} %broadcast_in_dim.13), calls=%async_computation.1 | async-start | bytes 786432 | tf_op jit(solution)/shard_map/all_to_all | solution.py:500
  98.4 44.7 %all-to-all-start.3 = ((bf16[16,144,256]{2,1,0:T(8,128)(2,1)}), bf16[16,144,256]{2,1,0:T(8,128)(2,1)S(1)}, u32[]{:S(2)}, u32[]{:S(2)}) async-start(bf16[16,144,256]{2,1,0:T(8,128)(2,1)} %broadcast_in_dim.28), calls=%async_computation.3 | async-start | bytes 2359296 | tf_op jit(solution)/shard_map/all_to_all | solution.py:500
  102.5 13.5 %collective-permute-start.9 = (bf16[256,1024]{1,0:T(8,128)(2,1)S(1)}, bf16[256,1024]{1,0:T(8,128)(2,1)S(1)}, u32[]{:S(2)}, u32[]{:S(2)}) collective-permute-start(bf16[256,1024]{1,0:T(8,128)(2,1)S(1)} %add_convert_fusion.d0), channel_id=1, source_target_pairs={{0,3},{1,0},{2,1},{3,2},{4,7},{5,4},{6,5},{7,6},{8,11},{9,8},{10,9... | collective-permute-start | bytes 1572872 | tf_op jit(solution)/shard_map/ppermute | solution.py:482
  105.4 13.1 %collective-permute-start.8 = (bf16[256,1024]{1,0:T(8,128)(2,1)S(1)}, bf16[256,1024]{1,0:T(8,128)(2,1)}, u32[]{:S(2)}, u32[]{:S(2)}) collective-permute-start(bf16[256,1024]{1,0:T(8,128)(2,1)S(1)} %add_convert_fusion.d0), channel_id=1, source_target_pairs={{0,2},{1,3},{2,0},{3,1},{4,6},{5,7},{6,4},{7,5},{8,10},{9,11},{10,... | collective-permute-start | bytes 1572872 | tf_op jit(solution)/shard_map/ppermute | solution.py:482
  105.7 26.3 %collective-permute-start.7 = (bf16[256,1024]{1,0:T(8,128)(2,1)S(1)}, bf16[256,1024]{1,0:T(8,128)(2,1)}, u32[]{:S(2)}, u32[]{:S(2)}) collective-permute-start(bf16[256,1024]{1,0:T(8,128)(2,1)S(1)} %add_convert_fusion.d0), channel_id=1, source_target_pairs={{0,1},{1,2},{2,3},{3,0},{4,5},{5,6},{6,7},{7,4},{8,9},{9,10},{10,1... | collective-permute-start | bytes 1572872 | tf_op jit(solution)/shard_map/ppermute | solution.py:482
  106.5 31.5 %collective-permute-start.14 = (f32[48,128]{1,0:T(8,128)S(1)}, f32[48,128]{1,0:T(8,128)S(1)}, u32[]{:S(2)}, u32[]{:S(2)}) collective-permute-start(f32[48,128]{1,0:T(8,128)S(1)} %reduce_sum.31.msg_ref), channel_id=1, source_target_pairs={{0,4},{4,0},{8,12},{12,8},{16,20},{20,16},{24,28},{28,24},{32,36},... | collective-permute-start | bytes 73736 | tf_op jit(solution)/shard_map/ppermute | solution.py:470
  143.2 34.1 %collective-permute-start.23 = (bf16[16,144,256]{2,1,0:T(8,128)(2,1)S(1)}, bf16[16,144,256]{2,1,0:T(8,128)(2,1)S(1)}, u32[]{:S(2)}, u32[]{:S(2)}) collective-permute-start(bf16[16,144,256]{2,1,0:T(8,128)(2,1)S(1)} %all-to-all-done.3.own_ref), channel_id=1, source_target_pairs={{0,4},{4,0},{8,12},{12,8},{16,20},{20,16},{24,28},{28,24},{32,36},... | collective-permute-start | bytes 3538952 | tf_op jit(solution)/shard_map/ppermute | solution.py:470
  145.3 7.7 %collective-permute-start.18 = (bf16[128,512]{1,0:T(8,128)(2,1)S(1)}, bf16[128,512]{1,0:T(8,128)(2,1)S(1)}, u32[]{:S(2)}, u32[]{:S(2)}) collective-permute-start(bf16[128,512]{1,0:T(8,128)(2,1)S(1)} %add_convert_fusion.3), channel_id=1, source_target_pairs={{0,24},{4,28},{8,0},{12,4},{16,8},{20,12},{24,16},{28,20},{32,56},... | collective-permute-start | bytes 393224 | tf_op jit(solution)/shard_map/ppermute | solution.py:474
  147.8 5.9 %collective-permute-start.17 = (bf16[128,512]{1,0:T(8,128)(2,1)S(1)}, bf16[128,512]{1,0:T(8,128)(2,1)S(1)}, u32[]{:S(2)}, u32[]{:S(2)}) collective-permute-start(bf16[128,512]{1,0:T(8,128)(2,1)S(1)} %add_convert_fusion.3), channel_id=1, source_target_pairs={{0,16},{4,20},{8,24},{12,28},{16,0},{20,4},{24,8},{28,12},{32,48},... | collective-permute-start | bytes 393224 | tf_op jit(solution)/shard_map/ppermute | solution.py:474
  148.4 9.2 %collective-permute-start.16 = (bf16[128,512]{1,0:T(8,128)(2,1)S(1)}, bf16[128,512]{1,0:T(8,128)(2,1)S(1)}, u32[]{:S(2)}, u32[]{:S(2)}) collective-permute-start(bf16[128,512]{1,0:T(8,128)(2,1)S(1)} %add_convert_fusion.3), channel_id=1, source_target_pairs={{0,8},{4,12},{8,16},{12,20},{16,24},{20,28},{24,0},{28,4},{32,40},... | collective-permute-start | bytes 393224 | tf_op jit(solution)/shard_map/ppermute | solution.py:474
  157.6 5.5 %collective-permute-start.21 = (bf16[128,512]{1,0:T(8,128)(2,1)S(1)}, bf16[128,512]{1,0:T(8,128)(2,1)S(1)}, u32[]{:S(2)}, u32[]{:S(2)}) collective-permute-start(bf16[128,512]{1,0:T(8,128)(2,1)S(1)} %add_convert_fusion.2), channel_id=1, source_target_pairs={{0,96},{4,100},{8,104},{12,108},{16,112},{20,116},{24,120},{28,124... | collective-permute-start | bytes 393224 | tf_op jit(solution)/shard_map/ppermute | solution.py:478
  160.2 5.8 %collective-permute-start.20 = (bf16[128,512]{1,0:T(8,128)(2,1)S(1)}, bf16[128,512]{1,0:T(8,128)(2,1)S(1)}, u32[]{:S(2)}, u32[]{:S(2)}) collective-permute-start(bf16[128,512]{1,0:T(8,128)(2,1)S(1)} %add_convert_fusion.2), channel_id=1, source_target_pairs={{0,64},{4,68},{8,72},{12,76},{16,80},{20,84},{24,88},{28,92},{32,9... | collective-permute-start | bytes 393224 | tf_op jit(solution)/shard_map/ppermute | solution.py:478
  160.7 9.2 %collective-permute-start.19 = (bf16[128,512]{1,0:T(8,128)(2,1)S(1)}, bf16[128,512]{1,0:T(8,128)(2,1)S(1)}, u32[]{:S(2)}, u32[]{:S(2)}) collective-permute-start(bf16[128,512]{1,0:T(8,128)(2,1)S(1)} %add_convert_fusion.2), channel_id=1, source_target_pairs={{0,32},{4,36},{8,40},{12,44},{16,48},{20,52},{24,56},{28,60},{32,6... | collective-permute-start | bytes 393224 | tf_op jit(solution)/shard_map/ppermute | solution.py:478
  170.0 4.1 %collective-permute-start.22 = (bf16[128,512]{1,0:T(8,128)(2,1)S(1)}, bf16[128,512]{1,0:T(8,128)(2,1)S(1)}, u32[]{:S(2)}, u32[]{:S(2)}) collective-permute-start(bf16[128,512]{1,0:T(8,128)(2,1)S(1)} %add_convert_fusion.1.own_ref), channel_id=1, source_target_pairs={{0,4},{4,0},{8,12},{12,8},{16,20},{20,16},{24,28},{28,24},{32,36},... | collective-permute-start | bytes 393224 | tf_op jit(solution)/shard_map/ppermute | solution.py:470
  (23 other events, 169.8 us)

commit v3 on v2

v3 whole, which is shorter than its diff:
```python
import functools

import jax
import jax.numpy as jnp
from jax import lax
from jax.experimental import pallas as pl
from jax.experimental.pallas import tpu as pltpu
from jax.sharding import PartitionSpec as P


D = 256
HD = 32
FH = 1024
N1 = 1024
N2 = 2048
TB = 512
HC = 256
F32 = jnp.float32
BF = jnp.bfloat16


def mm(a, b):
    return jnp.dot(a, b, preferred_element_type=F32)


def mm_nt(a, b):
    return lax.dot_general(a, b, (((1,), (1,)), ((), ())), preferred_element_type=F32)


def split2(x):
    hi = x.astype(BF)
    return hi, (x - hi.astype(F32)).astype(BF)


def flip(x):
    return x.astype(F32).T


def head_mask(rows, cols):
    r = lax.broadcasted_iota(jnp.int32, (rows, cols), 0) // HD
    c = lax.broadcasted_iota(jnp.int32, (rows, cols), 1) // HD
    return r == c


def pack_heads(full):
    full = jnp.where(head_mask(D, D), full, 0.0)
    parts = []
    for g in range(2):
        cols = full[:, 128 * g : 128 * g + 128]
        parts.append(sum(cols[128 * g + HD * h : 128 * g + HD * h + HD] for h in range(4)))
    return parts


def unpack_heads(packed):
    mask = head_mask(128, 128)
    zero = jnp.zeros((128, 128), F32)
    blocks = []
    for g in range(2):
        piece = packed[HD * g : HD * g + HD]
        blocks.append(jnp.where(mask, jnp.concatenate([piece] * 4, axis=0), 0.0))
    top = jnp.concatenate([blocks[0], zero], axis=1)
    low = jnp.concatenate([zero, blocks[1]], axis=1)
    return jnp.concatenate([top, low], axis=0)


def ordered(core, own, other):
    first = core == 0
    return jnp.where(first, own, other), jnp.where(first, other, own)


def row_of(halves):
    return jnp.concatenate([half[HD : HD + 8] for half in halves], axis=1)


def heads_of(halves):
    return unpack_heads(jnp.concatenate([half[:HD] for half in halves], axis=0))


def column_of(row):
    n = row.shape[1]
    r = lax.broadcasted_iota(jnp.int32, (n, n), 0)
    c = lax.broadcasted_iota(jnp.int32, (n, n), 1)
    return jnp.sum(jnp.where(r == c, row, 0.0), axis=1, keepdims=True)


def call(kernel, out_shape, flops, nbytes, name, scratch=(), after=(), limit=8, fetch=0):
    def run(at, *args):
        n_in, n_after = len(args), len(after)

        def body(*refs):
            ins, outs = list(refs[1 : 1 + n_in]), refs[1 + n_in + n_after :]
            if fetch:
                outs, bufs, sems = outs[: -fetch - 1], outs[-fetch - 1 : -1], outs[-1]
                copies = [pltpu.make_async_copy(ins[k], bufs[k], sems.at[k]) for k in range(fetch)]
                for copy in copies:
                    copy.start()
                for copy in copies:
                    copy.wait()
                ins[:fetch] = bufs
            kernel(refs[0], *ins, *outs)

        in_vmem = pl.BlockSpec(memory_space=pltpu.VMEM)
        in_any = pl.BlockSpec(memory_space=pl.ANY)
        more = [pltpu.VMEM(x.shape, x.dtype) for x in args[:fetch]]
        return pl.pallas_call(
            body,
            in_specs=[pl.BlockSpec(memory_space=pltpu.SMEM)]
            + [pl.BlockSpec(memory_space=pltpu.HBM)] * fetch
            + [in_vmem] * (n_in - fetch)
            + [in_any] * n_after,
            out_specs=[in_vmem] * len(out_shape),
            out_shape=out_shape,
            scratch_shapes=list(scratch) + (more + [pltpu.SemaphoreType.DMA((fetch,))] if fetch else []),
            compiler_params=pltpu.CompilerParams(vmem_limit_bytes=limit * 1024 * 1024),
            cost_estimate=pl.CostEstimate(flops=int(flops), bytes_accessed=int(nbytes), transcendentals=0),
            name=name,
        )(at, *args, *after)

    return run


def struct(shape, dtype):
    return jax.ShapeDtypeStruct(shape, dtype)


def add(terms, after=(), dtype=BF):
    if after:
        terms = lax.optimization_barrier((*terms, *after))[: len(terms)]
    total = terms[0].astype(F32)
    for term in terms[1:]:
        total = total + term.astype(F32)
    return total.astype(dtype)


def chips_kernel(at_ref, every_ref, out_ref):
    total = every_ref[0].astype(F32)
    for k in range(1, 16):
        total = total + every_ref[k].astype(F32)
    total = total.astype(out_ref.dtype)
    for k in range(16):
        out_ref[k] = total


def chips_call(at, every, after=()):
    return call(chips_kernel, (struct(every.shape, every.dtype),), 1e6, 1e6, "experts_sum", after=after)(at, every)[0]


def keys_values(tokt, keep, wk, wv):
    kpre = mm(flip(wk).astype(BF), tokt)
    val = mm(flip(wv).astype(BF), tokt).astype(BF)
    low = jnp.exp(jnp.minimum(kpre, 0.0))
    km = (keep * jnp.where(kpre > 0, kpre + 1.0, low)).astype(BF)
    return km, val, keep * jnp.where(kpre > 0, 1.0, low)


def keys_kernel(at_ref, tok_ref, keep_ref, coords_ref, wk_ref, wv_ref, ck_ref, msg_ref, keep_m, send_m, km_buf):
    core = at_ref[0]
    tokt = flip(tok_ref[...]).astype(BF)
    keep = keep_ref[...].astype(F32)
    ck_ref[0:3, :] = coords_ref[...]
    ck_ref[3:4, :] = keep
    km, val, _ = keys_values(tokt, keep, wk_ref[...], wv_ref[...])
    km_buf[...] = km
    parts = pack_heads(mm_nt(val, km))
    ks = mm_nt(jnp.ones((8, N1), BF), km)
    for g in range(2):
        msg_ref[40 * g : 40 * g + 32, :] = parts[g]
        msg_ref[40 * g + 32 : 40 * g + 40, :] = ks[:, 128 * g : 128 * g + 128]
    for ref, half in ((keep_m, core), (send_m, 1 - core)):
        rows = pl.ds(pl.multiple_of(half * 128, 128), 128)
        ref[...] = mm_nt(tokt, km_buf[rows, :]).astype(BF)


def keys_call(at, tokens, keep_row, coords, wk, wv):
    return call(
        keys_kernel,
        (struct((4, N1), F32), struct((80, 128), F32), struct((D, 128), BF), struct((D, 128), BF)),
        4e8, 3e6, "keys", [pltpu.VMEM((D, N1), BF)], fetch=5,
    )(at, tokens, keep_row, coords, wk, wv)


def again_kernel(at_ref, tok_ref, keep_ref, wq_ref, wk_ref, wv_ref, tokt_ref, q_ref, qslope_ref, km_ref, v_ref, slope_ref):
    tokt = flip(tok_ref[...]).astype(BF)
    tokt_ref[...] = tokt
    pre = mm(flip(wq_ref[...]).astype(BF), tokt)
    low = jnp.exp(jnp.minimum(pre, 0.0))
    q_ref[...] = jnp.where(pre > 0, pre + 1.0, low).astype(BF)
    qslope_ref[...] = jnp.where(pre > 0, 1.0, low)
    km_ref[...], v_ref[...], slope_ref[...] = keys_values(tokt, keep_ref[...].astype(F32), wk_ref[...], wv_ref[...])


def again_call(at, tokens, keep_row, wq, wk, wv, after):
    return call(
        again_kernel,
        (
            struct((D, N1), BF), struct((D, N1), BF), struct((D, N1), F32),
            struct((D, N1), BF), struct((D, N1), BF), struct((D, N1), F32),
        ),
        5e8, 3e6, "queries_keys_again", after=after, fetch=5,
    )(at, tokens, keep_row, wq, wk, wv)


def query_kernel(at_ref, tok_ref, oth_ref, wq_ref, tokt_ref, q_ref):
    wqt = flip(wq_ref[...]).astype(BF)
    for half, ref in enumerate((tok_ref, oth_ref)):
        tokt = flip(ref[...]).astype(BF)
        cols = slice(N1 * half, N1 * half + N1)
        tokt_ref[:, cols] = tokt
        pre = mm(wqt, tokt)
        q_ref[:, cols] = jnp.where(pre > 0, pre + 1.0, jnp.exp(jnp.minimum(pre, 0.0))).astype(BF)


def query_call(at, tokens, tokens_o, wq):
    out = (struct((D, N2), BF), struct((D, N2), BF))
    return call(query_kernel, out, 4e8, 3e6, "queries")(at, tokens, tokens_o, wq)


def gate_kernel(at_ref, ck_ref, cko_ref, wgeo_ref, bgeo_ref, wroute_ref, r_ref, g_ref):
    geo = [column_of(wgeo_ref[k : k + 1, :]) for k in range(3)]
    bias = column_of(bgeo_ref[...])
    for half, ref in enumerate((ck_ref, cko_ref)):
        cols = slice(N1 * half, N1 * half + N1)
        pre = bias
        for k in range(3):
            pre = pre + geo[k] * ref[k : k + 1, :]
        r = jnp.tanh(pre)
        r_ref[:, cols] = r
        logit = lax.dot_general(
            wroute_ref[...], r, (((0,), (0,)), ((), ())), precision=lax.Precision.HIGHEST, preferred_element_type=F32
        )
        expo = jnp.exp(logit)
        g_ref[:, cols] = expo / jnp.sum(expo, axis=0, keepdims=True)


def gate_call(at, ck, ck_o, wgeo, bgeo, wroute):
    out = (struct((64, N2), F32), struct((8, N2), F32))
    return call(gate_kernel, out, 1e8, 1e6, "gate")(at, ck, ck_o, wgeo, bgeo, wroute)


def back_kernel(at_ref, cot_ref, oth_ref, ck_ref, cko_ref, win_ref, wout_ref, dyt_ref, back_ref, wint_ref):
    core = at_ref[0]
    for half, (ref, keep_ref) in enumerate(((cot_ref, ck_ref), (oth_ref, cko_ref))):
        cot = ref[...]
        keep = keep_ref[3:4, :]
        cols = slice(N1 * half, N1 * half + N1)
        dyt_ref[:, cols] = (flip(cot) * keep).astype(BF)
        for j in range(0, FH, HC):
            back_ref[j : j + HC, cols] = (mm_nt(wout_ref[core, j : j + HC, :], cot) * keep).astype(BF)
    wint_ref[...] = flip(win_ref[core]).astype(BF)


def back_call(at, cot, cot_o, ck, ck_o, w_in, w_out):
    out = (struct((D, N2), BF), struct((FH, N2), BF), struct((FH, D), BF))
    return call(back_kernel, out, 11e8, 8e6, "cotangent_back")(at, cot, cot_o, ck, ck_o, w_in, w_out)


GELU_A = 0.7978845608028654
GELU_B = 0.7978845608028654 * 0.044715


def expert_kernel(
    at_ref, msg_ref, m_ref, mo_ref, tokt_ref, q_ref, dyt_ref, back_ref, g_ref, r_ref, win_ref, wint_ref,
    own_ref, oth_ref, kvt_ref, ks_ref, keep_msg, send_msg, pieces_ref,
    gw1, gw2, dkv, dks, route,
):
    core, expert, y = at_ref[0], at_ref[1], at_ref[2]
    halves = msg_ref[0:40, :], msg_ref[40:80, :]
    kvt = heads_of(halves)
    ks = row_of(halves)
    kvt_ref[...] = kvt
    ks_ref[...] = ks
    kvh, kvl = split2(kvt)
    ksh, ksl = split2(jnp.where(head_mask(D, D), ks[0:1], 0.0))

    def step(i, first):
        cols = slice(TB * i, TB * i + TB)
        q = q_ref[:, cols]
        num = mm(kvh, q) + mm(kvl, q)
        rden = 1.0 / (mm(ksh, q) + mm(ksl, q))
        attn = num * rden
        mid = (tokt_ref[:, cols].astype(F32) + attn).astype(BF)
        gates = g_ref[:, cols]
        mine = lax.broadcasted_iota(jnp.int32, gates.shape, 0) == expert
        gate = jnp.sum(jnp.where(mine, gates, 0.0), axis=0, keepdims=True)
        dyt = dyt_ref[:, cols].astype(F32)
        df = (dyt * gate).astype(BF)
        dmid = jnp.zeros((D, TB), F32)
        if i < N1 // TB:
            dmid = dyt * jnp.where(y == 0, 1.0, 0.0)
        stat = jnp.zeros((1, TB), F32)
        for j in range(0, FH, HC):
            rows = slice(j, j + HC)
            u = mm(wint_ref[rows, :], mid)
            u2 = u * u
            t = jnp.tanh(u * (GELU_A + GELU_B * u2))
            half = 0.5 + 0.5 * t
            act = (u * half).astype(BF)
            slope = half + 0.5 * u * (1.0 - t * t) * (GELU_A + 3.0 * GELU_B * u2)
            back = back_ref[rows, cols].astype(F32)
            stat = stat + jnp.sum(act.astype(F32) * back, axis=0, keepdims=True)
            du = (back * gate * slope).astype(BF)
            dw2, dw1 = mm_nt(act, df), mm_nt(du, mid)
            gw2[rows, :] = dw2 if first else gw2[rows, :] + dw2
            gw1[rows, :] = dw1 if first else gw1[rows, :] + dw1
            dmid = dmid + mm(win_ref[core, :, rows], du)
        stat = stat * gate
        turn = (jnp.where(mine, 1.0, 0.0) - gates) * stat
        dnum = dmid * rden
        dden = -jnp.sum((dnum * attn).reshape(8, HD, TB), axis=1)
        hi, lo = split2(dnum)
        dkv_part = mm_nt(q, hi) + mm_nt(q, lo)
        hi, lo = split2(dden)
        dks_part = mm_nt(hi, q) + mm_nt(lo, q)
        route_part = lax.dot_general(
            turn, r_ref[:, cols], (((1,), (1,)), ((), ())), precision=lax.Precision.HIGHEST, preferred_element_type=F32
        )
        dkv[...] = dkv_part if first else dkv[...] + dkv_part
        dks[...] = dks_part if first else dks[...] + dks_part
        route[...] = route_part if first else route[...] + route_part
        if i < N1 // TB:
            own_ref[:, cols] = dmid
        else:
            oth_ref[:, TB * i - N1 : TB * i - N1 + TB] = dmid.astype(BF)

    for i in range(N2 // TB):
        step(i, i == 0)

    m = (m_ref[...].astype(F32) + mo_ref[...].astype(F32)).astype(BF)
    for k in range(16):
        rows = slice(64 * k, 64 * k + 64)
        pieces_ref[k, 0:64, :] = gw1[rows, :].astype(BF)
        pieces_ref[k, 64:128, :] = gw2[rows, :].astype(BF)
        pieces_ref[k, 128:144, 0:128] = m[16 * k : 16 * k + 16]
        pieces_ref[k, 128:144, 128:256] = jnp.zeros((16, 128), BF)
    parts = pack_heads(dkv[...])
    r = lax.broadcasted_iota(jnp.int32, (8, D), 0)
    c = lax.broadcasted_iota(jnp.int32, (8, D), 1) // HD
    sums = jnp.where(r == c, dks[...], 0.0)
    last = [jnp.concatenate([route[...], jnp.zeros((8, 64), F32)], axis=1), jnp.zeros((8, 128), F32)]
    halves = [jnp.concatenate([parts[g], sums[:, 128 * g : 128 * g + 128], last[g]], axis=0) for g in range(2)]
    keep_msg[...], send_msg[...] = ordered(core, *halves)


def expert_call(at, msg, m, m_o, tokt, q, dyt, back, g, r, w_in, wint):
    return call(
        expert_kernel,
        (
            struct((D, N1), F32), struct((D, N1), BF), struct((D, D), F32), struct((8, D), F32),
            struct((48, 128), F32), struct((48, 128), F32), struct((16, 144, D), BF),
        ),
        6e9, 12e6, "expert",
        [pltpu.VMEM((FH, D), F32)] * 2
        + [pltpu.VMEM((D, D), F32), pltpu.VMEM((8, D), F32), pltpu.VMEM((8, 64), F32)],
        limit=16,
    )(at, msg, m, m_o, tokt, q, dyt, back, g, r, w_in, wint)


def dmid_kernel(at_ref, own_ref, oth_ref, *out_refs):
    for d, ref in enumerate(out_refs):
        cols = pl.ds(pl.multiple_of(lax.rem(at_ref[2] + d, 4) * 256, 256), 256)
        ref[...] = (own_ref[:, cols] + oth_ref[:, cols].astype(F32)).astype(BF)


def dmid_call(at, own, oth):
    return call(dmid_kernel, (struct((D, 256), BF),) * 4, 1e6, 2e6, "dmid_pieces")(at, own, oth)


def back_query_kernel(
    at_ref, d0, d1, d2, d3, kvt_ref, ks_ref, tokt_ref, q_ref, qslope_ref, wq_ref, gx_ref, gq_ref, dmid_ref
):
    for d, ref in enumerate((d0, d1, d2, d3)):
        cols = pl.ds(pl.multiple_of(lax.rem(at_ref[2] + 4 - d, 4) * 256, 256), 256)
        dmid_ref[:, cols] = ref[...].astype(F32)
    dmid = dmid_ref[...]
    q = q_ref[...]
    tokt = tokt_ref[...]
    kvt = kvt_ref[...]
    kvth, kvtl = split2(kvt)
    kvh, kvl = split2(kvt.T)
    ks = ks_ref[0:1, :]
    mask = head_mask(D, D)
    ksh, ksl = split2(jnp.where(mask, ks, 0.0))
    kch, kcl = split2(jnp.where(mask, column_of(ks), 0.0))
    num = mm(kvth, q) + mm(kvtl, q)
    rden = 1.0 / (mm(ksh, q) + mm(ksl, q))
    attn = num * rden
    dnum = dmid * rden
    nh, nl = split2(dnum)
    zh, zl = split2(dnum * attn)
    dq = (mm(kvh, nh) - mm(kch, zh)) + (mm(kvl, nh) - mm(kcl, zh)) + (mm(kvh, nl) - mm(kch, zl))
    wq = wq_ref[...]
    dqp = (dq * qslope_ref[...]).astype(BF)
    gx_ref[...] = dmid + mm(wq, dqp)
    gq_ref[...] = mm_nt(tokt, dqp)


def back_query_call(at, dm, kvt, ks, tokt, q, qslope, wq):
    out = (struct((D, N1), F32), struct((D, D), F32))
    return call(back_query_kernel, out, 2e9, 5e6, "back_query", [pltpu.VMEM((D, N1), F32)])(
        at, *dm, kvt, ks, tokt, q, qslope, wq
    )


def back_keys_kernel(at_ref, msg_ref, msgo_ref, km_ref, v_ref, slope_ref, tokt_ref, gq_ref, dk_ref, dv_ref, keep_ref, send_ref):
    core = at_ref[0]
    halves = ordered(core, msg_ref[...], msgo_ref[...])
    dkv = heads_of(halves)
    dks = jnp.sum(row_of(halves), axis=0, keepdims=True)
    hi, lo = split2(dkv)
    v = v_ref[...]
    dk = mm(hi, v) + mm(lo, v) + column_of(dks)
    dk = (dk * slope_ref[...]).astype(BF)
    hi, lo = split2(dkv.T)
    km = km_ref[...]
    dk_ref[...] = dk
    dv_ref[...] = (mm(hi, km) + mm(lo, km)).astype(BF)
    for ref, part in ((keep_ref, core), (send_ref, 1 - core)):
        rows = pl.ds(pl.multiple_of(part * 128, 128), 128)
        ref[:, 0:D] = gq_ref[rows, :].astype(ref.dtype)
        ref[:, D : 2 * D] = mm_nt(tokt_ref[rows, 0:N1], dk).astype(ref.dtype)


def back_keys_call(at, msg, msg_o, km, v, slope, tokt, gq):
    out = (struct((D, N1), BF), struct((D, N1), BF), struct((128, 2 * D), F32), struct((128, 2 * D), BF))
    return call(back_keys_kernel, out, 1e9, 4e6, "back_keys")(at, msg, msg_o, km, v, slope, tokt, gq)


def grad_x_kernel(at_ref, gx_ref, dk_ref, dv_ref, wk_ref, wv_ref, out_ref):
    total = gx_ref[...] + mm(wk_ref[...], dk_ref[...]) + mm(wv_ref[...], dv_ref[...])
    out_ref[...] = total.T.astype(BF)


def grad_x_call(at, gx, dk, dv, wk, wv):
    return call(grad_x_kernel, (struct((N1, D), BF),), 3e8, 3e6, "grad_x")(at, gx, dk, dv, wk, wv)[0]


def place_kernel(at_ref, own_ref, oth_ref, gin_ref, gout_ref):
    def put(ref, part):
        cols = slice(128 * part, 128 * part + 128)
        gin_ref[0] = jnp.concatenate([ref[k, 0:64, cols].astype(F32) for k in range(16)], axis=0).T
        for k in range(8):
            gout_ref[0, 64 * k : 64 * k + 64, :] = ref[8 * part + k, 64:128, :].astype(F32)

    step = pl.program_id(0)
    for s in range(4):
        pl.when(step == s)(lambda s=s: put(own_ref if s < 2 else oth_ref, s % 2))


def place_call(at, own, oth):
    expert = lambda i, at: jnp.where(i < 2, at[0], 1 - at[0])
    out = pl.BlockSpec((1, 128, FH), lambda i, at: (expert(i, at), lax.rem(i, 2), 0))
    out2 = pl.BlockSpec((1, 512, D), lambda i, at: (expert(i, at), lax.rem(i, 2), 0))
    return pl.pallas_call(
        place_kernel,
        grid_spec=pltpu.PrefetchScalarGridSpec(
            num_scalar_prefetch=1,
            grid=(4,),
            in_specs=[pl.BlockSpec(memory_space=pltpu.VMEM)] * 2,
            out_specs=[out, out2],
        ),
        out_shape=(struct((2, D, FH), F32), struct((2, FH, D), F32)),
        compiler_params=pltpu.CompilerParams(vmem_limit_bytes=32 * 1024 * 1024),
        cost_estimate=pl.CostEstimate(flops=1000000, bytes_accessed=7000000, transcendentals=0),
        name="place_experts",
    )(at, own, oth)


def place_m_kernel(at_ref, msg_ref, msgo_ref, own_ref, oth_ref, gv_ref, route_ref):
    core, y = at_ref[0], at_ref[2]
    halves = ordered(core, msg_ref[...], msgo_ref[...])
    hi, lo = split2(heads_of(halves))
    own = jnp.concatenate([own_ref[k, 128:144, 0:128].astype(F32) for k in range(16)], axis=0)
    oth = jnp.concatenate([oth_ref[k, 128:144, 0:128].astype(F32) for k in range(16)], axis=0)
    m = jnp.concatenate(ordered(core, own, oth), axis=1).astype(BF)
    gv_ref[...] = mm(m, hi) + mm(m, lo)
    sums = halves[0][40:48, 0:64]
    at_row = lax.broadcasted_iota(jnp.int32, sums.shape, 0)
    cols = [column_of(jnp.sum(jnp.where(at_row == 2 * y + e, sums, 0.0), axis=0, keepdims=True)) for e in range(2)]
    route_ref[...] = jnp.concatenate(cols, axis=1)


def place_m_call(at, msg, msg_o, own, oth):
    out = (struct((D, D), F32), struct((64, 2), F32))
    return call(place_m_kernel, out, 1e8, 1e6, "grad_wv")(at, msg, msg_o, own, oth)


def place_proj_kernel(at_ref, own_ref, oth_ref, gq_ref, gk_ref):
    core = at_ref[0]
    for ref, part in ((own_ref, core), (oth_ref, 1 - core)):
        rows = pl.ds(pl.multiple_of(part * 128, 128), 128)
        gq_ref[rows, :] = ref[:, 0:D].astype(F32)
        gk_ref[rows, :] = ref[:, D : 2 * D].astype(F32)


def place_proj_call(at, own, oth):
    return call(place_proj_kernel, (struct((D, D), F32),) * 2, 1e6, 1e6, "place_projections")(at, own, oth)


def swap_core(v):
    return lax.ppermute(v, "pts", [(i, i ^ 1) for i in range(32)])


def to_x(v, d):
    return lax.ppermute(v, "pts", [(i, (i & ~6) | ((i + 2 * d) & 6)) for i in range(32)])


def to_z(v, d):
    return lax.ppermute(v, "pts", [(i, (i + 8 * d) % 32) for i in range(32)])


def to_y(v, d):
    return lax.ppermute(v, "exp", [(i, (i + d) % 4) for i in range(4)])


def star(v, to):
    return [to(v, d) for d in (1, 2, 3)]


CHIPS = [[2 * k + core for k in range(16)] for core in range(2)]


def exchange(v):
    return lax.all_to_all(v, "pts", 0, 0, axis_index_groups=CHIPS)


def on_device(
    tokens, coords, keep, cotangent, w_query, w_key, w_value, w_geo, b_geo, w_route, w_in, w_out
):
    pts = lax.axis_index("pts")
    y = lax.axis_index("exp")
    core = pts % 2
    at = jnp.stack([core, 2 * y + core, y]).astype(jnp.int32)

    tokens_o, cot_o = swap_core(tokens), swap_core(cotangent)
    ck, msg, m, m_away = keys_call(at, tokens, keep[None, :], coords, w_key, w_value)
    ck_o, m_o = swap_core(ck), swap_core(m_away)
    tokt, q = query_call(at, tokens, tokens_o, w_query)
    r, g = gate_call(at, ck, ck_o, w_geo, b_geo[None, :], w_route)
    dyt, back, wint = back_call(at, cotangent, cot_o, ck, ck_o, w_in, w_out)

    msg = add([msg, swap_core(msg)], (), F32)
    msg = add([msg] + star(msg, to_x), (q, g), F32)
    msg = add([msg] + star(msg, to_z), (back,), F32)
    own, oth, kvt, ks, msg2, msg2_away, pieces = expert_call(
        at, msg, m, m_o, tokt, q, dyt, back, g, r, w_in, wint
    )

    pieces = exchange(pieces)

    d0, d1, d2, d3 = dmid_call(at, own, swap_core(oth))
    dm = add([d0, to_y(d1, 1), to_y(d2, 2), to_y(d3, 3)])

    msg2 = add([msg2, swap_core(msg2_away)], (d0,), F32)
    msg2 = add([msg2] + star(msg2, to_y), (dm,), F32)
    dm = [dm] + star(dm, to_y)
    msg2 = msg2_z = add([msg2] + star(msg2, to_z), (), F32)

    pieces = chips_call(at, pieces, (msg2_z,))

    tokt, q, qslope, km, v, slope = again_call(at, tokens, keep[None, :], w_query, w_key, w_value, (pieces,))
    gx, gq = back_query_call(at, dm, kvt, ks, tokt, q, qslope, w_query)
    msg2 = add([msg2] + star(msg2, to_x), (gq,), F32)
    msg2_o = swap_core(msg2)
    dk, dv, part, away = back_keys_call(at, msg2, msg2_o, km, v, slope, tokt, gq)

    pieces = exchange(pieces)
    pieces_o = swap_core(pieces)
    grad_x = grad_x_call(at, gx, dk, dv, w_key, w_value)
    grad_w_in, grad_w_out = place_call(at, pieces, pieces_o)
    grad_wv, grad_route = place_m_call(at, msg2, msg2_o, pieces, pieces_o)

    part = add([part, swap_core(away)])
    part = add([part] + star(part, to_x), (grad_x,))
    part = add([part] + star(part, to_z), (grad_w_in, grad_wv))
    grad_wq, grad_wk = place_proj_call(at, part, swap_core(part))
    return (grad_x, grad_wq, grad_wk, grad_wv, grad_w_in, grad_w_out, grad_route)


def solution(mesh):
    in_specs = (
        P("pts", None),
        P(None, "pts"),
        P("pts"),
        P("pts", None),
        P(),
        P(),
        P(),
        P(),
        P(),
        P(),
        P("exp", None, None),
        P("exp", None, None),
    )
    out_specs = (
        P("pts", None),
        P(),
        P(),
        P(),
        P("exp", None, None),
        P("exp", None, None),
        P(None, "exp"),
    )
    return jax.shard_map(
        on_device, mesh=mesh, in_specs=in_specs, out_specs=out_specs, check_vma=False
    )
```

time: 191 us -> 133 us (0.70)
  waiting for transfers between devices: 71.6 us -> 23.9 us
  Pallas kernels: 60.9 us -> 40 us
  starting transfers between devices: 43.4 us -> 53.9 us
  local copies, waits for them, and re-layouts: 9.83 us -> 12.9 us
  other arithmetic: 2.78 us -> 0.39 us
    all_to_all x4 -> x2, waiting for transfers between devices: 25.1 us -> 0.17 us  [exchange(): return lax.all_to_all(v, 'pts', 0, 0, axis_index_groups=CHIPS)]
    ppermute x6 -> x9, waiting for transfers between devices: 25.7 us -> 4.11 us  [to_y(): return lax.ppermute(v, 'exp', [(i, (i + d) % 4) for i in range(4)])]
    pallas_call x11 -> x14, Pallas kernels: 60.9 us -> 40 us  [the longest x13 36.8 us: run(): pl.pallas_call(body, in_specs=[pl.BlockSpec(memory_space=pltpu.SMEM)] + [...]
    all_to_all x4 -> x2, starting transfers between devices: 19.1 us -> 8.97 us  [exchange(): return lax.all_to_all(v, 'pts', 0, 0, axis_index_groups=CHIPS)]
    ppermute x3 -> x9, starting transfers between devices: 3.67 us -> 11.4 us  [to_z(): return lax.ppermute(v, 'pts', [(i, (i + 8 * d) % 32) for i in range(32)])]
    ppermute x3 -> x9, starting transfers between devices: 3.68 us -> 9.69 us  [to_x(): lax.ppermute(v, 'pts', [(i, i & ~6 | i + 2 * d & 6) for i in range(32)])]
    ppermute x12 -> x11, starting transfers between devices: 9.25 us -> 15.1 us  [swap_core(): return lax.ppermute(v, 'pts', [(i, i ^ 1) for i in range(32)])]
    unnamed x40 -> x56, local copies, waits for them, and re-layouts: 7.22 us -> 12.9 us
  transfers between devices with their start and end apart: 28 -> 40, of which waited for: 18 -> 19; matrix products, arithmetic and copies ran while one was open for 3% -> 1% of each run, Pallas kernels for 17% -> 16%
where the time goes in v3:
time: 133 us; the launch traced here: 132 us
  starting transfers between devices  53.9 us (41%)
  Pallas kernels  40 us (30%)
  waiting for transfers between devices  23.9 us (18%)
  local copies, waits for them, and re-layouts  12.9 us (10%)
    pallas_call x13, Pallas kernels, run(): pl.pallas_call(body, in_specs=[pl.BlockSpec(memory_space=pltpu.SMEM)] + [...  36.8 us
    ppermute x11, starting transfers between devices, swap_core(): return lax.ppermute(v, 'pts', [(i, i ^ 1) for i in range(32)])  15.1 us
    unnamed x56, local copies, waits for them, and re-layouts  12.9 us
    ppermute x9, starting transfers between devices, to_z(): return lax.ppermute(v, 'pts', [(i, (i + 8 * d) % 32) for i in range(32)])  11.4 us
    ppermute x9, starting transfers between devices, to_x(): lax.ppermute(v, 'pts', [(i, i & ~6 | i + 2 * d & 6) for i in range(32)])  9.69 us
    all_to_all x2, starting transfers between devices, exchange(): return lax.all_to_all(v, 'pts', 0, 0, axis_index_groups=CHIPS)  8.97 us
    ppermute x9, starting transfers between devices, to_y(): return lax.ppermute(v, 'exp', [(i, (i + d) % 4) for i in range(4)])  8.78 us
    ppermute x9, waiting for transfers between devices, to_x(): lax.ppermute(v, 'pts', [(i, i & ~6 | i + 2 * d & 6) for i in range(32)])  7.89 us
  transfers between devices with their start and end apart: 40, of which 19 were waited for; matrix products, arithmetic and copies ran while one was open for 1% of the time, Pallas kernels for 16%

profile of v3, /device:TPU:1, one launch (start us, length us, event | category | flops | bytes accessed | tf_op | source)
XLA Modules:
  0.0 132.1 jit_solution(16337956058529929754)
XLA Ops:
  6.6 2.2 %keys.1 = (f32[4,1024]{1,0:T(4,128)S(1)}, f32[80,128]{1,0:T(8,128)S(1)}, bf16[256,128]{1,0:T(8,128)(2,1)S(1)}, bf16[256,128]{1,0:T(8,128)(2,1)S(1)}) custom-call(s32[3]{0:T(128)S(1)} %pad_add_fusion.refs_0_.at_ref, bf16[1024,256]{1,0:T(8,128)(2,1)S(1)} %copy-done, s32[1,1024]{1,0:T(1,128)S(1)} %bitcast.5, f32[3,1024]{1,0:T(4,128)S(1)} %copy-done.21, ...), custom_call_target="tpu_custom_call" | custom-call | flops 400000000 | bytes 3000000 | tf_op jit(solution)/shard_map/keys/pallas_call | solution.py:105
  10.2 2.6 %collective-permute-start.3 = (f32[80,128]{1,0:T(8,128)S(1)}, f32[80,128]{1,0:T(8,128)S(1)}, u32[]{:S(2)}, u32[]{:S(2)}) collective-permute-start(f32[80,128]{1,0:T(8,128)S(1)} %add.90), channel_id=1, source_target_pairs={{0,24},{4,28},{8,0},{12,4},{16,8},{20,12},{24,16},{28,20},{32,56},... | collective-permute-start | bytes 122888 | tf_op jit(solution)/shard_map/ppermute | solution.py:504
  16.2 1.9 %queries.1 = (bf16[256,2048]{1,0:T(8,128)(2,1)S(1)}, bf16[256,2048]{1,0:T(8,128)(2,1)S(1)}) custom-call(s32[3]{0:T(128)S(1)} %pad_add_fusion.refs_0_.at_ref, bf16[1024,256]{1,0:T(8,128)(2,1)S(1)} %copy-done.1, bf16[1024,256]{1,0:T(8,128)(2,1)} %collective-permute-done.4.refs_2_, bf16[256,256]{1,0:T(8,128)(2,1)S(1)} %copy-done.6), custom_call_target="tpu_custom_call" | custom-call | flops 400000000 | bytes 3000000 | tf_op jit(solution)/shard_map/queries/pallas_call | solution.py:105
  18.2 3.8 %collective-permute-start.8 = (f32[80,128]{1,0:T(8,128)S(1)}, f32[80,128]{1,0:T(8,128)S(1)}, u32[]{:S(2)}, u32[]{:S(2)}) collective-permute-start(f32[80,128]{1,0:T(8,128)S(1)} %add_add_fusion.1), channel_id=1, source_target_pairs={{0,96},{4,100},{8,104},{12,108},{16,112},{20,116},{24,120},{28,124... | collective-permute-start | bytes 122888 | tf_op jit(solution)/shard_map/ppermute | solution.py:508
  23.8 2.5 %cotangent_back.1 = (bf16[256,2048]{1,0:T(8,128)(2,1)S(1)}, bf16[1024,2048]{1,0:T(8,128)(2,1)S(1)}, bf16[1024,256]{1,0:T(8,128)(2,1)S(1)}) custom-call(s32[3]{0:T(128)S(1)} %pad_add_fusion.refs_0_.at_ref, bf16[1024,256]{1,0:T(8,128)(2,1)S(1)} %copy-done.14, bf16[1024,256]{1,0:T(8,128)(2,1)} %collective-permute-done.9.refs_2_, ...), custom_call_target="tpu_custom_call" | custom-call | flops 1100000000 | bytes 8000000 | tf_op jit(solution)/shard_map/cotangent_back/pallas_call | solution.py:105
  26.6 15.6 %expert.1 = (f32[256,1024]{1,0:T(8,128)S(1)}, bf16[256,1024]{1,0:T(8,128)(2,1)}, f32[256,256]{1,0:T(8,128)S(1)}, f32[8,256]{1,0:T(8,128)S(1)}, f32[48,128]{1,0:T...) custom-call(s32[3]{0:T(128)S(1)} %pad_add_fusion.refs_0_.at_ref, f32[80,128]{1,0:T(8,128)S(1)} %add_add_fusion.refs_1_, ...), custom_call_target="tpu_custom_call" | custom-call | flops 6000000000 | bytes 12000000 | tf_op jit(solution)/shard_map/expert/pallas_call | solution.py:105
  42.8 2.7 %collective-permute-start.11 = (bf16[256,1024]{1,0:T(8,128)(2,1)}, bf16[256,1024]{1,0:T(8,128)(2,1)S(1)}, u32[]{:S(2)}, u32[]{:S(2)}) collective-permute-start(bf16[256,1024]{1,0:T(8,128)(2,1)} %get-tuple-element.93), channel_id=1, source_target_pairs={{0,4},{4,0},{8,12},{12,8},{16,20},{20,16},{24,28},{28,24},{32,36},... | collective-permute-start | bytes 1572872 | tf_op jit(solution)/shard_map/ppermute | solution.py:500
  45.5 3.9 %all-to-all-start = ((bf16[16,144,256]{2,1,0:T(8,128)(2,1)}), bf16[16,144,256]{2,1,0:T(8,128)(2,1)S(1)}, u32[]{:S(2)}, u32[]{:S(2)}) async-start(bf16[16,144,256]{2,1,0:T(8,128)(2,1)} %get-tuple-element.100), calls=%async_computation | async-start | bytes 2359296 | tf_op jit(solution)/shard_map/all_to_all | solution.py:523
  51.5 2.6 %collective-permute-start.13 = (bf16[256,256]{1,0:T(8,128)(2,1)S(1)}, bf16[256,256]{1,0:T(8,128)(2,1)S(1)}, u32[]{:S(2)}, u32[]{:S(2)}) collective-permute-start(bf16[256,256]{1,0:T(8,128)(2,1)S(1)} %get-tuple-element.96), channel_id=1, source_target_pairs={{0,2},{1,3},{2,0},{3,1},{4,6},{5,7},{6,4},{7,5},{8,10},{9,11},{10,... | collective-permute-start | bytes 393224 | tf_op jit(solution)/shard_map/ppermute | solution.py:512
  57.2 2.2 %collective-permute-start.20 = (f32[48,128]{1,0:T(8,128)S(1)}, f32[48,128]{1,0:T(8,128)S(1)}, u32[]{:S(2)}, u32[]{:S(2)}) collective-permute-start(f32[48,128]{1,0:T(8,128)S(1)} %add.100), channel_id=1, source_target_pairs={{0,2},{1,3},{2,0},{3,1},{4,6},{5,7},{6,4},{7,5},{8,10},{9,11},{10,... | collective-permute-start | bytes 73736 | tf_op jit(solution)/shard_map/ppermute | solution.py:512
  61.7 1.8 %collective-permute-done.19 = f32[48,128]{1,0:T(8,128)S(1)} collective-permute-done((f32[48,128]{1,0:T(8,128)S(1)}, f32[48,128]{1,0:T(8,128)S(1)}, u32[]{:S(2)}, u32[]{:S(2)}) %collective-permute-start.19) | collective-permute-done | bytes 24608 | tf_op jit(solution)/shard_map/ppermute | solution.py:512
  63.5 2.9 %collective-permute-start.24 = (f32[48,128]{1,0:T(8,128)S(1)}, f32[48,128]{1,0:T(8,128)S(1)}, u32[]{:S(2)}, u32[]{:S(2)}) collective-permute-start(f32[48,128]{1,0:T(8,128)S(1)} %add_add_fusion.4), channel_id=1, source_target_pairs={{0,96},{4,100},{8,104},{12,108},{16,112},{20,116},{24,120},{28,124... | collective-permute-start | bytes 73736 | tf_op jit(solution)/shard_map/ppermute | solution.py:508
  67.6 3.1 %collective-permute-done.23 = f32[48,128]{1,0:T(8,128)S(1)} collective-permute-done((f32[48,128]{1,0:T(8,128)S(1)}, f32[48,128]{1,0:T(8,128)S(1)}, u32[]{:S(2)}, u32[]{:S(2)}) %collective-permute-start.23) | collective-permute-done | bytes 24608 | tf_op jit(solution)/shard_map/ppermute | solution.py:508
  72.7 5.0 %all-to-all-start.1 = ((bf16[16,144,256]{2,1,0:T(8,128)(2,1)}), bf16[16,144,256]{2,1,0:T(8,128)(2,1)S(1)}, u32[]{:S(2)}, u32[]{:S(2)}) async-start(bf16[16,144,256]{2,1,0:T(8,128)(2,1)} %experts_sum.1.refs_6_), calls=%async_computation.1 | async-start | bytes 2359296 | tf_op jit(solution)/shard_map/all_to_all | solution.py:523
  79.3 2.6 %collective-permute-start.27 = (f32[48,128]{1,0:T(8,128)S(1)}, f32[48,128]{1,0:T(8,128)S(1)}, u32[]{:S(2)}, u32[]{:S(2)}) collective-permute-start(f32[48,128]{1,0:T(8,128)S(1)} %add_add_fusion.3.refs_2_), channel_id=1, source_target_pairs={{0,24},{4,28},{8,0},{12,4},{16,8},{20,12},{24,16},{28,20},{32,56},... | collective-permute-start | bytes 73736 | tf_op jit(solution)/shard_map/ppermute | solution.py:504
  82.5 2.2 %queries_keys_again.1 = (bf16[256,1024]{1,0:T(8,128)(2,1)S(1)}, bf16[256,1024]{1,0:T(8,128)(2,1)S(1)}, f32[256,1024]{1,0:T(8,128)S(1)}, bf16[256,1024]{1,0:T(8,1...) custom-call(s32[3]{0:T(128)S(1)} %pad_add_fusion.refs_0_.at_ref, bf16[1024,256]{1,0:T(8,128)(2,1)S(1)} %copy-done.1, ...), custom_call_target="tpu_custom_call" | custom-call | flops 500000000 | bytes 3000000 | tf_op jit(solution)/shard_map/queries_keys_again/pallas_call | solution.py:105
  87.0 2.8 %back_query.1 = (f32[256,1024]{1,0:T(8,128)S(1)}, f32[256,256]{1,0:T(8,128)S(1)}) custom-call(s32[3]{0:T(128)S(1)} %pad_add_fusion.refs_0_.at_ref, bf16[256,256]{1,0:T(8,128)(2,1)S(1)} %add_convert_fusion.3.refs_1_, bf16[256,256]{1,0:T(8,128)(2,1)S(1)} %collective-permute-done.15.refs_2_, bf16[256,256]{1,0:T(8,128)(2,1)S(1)} %collective-permute-done.16.refs_3_, ...), custom_call_target="tpu_custom_call" | custom-call | flops 2000000000 | bytes 5000000 | tf_op jit(solution)/shard_map/back_query/pallas_call | solution.py:105
  92.7 5.7 %collective-permute-start.36 = (bf16[16,144,256]{2,1,0:T(8,128)(2,1)S(1)}, bf16[16,144,256]{2,1,0:T(8,128)(2,1)S(1)}, u32[]{:S(2)}, u32[]{:S(2)}) collective-permute-start(bf16[16,144,256]{2,1,0:T(8,128)(2,1)S(1)} %all-to-all-done.1.own_ref.refs_3_), channel_id=1, source_target_pairs={{0,4},{4,0},{8,12},{12,8},{16,20},{20,16},{24,28},{28,24},{32,36},... | collective-permute-start | bytes 3538952 | tf_op jit(solution)/shard_map/ppermute | solution.py:500
  98.8 2.1 %collective-permute-done.28.refs_2_ = f32[48,128]{1,0:T(8,128)S(1)} collective-permute-done((f32[48,128]{1,0:T(8,128)S(1)}, f32[48,128]{1,0:T(8,128)S(1)}, u32[]{:S(2)}, u32[]{:S(2)}) %collective-permute-start.28) | collective-permute-done | bytes 24608 | tf_op jit(solution)/shard_map/ppermute | solution.py:500
  108.4 2.2 %collective-permute-start.31 = (bf16[128,512]{1,0:T(8,128)(2,1)S(1)}, bf16[128,512]{1,0:T(8,128)(2,1)S(1)}, u32[]{:S(2)}, u32[]{:S(2)}) collective-permute-start(bf16[128,512]{1,0:T(8,128)(2,1)S(1)} %add_convert_fusion.2), channel_id=1, source_target_pairs={{0,16},{4,20},{8,24},{12,28},{16,0},{20,4},{24,8},{28,12},{32,48},... | collective-permute-start | bytes 393224 | tf_op jit(solution)/shard_map/ppermute | solution.py:504
  110.6 1.9 %grad_x.1 = bf16[1024,256]{1,0:T(8,128)(2,1)} custom-call(s32[3]{0:T(128)S(1)} %pad_add_fusion.refs_0_.at_ref, f32[256,1024]{1,0:T(8,128)S(1)} %get-tuple-element.112.refs_1_, bf16[256,1024]{1,0:T(8,128)(2,1)S(1)} %get-tuple-element.121.refs_2_, bf16[256,1024]{1,0:T(8,128)(2,1)S(1)} %get-tuple-element.122.refs_3_, bf16[256,256]{1,0:T(8,128)(2,1)S(1)} %copy-done.3, ...), custom_call_target="tpu_custom_call" | custom-call | flops 300000000 | bytes 3000000 | tf_op jit(solution)/shard_map/grad_x/pallas_call | solution.py:105
  114.7 3.0 %collective-permute-done.30 = bf16[128,512]{1,0:T(8,128)(2,1)S(1)} collective-permute-done((bf16[128,512]{1,0:T(8,128)(2,1)S(1)}, bf16[128,512]{1,0:T(8,128)(2,1)S(1)}, u32[]{:S(2)}, u32[]{:S(2)}) %collective-permute-start.30) | collective-permute-done | bytes 131104 | tf_op jit(solution)/shard_map/ppermute | solution.py:504
  120.5 3.2 %place_experts.1 = (f32[2,256,1024]{2,1,0:T(8,128)}, f32[2,1024,256]{2,1,0:T(8,128)}) custom-call(s32[3]{0:T(128)S(1)} %pad_add_fusion.refs_0_.at_ref, bf16[16,144,256]{2,1,0:T(8,128)(2,1)S(1)} %all-to-all-done.1.own_ref.refs_3_, bf16[16,144,256]{2,1,0:T(8,128)(2,1)S(1)} %collective-permute-done.36.oth_ref.refs_4_), custom_call_target="tpu_custom_call" | custom-call | flops 1000000 | bytes 7000000 | tf_op jit(solution)/shard_map/place_experts/pallas_call | solution.py:453
  125.2 3.1 %collective-permute-done.33 = bf16[128,512]{1,0:T(8,128)(2,1)S(1)} collective-permute-done((bf16[128,512]{1,0:T(8,128)(2,1)S(1)}, bf16[128,512]{1,0:T(8,128)(2,1)S(1)}, u32[]{:S(2)}, u32[]{:S(2)}) %collective-permute-start.33) | collective-permute-done | bytes 131104 | tf_op jit(solution)/shard_map/ppermute | solution.py:508
  (138 shorter events, 49.6 us)
Async XLA Ops:
  0.7 14.3 %collective-permute-start.4 = (bf16[1024,256]{1,0:T(8,128)(2,1)}, bf16[1024,256]{1,0:T(8,128)(2,1)}, u32[]{:S(2)}, u32[]{:S(2)}) collective-permute-start(bf16[1024,256]{1,0:T(8,128)(2,1)} %refs_1_.7), channel_id=1, source_target_pairs={{0,4},{4,0},{8,12},{12,8},{16,20},{20,16},{24,28},{28,24},{32,36},... | collective-permute-start | bytes 1572872 | tf_op jit(solution)/shard_map/ppermute | solution.py:500
  2.2 20.5 %collective-permute-start.9 = (bf16[1024,256]{1,0:T(8,128)(2,1)}, bf16[1024,256]{1,0:T(8,128)(2,1)}, u32[]{:S(2)}, u32[]{:S(2)}) collective-permute-start(bf16[1024,256]{1,0:T(8,128)(2,1)} %refs_1_.6), channel_id=1, source_target_pairs={{0,4},{4,0},{8,12},{12,8},{16,20},{20,16},{24,28},{28,24},{32,36},... | collective-permute-start | bytes 1572872 | tf_op jit(solution)/shard_map/ppermute | solution.py:500
  10.2 8.0 %collective-permute-start.3 = (f32[80,128]{1,0:T(8,128)S(1)}, f32[80,128]{1,0:T(8,128)S(1)}, u32[]{:S(2)}, u32[]{:S(2)}) collective-permute-start(f32[80,128]{1,0:T(8,128)S(1)} %add.90), channel_id=1, source_target_pairs={{0,24},{4,28},{8,0},{12,4},{16,8},{20,12},{24,16},{28,20},{32,56},... | collective-permute-start | bytes 122888 | tf_op jit(solution)/shard_map/ppermute | solution.py:504
  12.7 5.4 %collective-permute-start.2 = (f32[80,128]{1,0:T(8,128)S(1)}, f32[80,128]{1,0:T(8,128)S(1)}, u32[]{:S(2)}, u32[]{:S(2)}) collective-permute-start(f32[80,128]{1,0:T(8,128)S(1)} %add.90), channel_id=1, source_target_pairs={{0,16},{4,20},{8,24},{12,28},{16,0},{20,4},{24,8},{28,12},{32,48},... | collective-permute-start | bytes 122888 | tf_op jit(solution)/shard_map/ppermute | solution.py:504
  14.9 11.6 %collective-permute-start.10 = (bf16[256,128]{1,0:T(8,128)(2,1)S(1)}, bf16[256,128]{1,0:T(8,128)(2,1)S(1)}, u32[]{:S(2)}, u32[]{:S(2)}) collective-permute-start(bf16[256,128]{1,0:T(8,128)(2,1)S(1)} %get-tuple-element.87), channel_id=1, source_target_pairs={{0,4},{4,0},{8,12},{12,8},{16,20},{20,16},{24,28},{28,24},{32,36},... | collective-permute-start | bytes 196616 | tf_op jit(solution)/shard_map/ppermute | solution.py:500
  18.2 8.1 %collective-permute-start.8 = (f32[80,128]{1,0:T(8,128)S(1)}, f32[80,128]{1,0:T(8,128)S(1)}, u32[]{:S(2)}, u32[]{:S(2)}) collective-permute-start(f32[80,128]{1,0:T(8,128)S(1)} %add_add_fusion.1), channel_id=1, source_target_pairs={{0,96},{4,100},{8,104},{12,108},{16,112},{20,116},{24,120},{28,124... | collective-permute-start | bytes 122888 | tf_op jit(solution)/shard_map/ppermute | solution.py:508
  42.8 6.6 %collective-permute-start.11 = (bf16[256,1024]{1,0:T(8,128)(2,1)}, bf16[256,1024]{1,0:T(8,128)(2,1)S(1)}, u32[]{:S(2)}, u32[]{:S(2)}) collective-permute-start(bf16[256,1024]{1,0:T(8,128)(2,1)} %get-tuple-element.93), channel_id=1, source_target_pairs={{0,4},{4,0},{8,12},{12,8},{16,20},{20,16},{24,28},{28,24},{32,36},... | collective-permute-start | bytes 1572872 | tf_op jit(solution)/shard_map/ppermute | solution.py:500
  45.5 25.5 %all-to-all-start = ((bf16[16,144,256]{2,1,0:T(8,128)(2,1)}), bf16[16,144,256]{2,1,0:T(8,128)(2,1)S(1)}, u32[]{:S(2)}, u32[]{:S(2)}) async-start(bf16[16,144,256]{2,1,0:T(8,128)(2,1)} %get-tuple-element.100), calls=%async_computation | async-start | bytes 2359296 | tf_op jit(solution)/shard_map/all_to_all | solution.py:523
  50.1 9.2 %collective-permute-start.12 = (bf16[256,256]{1,0:T(8,128)(2,1)S(1)}, bf16[256,256]{1,0:T(8,128)(2,1)S(1)}, u32[]{:S(2)}, u32[]{:S(2)}) collective-permute-start(bf16[256,256]{1,0:T(8,128)(2,1)S(1)} %get-tuple-element.95), channel_id=1, source_target_pairs={{0,1},{1,2},{2,3},{3,0},{4,5},{5,6},{6,7},{7,4},{8,9},{9,10},{10,1... | collective-permute-start | bytes 393224 | tf_op jit(solution)/shard_map/ppermute | solution.py:512
  51.5 8.8 %collective-permute-start.13 = (bf16[256,256]{1,0:T(8,128)(2,1)S(1)}, bf16[256,256]{1,0:T(8,128)(2,1)S(1)}, u32[]{:S(2)}, u32[]{:S(2)}) collective-permute-start(bf16[256,256]{1,0:T(8,128)(2,1)S(1)} %get-tuple-element.96), channel_id=1, source_target_pairs={{0,2},{1,3},{2,0},{3,1},{4,6},{5,7},{6,4},{7,5},{8,10},{9,11},{10,... | collective-permute-start | bytes 393224 | tf_op jit(solution)/shard_map/ppermute | solution.py:512
  54.1 6.2 %collective-permute-start.14 = (bf16[256,256]{1,0:T(8,128)(2,1)S(1)}, bf16[256,256]{1,0:T(8,128)(2,1)S(1)}, u32[]{:S(2)}, u32[]{:S(2)}) collective-permute-start(bf16[256,256]{1,0:T(8,128)(2,1)S(1)} %get-tuple-element.97), channel_id=1, source_target_pairs={{0,3},{1,0},{2,1},{3,2},{4,7},{5,4},{6,5},{7,6},{8,11},{9,8},{10,9... | collective-permute-start | bytes 393224 | tf_op jit(solution)/shard_map/ppermute | solution.py:512
  72.7 20.0 %all-to-all-start.1 = ((bf16[16,144,256]{2,1,0:T(8,128)(2,1)}), bf16[16,144,256]{2,1,0:T(8,128)(2,1)S(1)}, u32[]{:S(2)}, u32[]{:S(2)}) async-start(bf16[16,144,256]{2,1,0:T(8,128)(2,1)} %experts_sum.1.refs_6_), calls=%async_computation.1 | async-start | bytes 2359296 | tf_op jit(solution)/shard_map/all_to_all | solution.py:523
  77.8 8.7 %collective-permute-start.17 = (bf16[256,256]{1,0:T(8,128)(2,1)S(1)}, bf16[256,256]{1,0:T(8,128)(2,1)S(1)}, u32[]{:S(2)}, u32[]{:S(2)}) collective-permute-start(bf16[256,256]{1,0:T(8,128)(2,1)S(1)} %add_convert_fusion.3.refs_1_), channel_id=1, source_target_pairs={{0,3},{1,0},{2,1},{3,2},{4,7},{5,4},{6,5},{7,6},{8,11},{9,8},{10,9... | collective-permute-start | bytes 393224 | tf_op jit(solution)/shard_map/ppermute | solution.py:512
  78.3 8.7 %collective-permute-start.16 = (bf16[256,256]{1,0:T(8,128)(2,1)S(1)}, bf16[256,256]{1,0:T(8,128)(2,1)S(1)}, u32[]{:S(2)}, u32[]{:S(2)}) collective-permute-start(bf16[256,256]{1,0:T(8,128)(2,1)S(1)} %add_convert_fusion.3.refs_1_), channel_id=1, source_target_pairs={{0,2},{1,3},{2,0},{3,1},{4,6},{5,7},{6,4},{7,5},{8,10},{9,11},{10,... | collective-permute-start | bytes 393224 | tf_op jit(solution)/shard_map/ppermute | solution.py:512
  79.3 7.8 %collective-permute-start.15 = (bf16[256,256]{1,0:T(8,128)(2,1)S(1)}, bf16[256,256]{1,0:T(8,128)(2,1)S(1)}, u32[]{:S(2)}, u32[]{:S(2)}) collective-permute-start(bf16[256,256]{1,0:T(8,128)(2,1)S(1)} %add_convert_fusion.3.refs_1_), channel_id=1, source_target_pairs={{0,1},{1,2},{2,3},{3,0},{4,5},{5,6},{6,7},{7,4},{8,9},{9,10},{10,1... | collective-permute-start | bytes 393224 | tf_op jit(solution)/shard_map/ppermute | solution.py:512
  79.3 10.5 %collective-permute-start.27 = (f32[48,128]{1,0:T(8,128)S(1)}, f32[48,128]{1,0:T(8,128)S(1)}, u32[]{:S(2)}, u32[]{:S(2)}) collective-permute-start(f32[48,128]{1,0:T(8,128)S(1)} %add_add_fusion.3.refs_2_), channel_id=1, source_target_pairs={{0,24},{4,28},{8,0},{12,4},{16,8},{20,12},{24,16},{28,20},{32,56},... | collective-permute-start | bytes 73736 | tf_op jit(solution)/shard_map/ppermute | solution.py:504
  81.9 9.4 %collective-permute-start.26 = (f32[48,128]{1,0:T(8,128)S(1)}, f32[48,128]{1,0:T(8,128)S(1)}, u32[]{:S(2)}, u32[]{:S(2)}) collective-permute-start(f32[48,128]{1,0:T(8,128)S(1)} %add_add_fusion.3.refs_2_), channel_id=1, source_target_pairs={{0,16},{4,20},{8,24},{12,28},{16,0},{20,4},{24,8},{28,12},{32,48},... | collective-permute-start | bytes 73736 | tf_op jit(solution)/shard_map/ppermute | solution.py:504
  86.5 6.1 %collective-permute-start.25 = (f32[48,128]{1,0:T(8,128)S(1)}, f32[48,128]{1,0:T(8,128)S(1)}, u32[]{:S(2)}, u32[]{:S(2)}) collective-permute-start(f32[48,128]{1,0:T(8,128)S(1)} %add_add_fusion.3.refs_2_), channel_id=1, source_target_pairs={{0,8},{4,12},{8,16},{12,20},{16,24},{20,28},{24,0},{28,4},{32,40},... | collective-permute-start | bytes 73736 | tf_op jit(solution)/shard_map/ppermute | solution.py:504
  92.7 27.8 %collective-permute-start.36 = (bf16[16,144,256]{2,1,0:T(8,128)(2,1)S(1)}, bf16[16,144,256]{2,1,0:T(8,128)(2,1)S(1)}, u32[]{:S(2)}, u32[]{:S(2)}) collective-permute-start(bf16[16,144,256]{2,1,0:T(8,128)(2,1)S(1)} %all-to-all-done.1.own_ref.refs_3_), channel_id=1, source_target_pairs={{0,4},{4,0},{8,12},{12,8},{16,20},{20,16},{24,28},{28,24},{32,36},... | collective-permute-start | bytes 3538952 | tf_op jit(solution)/shard_map/ppermute | solution.py:500
  108.4 6.3 %collective-permute-start.31 = (bf16[128,512]{1,0:T(8,128)(2,1)S(1)}, bf16[128,512]{1,0:T(8,128)(2,1)S(1)}, u32[]{:S(2)}, u32[]{:S(2)}) collective-permute-start(bf16[128,512]{1,0:T(8,128)(2,1)S(1)} %add_convert_fusion.2), channel_id=1, source_target_pairs={{0,16},{4,20},{8,24},{12,28},{16,0},{20,4},{24,8},{28,12},{32,48},... | collective-permute-start | bytes 393224 | tf_op jit(solution)/shard_map/ppermute | solution.py:504
  110.6 7.1 %collective-permute-start.30 = (bf16[128,512]{1,0:T(8,128)(2,1)S(1)}, bf16[128,512]{1,0:T(8,128)(2,1)S(1)}, u32[]{:S(2)}, u32[]{:S(2)}) collective-permute-start(bf16[128,512]{1,0:T(8,128)(2,1)S(1)} %add_convert_fusion.2), channel_id=1, source_target_pairs={{0,8},{4,12},{8,16},{12,20},{16,24},{20,28},{24,0},{28,4},{32,40},... | collective-permute-start | bytes 393224 | tf_op jit(solution)/shard_map/ppermute | solution.py:504
  117.8 7.4 %collective-permute-start.35 = (bf16[128,512]{1,0:T(8,128)(2,1)S(1)}, bf16[128,512]{1,0:T(8,128)(2,1)S(1)}, u32[]{:S(2)}, u32[]{:S(2)}) collective-permute-start(bf16[128,512]{1,0:T(8,128)(2,1)S(1)} %add_convert_fusion.1), channel_id=1, source_target_pairs={{0,96},{4,100},{8,104},{12,108},{16,112},{20,116},{24,120},{28,124... | collective-permute-start | bytes 393224 | tf_op jit(solution)/shard_map/ppermute | solution.py:508
  119.3 5.9 %collective-permute-start.34 = (bf16[128,512]{1,0:T(8,128)(2,1)S(1)}, bf16[128,512]{1,0:T(8,128)(2,1)S(1)}, u32[]{:S(2)}, u32[]{:S(2)}) collective-permute-start(bf16[128,512]{1,0:T(8,128)(2,1)S(1)} %add_convert_fusion.1), channel_id=1, source_target_pairs={{0,64},{4,68},{8,72},{12,76},{16,80},{20,84},{24,88},{28,92},{32,9... | collective-permute-start | bytes 393224 | tf_op jit(solution)/shard_map/ppermute | solution.py:508
  120.3 8.0 %collective-permute-start.33 = (bf16[128,512]{1,0:T(8,128)(2,1)S(1)}, bf16[128,512]{1,0:T(8,128)(2,1)S(1)}, u32[]{:S(2)}, u32[]{:S(2)}) collective-permute-start(bf16[128,512]{1,0:T(8,128)(2,1)S(1)} %add_convert_fusion.1), channel_id=1, source_target_pairs={{0,32},{4,36},{8,40},{12,44},{16,48},{20,52},{24,56},{28,60},{32,6... | collective-permute-start | bytes 393224 | tf_op jit(solution)/shard_map/ppermute | solution.py:508
  (43 other events, 204.6 us)

commit v4 on v3

--- a/solution.py
+++ b/solution.py
@@ -13,8 +13,9 @@
 FH = 1024
 N1 = 1024
 N2 = 2048
-TB = 512
-HC = 256
+TB = 1024
+HC = 1024
+LIMIT = 36
 F32 = jnp.float32
 BF = jnp.bfloat16
 
@@ -114,7 +115,7 @@
             compiler_params=pltpu.CompilerParams(vmem_limit_bytes=limit * 1024 * 1024),
             cost_estimate=pl.CostEstimate(flops=int(flops), bytes_accessed=int(nbytes), transcendentals=0),
             name=name,
-        )(at, *args, *after)
+        )(at, *[pltpu.with_memory_space_constraint(x, pltpu.HBM) for x in args[:fetch]], *args[fetch:], *after)
 
     return run
 
@@ -136,13 +137,12 @@
     total = every_ref[0].astype(F32)
     for k in range(1, 16):
         total = total + every_ref[k].astype(F32)
-    total = total.astype(out_ref.dtype)
-    for k in range(16):
-        out_ref[k] = total
+    out_ref[...] = total.astype(out_ref.dtype)
 
 
 def chips_call(at, every, after=()):
-    return call(chips_kernel, (struct(every.shape, every.dtype),), 1e6, 1e6, "experts_sum", after=after)(at, every)[0]
+    out = struct(every.shape[1:], every.dtype)
+    return call(chips_kernel, (out,), 1e6, 1e6, "experts_sum", after=after)(at, every)[0]
 
 
 def keys_values(tokt, keep, wk, wv):
@@ -237,21 +237,28 @@
     return call(gate_kernel, out, 1e8, 1e6, "gate")(at, ck, ck_o, wgeo, bgeo, wroute)
 
 
-def back_kernel(at_ref, cot_ref, oth_ref, ck_ref, cko_ref, win_ref, wout_ref, dyt_ref, back_ref, wint_ref):
+def own_gate(at_ref, gates):
+    mine = lax.broadcasted_iota(jnp.int32, gates.shape, 0) == at_ref[1]
+    return jnp.sum(jnp.where(mine, gates, 0.0), axis=0, keepdims=True), mine
+
+
+def back_kernel(at_ref, cot_ref, oth_ref, ck_ref, cko_ref, g_ref, win_ref, wout_ref, dy_ref, df_ref, back_ref, wint_ref):
     core = at_ref[0]
+    dy_ref[...] = (flip(cot_ref[...]) * ck_ref[3:4, :] * jnp.where(at_ref[2] == 0, 1.0, 0.0)).astype(BF)
     for half, (ref, keep_ref) in enumerate(((cot_ref, ck_ref), (oth_ref, cko_ref))):
         cot = ref[...]
         keep = keep_ref[3:4, :]
         cols = slice(N1 * half, N1 * half + N1)
-        dyt_ref[:, cols] = (flip(cot) * keep).astype(BF)
-        for j in range(0, FH, HC):
-            back_ref[j : j + HC, cols] = (mm_nt(wout_ref[core, j : j + HC, :], cot) * keep).astype(BF)
+        gate = keep * own_gate(at_ref, g_ref[:, cols])[0]
+        df_ref[:, cols] = (flip(cot) * gate).astype(BF)
+        for j in range(0, FH, 256):
+            back_ref[j : j + 256, cols] = (mm_nt(wout_ref[core, j : j + 256, :], cot) * gate).astype(BF)
     wint_ref[...] = flip(win_ref[core]).astype(BF)
 
 
-def back_call(at, cot, cot_o, ck, ck_o, w_in, w_out):
-    out = (struct((D, N2), BF), struct((FH, N2), BF), struct((FH, D), BF))
-    return call(back_kernel, out, 11e8, 8e6, "cotangent_back")(at, cot, cot_o, ck, ck_o, w_in, w_out)
+def back_call(at, cot, cot_o, ck, ck_o, g, w_in, w_out):
+    out = (struct((D, N1), BF), struct((D, N2), BF), struct((FH, N2), BF), struct((FH, D), BF))
+    return call(back_kernel, out, 11e8, 8e6, "cotangent_back")(at, cot, cot_o, ck, ck_o, g, w_in, w_out)
 
 
 GELU_A = 0.7978845608028654
@@ -259,11 +266,11 @@
 
 
 def expert_kernel(
-    at_ref, msg_ref, m_ref, mo_ref, tokt_ref, q_ref, dyt_ref, back_ref, g_ref, r_ref, win_ref, wint_ref,
+    at_ref, msg_ref, m_ref, mo_ref, tokt_ref, q_ref, dy_ref, df_ref, back_ref, g_ref, r_ref, win_ref, wint_ref,
     own_ref, oth_ref, kvt_ref, ks_ref, keep_msg, send_msg, pieces_ref,
-    gw1, gw2, dkv, dks, route,
+    gw1, gw2, dkv, route,
 ):
-    core, expert, y = at_ref[0], at_ref[1], at_ref[2]
+    core = at_ref[0]
     halves = msg_ref[0:40, :], msg_ref[40:80, :]
     kvt = heads_of(halves)
     ks = row_of(halves)
@@ -271,56 +278,52 @@
     ks_ref[...] = ks
     kvh, kvl = split2(kvt)
     ksh, ksl = split2(jnp.where(head_mask(D, D), ks[0:1], 0.0))
+    sums = jnp.concatenate([kvh, kvl, ksh, ksl], axis=0)
 
     def step(i, first):
         cols = slice(TB * i, TB * i + TB)
         q = q_ref[:, cols]
-        num = mm(kvh, q) + mm(kvl, q)
-        rden = 1.0 / (mm(ksh, q) + mm(ksl, q))
-        attn = num * rden
+        both = mm(sums, q)
+        rden = 1.0 / (both[2 * D : 3 * D] + both[3 * D :])
+        attn = (both[:D] + both[D : 2 * D]) * rden
         mid = (tokt_ref[:, cols].astype(F32) + attn).astype(BF)
-        gates = g_ref[:, cols]
-        mine = lax.broadcasted_iota(jnp.int32, gates.shape, 0) == expert
-        gate = jnp.sum(jnp.where(mine, gates, 0.0), axis=0, keepdims=True)
-        dyt = dyt_ref[:, cols].astype(F32)
-        df = (dyt * gate).astype(BF)
-        dmid = jnp.zeros((D, TB), F32)
-        if i < N1 // TB:
-            dmid = dyt * jnp.where(y == 0, 1.0, 0.0)
+        df = df_ref[:, cols]
+        dmid = dy_ref[:, cols].astype(F32) if TB * i < N1 else jnp.zeros((D, TB), F32)
         stat = jnp.zeros((1, TB), F32)
         for j in range(0, FH, HC):
             rows = slice(j, j + HC)
             u = mm(wint_ref[rows, :], mid)
             u2 = u * u
-            t = jnp.tanh(u * (GELU_A + GELU_B * u2))
-            half = 0.5 + 0.5 * t
-            act = (u * half).astype(BF)
-            slope = half + 0.5 * u * (1.0 - t * t) * (GELU_A + 3.0 * GELU_B * u2)
+            half = 0.5 + 0.5 * jnp.tanh(u * (GELU_A + GELU_B * u2))
+            act = u * half
+            slope = half + act * (1.0 - half) * (2.0 * GELU_A + 6.0 * GELU_B * u2)
             back = back_ref[rows, cols].astype(F32)
-            stat = stat + jnp.sum(act.astype(F32) * back, axis=0, keepdims=True)
-            du = (back * gate * slope).astype(BF)
+            stat = stat + jnp.sum(act * back, axis=0, keepdims=True)
+            act = act.astype(BF)
+            du = (back * slope).astype(BF)
             dw2, dw1 = mm_nt(act, df), mm_nt(du, mid)
             gw2[rows, :] = dw2 if first else gw2[rows, :] + dw2
             gw1[rows, :] = dw1 if first else gw1[rows, :] + dw1
             dmid = dmid + mm(win_ref[core, :, rows], du)
-        stat = stat * gate
+        gates = g_ref[:, cols]
+        mine = own_gate(at_ref, gates)[1]
         turn = (jnp.where(mine, 1.0, 0.0) - gates) * stat
         dnum = dmid * rden
         dden = -jnp.sum((dnum * attn).reshape(8, HD, TB), axis=1)
-        hi, lo = split2(dnum)
-        dkv_part = mm_nt(q, hi) + mm_nt(q, lo)
-        hi, lo = split2(dden)
-        dks_part = mm_nt(hi, q) + mm_nt(lo, q)
+        lhs = jnp.concatenate([*split2(dnum), *split2(jnp.concatenate([dden, dden], axis=0))], axis=0)
+        dkv_part = mm_nt(lhs, q)
         route_part = lax.dot_general(
             turn, r_ref[:, cols], (((1,), (1,)), ((), ())), precision=lax.Precision.HIGHEST, preferred_element_type=F32
         )
         dkv[...] = dkv_part if first else dkv[...] + dkv_part
-        dks[...] = dks_part if first else dks[...] + dks_part
         route[...] = route_part if first else route[...] + route_part
-        if i < N1 // TB:
-            own_ref[:, cols] = dmid
-        else:
-            oth_ref[:, TB * i - N1 : TB * i - N1 + TB] = dmid.astype(BF)
+        for k in range(TB // 512):
+            at_col = TB * i + 512 * k
+            piece = dmid[:, 512 * k : 512 * k + 512]
+            if at_col < N1:
+                own_ref[:, at_col : at_col + 512] = piece
+            else:
+                oth_ref[:, at_col - N1 : at_col - N1 + 512] = piece.astype(BF)
 
     for i in range(N2 // TB):
         step(i, i == 0)
@@ -332,16 +335,16 @@
         pieces_ref[k, 64:128, :] = gw2[rows, :].astype(BF)
         pieces_ref[k, 128:144, 0:128] = m[16 * k : 16 * k + 16]
         pieces_ref[k, 128:144, 128:256] = jnp.zeros((16, 128), BF)
-    parts = pack_heads(dkv[...])
+    parts = pack_heads(dkv[0:D, :] + dkv[D : 2 * D, :])
     r = lax.broadcasted_iota(jnp.int32, (8, D), 0)
     c = lax.broadcasted_iota(jnp.int32, (8, D), 1) // HD
-    sums = jnp.where(r == c, dks[...], 0.0)
+    sums = jnp.where(r == c, dkv[2 * D : 2 * D + 8, :] + dkv[2 * D + 16 : 2 * D + 24, :], 0.0)
     last = [jnp.concatenate([route[...], jnp.zeros((8, 64), F32)], axis=1), jnp.zeros((8, 128), F32)]
     halves = [jnp.concatenate([parts[g], sums[:, 128 * g : 128 * g + 128], last[g]], axis=0) for g in range(2)]
     keep_msg[...], send_msg[...] = ordered(core, *halves)
 
 
-def expert_call(at, msg, m, m_o, tokt, q, dyt, back, g, r, w_in, wint):
+def expert_call(at, msg, m, m_o, tokt, q, dy, df, back, g, r, w_in, wint):
     return call(
         expert_kernel,
         (
@@ -349,20 +352,22 @@
             struct((48, 128), F32), struct((48, 128), F32), struct((16, 144, D), BF),
         ),
         6e9, 12e6, "expert",
-        [pltpu.VMEM((FH, D), F32)] * 2
-        + [pltpu.VMEM((D, D), F32), pltpu.VMEM((8, D), F32), pltpu.VMEM((8, 64), F32)],
-        limit=16,
-    )(at, msg, m, m_o, tokt, q, dyt, back, g, r, w_in, wint)
-
-
-def dmid_kernel(at_ref, own_ref, oth_ref, *out_refs):
+        [pltpu.VMEM((FH, D), F32)] * 2 + [pltpu.VMEM((2 * D + 32, D), F32), pltpu.VMEM((8, 64), F32)],
+        limit=LIMIT,
+    )(at, msg, m, m_o, tokt, q, dy, df, back, g, r, w_in, wint)
+
+
+def dmid_kernel(at_ref, own_ref, oth_ref, msg_ref, msgo_ref, *out_refs):
+    hi, lo = split2(msg_ref[...] + msgo_ref[...])
     for d, ref in enumerate(out_refs):
         cols = pl.ds(pl.multiple_of(lax.rem(at_ref[2] + d, 4) * 256, 256), 256)
-        ref[...] = (own_ref[:, cols] + oth_ref[:, cols].astype(F32)).astype(BF)
-
-
-def dmid_call(at, own, oth):
-    return call(dmid_kernel, (struct((D, 256), BF),) * 4, 1e6, 2e6, "dmid_pieces")(at, own, oth)
+        ref[0:256, :] = (own_ref[:, cols] + oth_ref[:, cols].astype(F32)).astype(BF)
+        ref[256:304, 0:128] = hi
+        ref[256:304, 128:256] = lo
+
+
+def dmid_call(at, own, oth, msg, msg_o):
+    return call(dmid_kernel, (struct((304, 256), BF),) * 4, 1e6, 2e6, "dmid_pieces")(at, own, oth, msg, msg_o)
 
 
 def back_query_kernel(
@@ -404,13 +409,13 @@
 def back_keys_kernel(at_ref, msg_ref, msgo_ref, km_ref, v_ref, slope_ref, tokt_ref, gq_ref, dk_ref, dv_ref, keep_ref, send_ref):
     core = at_ref[0]
     halves = ordered(core, msg_ref[...], msgo_ref[...])
-    dkv = heads_of(halves)
+    dkvt = heads_of(halves)
     dks = jnp.sum(row_of(halves), axis=0, keepdims=True)
-    hi, lo = split2(dkv)
+    hi, lo = split2(dkvt.T)
     v = v_ref[...]
     dk = mm(hi, v) + mm(lo, v) + column_of(dks)
     dk = (dk * slope_ref[...]).astype(BF)
-    hi, lo = split2(dkv.T)
+    hi, lo = split2(dkvt)
     km = km_ref[...]
     dk_ref[...] = dk
     dv_ref[...] = (mm(hi, km) + mm(lo, km)).astype(BF)
@@ -434,44 +439,55 @@
     return call(grad_x_kernel, (struct((N1, D), BF),), 3e8, 3e6, "grad_x")(at, gx, dk, dv, wk, wv)[0]
 
 
-def place_kernel(at_ref, own_ref, oth_ref, gin_ref, gout_ref):
-    def put(ref, part):
-        cols = slice(128 * part, 128 * part + 128)
-        gin_ref[0] = jnp.concatenate([ref[k, 0:64, cols].astype(F32) for k in range(16)], axis=0).T
-        for k in range(8):
-            gout_ref[0, 64 * k : 64 * k + 64, :] = ref[8 * part + k, 64:128, :].astype(F32)
-
-    step = pl.program_id(0)
-    for s in range(4):
-        pl.when(step == s)(lambda s=s: put(own_ref if s < 2 else oth_ref, s % 2))
-
-
-def place_call(at, own, oth):
-    expert = lambda i, at: jnp.where(i < 2, at[0], 1 - at[0])
-    out = pl.BlockSpec((1, 128, FH), lambda i, at: (expert(i, at), lax.rem(i, 2), 0))
-    out2 = pl.BlockSpec((1, 512, D), lambda i, at: (expert(i, at), lax.rem(i, 2), 0))
+def origin(at_ref, dx, dz):
+    return lax.rem(at_ref[4] + 4 - dz, 4) * 4 + lax.rem(at_ref[3] + 4 - dx, 4)
+
+
+def place_kernel(at_ref, *refs):
+    ins, (gin_ref, gout_ref, buf) = refs[:8], refs[8:]
+
+    def put(side):
+        for dx in range(4):
+            for dz in range(4):
+                rows = pl.ds(pl.multiple_of(origin(at_ref, dx, dz) * 64, 64), 64)
+                buf[rows, :] = ins[4 * side + dx][dz, 0:64, :].astype(F32)
+                gout_ref[0, rows, :] = ins[4 * side + dx][dz, 64:128, :].astype(F32)
+        for j in range(0, FH, 256):
+            gin_ref[0, :, j : j + 256] = buf[j : j + 256, :].T
+
+    for side in range(2):
+        pl.when(pl.program_id(0) == side)(lambda side=side: put(side))
+
+
+def place_call(at, pieces):
+    expert = lambda i, at: (jnp.where(i == 0, at[0], 1 - at[0]), 0, 0)
     return pl.pallas_call(
         place_kernel,
         grid_spec=pltpu.PrefetchScalarGridSpec(
             num_scalar_prefetch=1,
-            grid=(4,),
-            in_specs=[pl.BlockSpec(memory_space=pltpu.VMEM)] * 2,
-            out_specs=[out, out2],
+            grid=(2,),
+            in_specs=[pl.BlockSpec(memory_space=pltpu.VMEM)] * 8,
+            out_specs=[pl.BlockSpec((1, D, FH), expert), pl.BlockSpec((1, FH, D), expert)],
+            scratch_shapes=[pltpu.VMEM((FH, D), F32)],
         ),
         out_shape=(struct((2, D, FH), F32), struct((2, FH, D), F32)),
-        compiler_params=pltpu.CompilerParams(vmem_limit_bytes=32 * 1024 * 1024),
+        compiler_params=pltpu.CompilerParams(vmem_limit_bytes=16 * 1024 * 1024),
         cost_estimate=pl.CostEstimate(flops=1000000, bytes_accessed=7000000, transcendentals=0),
         name="place_experts",
-    )(at, own, oth)
-
-
-def place_m_kernel(at_ref, msg_ref, msgo_ref, own_ref, oth_ref, gv_ref, route_ref):
+    )(at, *pieces)
+
+
+def place_m_kernel(at_ref, msg_ref, msgo_ref, *refs):
+    ins, (gv_ref, route_ref, buf) = refs[:8], refs[8:]
     core, y = at_ref[0], at_ref[2]
     halves = ordered(core, msg_ref[...], msgo_ref[...])
-    hi, lo = split2(heads_of(halves))
-    own = jnp.concatenate([own_ref[k, 128:144, 0:128].astype(F32) for k in range(16)], axis=0)
-    oth = jnp.concatenate([oth_ref[k, 128:144, 0:128].astype(F32) for k in range(16)], axis=0)
-    m = jnp.concatenate(ordered(core, own, oth), axis=1).astype(BF)
+    hi, lo = split2(heads_of(halves).T)
+    for side in range(2):
+        for dx in range(4):
+            for dz in range(4):
+                rows = pl.ds(pl.multiple_of(origin(at_ref, dx, dz) * 16, 16), 16)
+                buf[side, rows, :] = ins[4 * side + dx][dz, 128:144, 0:128]
+    m = jnp.concatenate(ordered(core, buf[0], buf[1]), axis=1)
     gv_ref[...] = mm(m, hi) + mm(m, lo)
     sums = halves[0][40:48, 0:64]
     at_row = lax.broadcasted_iota(jnp.int32, sums.shape, 0)
@@ -479,9 +495,9 @@
     route_ref[...] = jnp.concatenate(cols, axis=1)
 
 
-def place_m_call(at, msg, msg_o, own, oth):
+def place_m_call(at, msg, msg_o, pieces):
     out = (struct((D, D), F32), struct((64, 2), F32))
-    return call(place_m_kernel, out, 1e8, 1e6, "grad_wv")(at, msg, msg_o, own, oth)
+    return call(place_m_kernel, out, 1e8, 1e6, "grad_wv", [pltpu.VMEM((2, D, 128), BF)])(at, msg, msg_o, *pieces)
 
 
 def place_proj_kernel(at_ref, own_ref, oth_ref, gq_ref, gk_ref):
@@ -529,29 +545,28 @@
     pts = lax.axis_index("pts")
     y = lax.axis_index("exp")
     core = pts % 2
-    at = jnp.stack([core, 2 * y + core, y]).astype(jnp.int32)
+    at = jnp.stack([core, 2 * y + core, y, (pts // 2) % 4, pts // 8]).astype(jnp.int32)
 
     tokens_o, cot_o = swap_core(tokens), swap_core(cotangent)
     ck, msg, m, m_away = keys_call(at, tokens, keep[None, :], coords, w_key, w_value)
     ck_o, m_o = swap_core(ck), swap_core(m_away)
     tokt, q = query_call(at, tokens, tokens_o, w_query)
     r, g = gate_call(at, ck, ck_o, w_geo, b_geo[None, :], w_route)
-    dyt, back, wint = back_call(at, cotangent, cot_o, ck, ck_o, w_in, w_out)
+    dy, df, back, wint = back_call(at, cotangent, cot_o, ck, ck_o, g, w_in, w_out)
 
     msg = add([msg, swap_core(msg)], (), F32)
     msg = add([msg] + star(msg, to_x), (q, g), F32)
     msg = add([msg] + star(msg, to_z), (back,), F32)
     own, oth, kvt, ks, msg2, msg2_away, pieces = expert_call(
-        at, msg, m, m_o, tokt, q, dyt, back, g, r, w_in, wint
+        at, msg, m, m_o, tokt, q, dy, df, back, g, r, w_in, wint
     )
 
     pieces = exchange(pieces)
 
-    d0, d1, d2, d3 = dmid_call(at, own, swap_core(oth))
-    dm = add([d0, to_y(d1, 1), to_y(d2, 2), to_y(d3, 3)])
-
-    msg2 = add([msg2, swap_core(msg2_away)], (d0,), F32)
-    msg2 = add([msg2] + star(msg2, to_y), (dm,), F32)
+    p0, p1, p2, p3 = dmid_call(at, own, swap_core(oth), msg2, swap_core(msg2_away))
+    arrived = [p0, to_y(p1, 1), to_y(p2, 2), to_y(p3, 3)]
+    msg2 = add([p[256:, :128] for p in arrived] + [p[256:, 128:] for p in arrived], (), F32)
+    dm = add([p[:256] for p in arrived])
     dm = [dm] + star(dm, to_y)
     msg2 = msg2_z = add([msg2] + star(msg2, to_z), (), F32)
 
@@ -563,15 +578,16 @@
     msg2_o = swap_core(msg2)
     dk, dv, part, away = back_keys_call(at, msg2, msg2_o, km, v, slope, tokt, gq)
 
-    pieces = exchange(pieces)
-    pieces_o = swap_core(pieces)
+    pieces = jnp.stack([pieces] + star(pieces, to_z))
+    pieces = [pieces] + star(pieces, to_x)
+    pieces = pieces + [swap_core(piece) for piece in pieces]
     grad_x = grad_x_call(at, gx, dk, dv, w_key, w_value)
-    grad_w_in, grad_w_out = place_call(at, pieces, pieces_o)
-    grad_wv, grad_route = place_m_call(at, msg2, msg2_o, pieces, pieces_o)
+    grad_w_in, grad_w_out = place_call(at, pieces)
+    grad_wv, grad_route = place_m_call(at, msg2, msg2_o, pieces)
 
     part = add([part, swap_core(away)])
-    part = add([part] + star(part, to_x), (grad_x,))
-    part = add([part] + star(part, to_z), (grad_w_in, grad_wv))
+    part = add([part] + star(part, to_z), (grad_x,))
+    part = add([part] + star(part, to_x), (grad_w_in, grad_wv))
     grad_wq, grad_wk = place_proj_call(at, part, swap_core(part))
     return (grad_x, grad_wq, grad_wk, grad_wv, grad_w_in, grad_w_out, grad_route)
 

time: 133 us -> 119 us (0.89)
  local copies, waits for them, and re-layouts: 12.9 us -> 4.21 us
  Pallas kernels: 40 us -> 35.6 us
    unnamed x56 -> x32, local copies, waits for them, and re-layouts: 12.9 us -> 4.13 us
    all_to_all x2 -> x1, starting transfers between devices: 8.97 us -> 4.66 us  [exchange(): return lax.all_to_all(v, 'pts', 0, 0, axis_index_groups=CHIPS)]
    pallas_call x13, Pallas kernels: 36.8 us -> 32.5 us  [run(): pl.pallas_call(body, in_specs=[pl.BlockSpec(memory_space=pltpu.SMEM)] + [...]
    ppermute x11 -> x14, waiting for transfers between devices: 5.03 us -> 1.29 us  [swap_core(): return lax.ppermute(v, 'pts', [(i, i ^ 1) for i in range(32)])]
    ppermute x9 -> x12, waiting for transfers between devices: 6.74 us -> 9.73 us  [to_z(): return lax.ppermute(v, 'pts', [(i, (i + 8 * d) % 32) for i in range(32)])]
    ppermute x11 -> x14, starting transfers between devices: 15.1 us -> 17.2 us  [swap_core(): return lax.ppermute(v, 'pts', [(i, i ^ 1) for i in range(32)])]
    ppermute x9 -> x6, waiting for transfers between devices: 4.11 us -> 6.15 us  [to_y(): return lax.ppermute(v, 'exp', [(i, (i + d) % 4) for i in range(4)])]
    ppermute x9 -> x12, waiting for transfers between devices: 7.89 us -> 5.92 us  [to_x(): lax.ppermute(v, 'pts', [(i, i & ~6 | i + 2 * d & 6) for i in range(32)])]
  transfers between devices with their start and end apart: 40 -> 45, of which waited for: 19 -> 15; matrix products, arithmetic and copies ran while one was open for 1% -> 1% of each run, Pallas kernels for 16% -> 20%
where the time goes in v4:
time: 119 us
  starting transfers between devices  54.3 us (46%)
  Pallas kernels  35.6 us (30%)
  waiting for transfers between devices  23.1 us (19%)
  local copies, waits for them, and re-layouts  4.21 us (4%)
    pallas_call x13, Pallas kernels, run(): pl.pallas_call(body, in_specs=[pl.BlockSpec(memory_space=pltpu.SMEM)] + [...  32.5 us
    ppermute x14, starting transfers between devices, swap_core(): return lax.ppermute(v, 'pts', [(i, i ^ 1) for i in range(32)])  17.2 us
    ppermute x12, starting transfers between devices, to_z(): return lax.ppermute(v, 'pts', [(i, (i + 8 * d) % 32) for i in range(32)])  13.2 us
    ppermute x12, starting transfers between devices, to_x(): lax.ppermute(v, 'pts', [(i, i & ~6 | i + 2 * d & 6) for i in range(32)])  11.2 us
    ppermute x12, waiting for transfers between devices, to_z(): return lax.ppermute(v, 'pts', [(i, (i + 8 * d) % 32) for i in range(32)])  9.73 us
    ppermute x6, starting transfers between devices, to_y(): return lax.ppermute(v, 'exp', [(i, (i + d) % 4) for i in range(4)])  8 us
    ppermute x6, waiting for transfers between devices, to_y(): return lax.ppermute(v, 'exp', [(i, (i + d) % 4) for i in range(4)])  6.15 us
    ppermute x12, waiting for transfers between devices, to_x(): lax.ppermute(v, 'pts', [(i, i & ~6 | i + 2 * d & 6) for i in range(32)])  5.92 us
  transfers between devices with their start and end apart: 45, of which 15 were waited for; matrix products, arithmetic and copies ran while one was open for 1% of the time, Pallas kernels for 20%

profile of v4, /device:TPU:1, one launch (start us, length us, event | category | flops | bytes accessed | tf_op | source)
XLA Modules:
  0.0 118.6 jit_solution(14072134655464515792)
XLA Ops:
  2.4 2.9 %keys.1 = (f32[4,1024]{1,0:T(4,128)S(1)}, f32[80,128]{1,0:T(8,128)S(1)}, bf16[256,128]{1,0:T(8,128)(2,1)S(1)}, bf16[256,128]{1,0:T(8,128)(2,1)S(1)}) custom-call(s32[5]{0:T(128)S(1)} %stack.38.refs_0_.at_ref, bf16[1024,256]{1,0:T(8,128)(2,1)} %refs_1_.7, s32[1,1024]{1,0:T(1,128)} %bitcast.16, f32[3,1024]{1,0:T(4,128)} %refs_3_.4, bf16[256,256]{1,0:T(8,128)(2,1)} %refs_4_.5, ...), custom_call_target="tpu_custom_call" | custom-call | flops 400000000 | bytes 3000000 | tf_op jit(solution)/shard_map/keys/pallas_call | solution.py:106
  7.2 2.6 %collective-permute-start.3 = (f32[80,128]{1,0:T(8,128)S(1)}, f32[80,128]{1,0:T(8,128)S(1)}, u32[]{:S(2)}, u32[]{:S(2)}) collective-permute-start(f32[80,128]{1,0:T(8,128)S(1)} %add.105), channel_id=1, source_target_pairs={{0,24},{4,28},{8,0},{12,4},{16,8},{20,12},{24,16},{28,20},{32,56},... | collective-permute-start | bytes 122888 | tf_op jit(solution)/shard_map/ppermute | solution.py:520
  14.7 1.9 %queries.1 = (bf16[256,2048]{1,0:T(8,128)(2,1)S(1)}, bf16[256,2048]{1,0:T(8,128)(2,1)S(1)}) custom-call(s32[5]{0:T(128)S(1)} %stack.38.refs_0_.at_ref, bf16[1024,256]{1,0:T(8,128)(2,1)S(1)} %copy-done.6, bf16[1024,256]{1,0:T(8,128)(2,1)} %collective-permute-done.4.refs_2_, bf16[256,256]{1,0:T(8,128)(2,1)S(1)} %copy-done.7), custom_call_target="tpu_custom_call" | custom-call | flops 400000000 | bytes 3000000 | tf_op jit(solution)/shard_map/queries/pallas_call | solution.py:106
  16.7 3.8 %collective-permute-start.8 = (f32[80,128]{1,0:T(8,128)S(1)}, f32[80,128]{1,0:T(8,128)S(1)}, u32[]{:S(2)}, u32[]{:S(2)}) collective-permute-start(f32[80,128]{1,0:T(8,128)S(1)} %add_add_fusion.1), channel_id=1, source_target_pairs={{0,96},{4,100},{8,104},{12,108},{16,112},{20,116},{24,120},{28,124... | collective-permute-start | bytes 122888 | tf_op jit(solution)/shard_map/ppermute | solution.py:524
  21.3 2.7 %cotangent_back.1 = (bf16[256,1024]{1,0:T(8,128)(2,1)S(1)}, bf16[256,2048]{1,0:T(8,128)(2,1)S(1)}, bf16[1024,2048]{1,0:T(8,128)(2,1)S(1)}, bf16[1024,256]{1,0:T(8,128)(2,1)S(1)}) custom-call(s32[5]{0:T(128)S(1)} %stack.38.refs_0_.at_ref, bf16[1024,256]{1,0:T(8,128)(2,1)S(1)} %copy-done.5, bf16[1024,256]{1,0:T(8,128)(2,1)} %collective-permute-done.9.refs_2_, ...), custom_call_target="tpu_custom_call" | custom-call | flops 1100000000 | bytes 8000000 | tf_op jit(solution)/shard_map/cotangent_back/pallas_call | solution.py:106
  25.5 10.6 %expert.1 = (f32[256,1024]{1,0:T(8,128)S(1)}, bf16[256,1024]{1,0:T(8,128)(2,1)S(1)}, f32[256,256]{1,0:T(8,128)S(1)}, f32[8,256]{1,0:T(8,128)S(1)}, f32[48,128]{1...) custom-call(s32[5]{0:T(128)S(1)} %stack.38.refs_0_.at_ref, f32[80,128]{1,0:T(8,128)S(1)} %add_add_fusion.refs_1_, ...), custom_call_target="tpu_custom_call" | custom-call | flops 6000000000 | bytes 12000000 | tf_op jit(solution)/shard_map/expert/pallas_call | solution.py:106
  38.0 4.7 %all-to-all-start = ((bf16[16,144,256]{2,1,0:T(8,128)(2,1)}), bf16[16,144,256]{2,1,0:T(8,128)(2,1)S(1)}, u32[]{:S(2)}, u32[]{:S(2)}) async-start(bf16[16,144,256]{2,1,0:T(8,128)(2,1)} %get-tuple-element.98), calls=%async_computation | async-start | bytes 2359296 | tf_op jit(solution)/shard_map/all_to_all | solution.py:539
  46.0 2.6 %collective-permute-start.14 = (bf16[304,256]{1,0:T(8,128)(2,1)S(1)}, bf16[304,256]{1,0:T(8,128)(2,1)S(1)}, u32[]{:S(2)}, u32[]{:S(2)}) collective-permute-start(bf16[304,256]{1,0:T(8,128)(2,1)S(1)} %get-tuple-element.94), channel_id=1, source_target_pairs={{0,2},{1,3},{2,0},{3,1},{4,6},{5,7},{6,4},{7,5},{8,10},{9,11},{10,... | collective-permute-start | bytes 466952 | tf_op jit(solution)/shard_map/ppermute | solution.py:528
  51.4 4.4 %collective-permute-done.14 = bf16[304,256]{1,0:T(8,128)(2,1)S(1)} collective-permute-done((bf16[304,256]{1,0:T(8,128)(2,1)S(1)}, bf16[304,256]{1,0:T(8,128)(2,1)S(1)}, u32[]{:S(2)}, u32[]{:S(2)}) %collective-permute-start.14) | collective-permute-done | bytes 155680 | tf_op jit(solution)/shard_map/ppermute | solution.py:528
  55.9 2.7 %collective-permute-start.21 = (f32[48,128]{1,0:T(8,128)S(1)}, f32[48,128]{1,0:T(8,128)S(1)}, u32[]{:S(2)}, u32[]{:S(2)}) collective-permute-start(f32[48,128]{1,0:T(8,128)S(1)} %convert_add_fusion), channel_id=1, source_target_pairs={{0,96},{4,100},{8,104},{12,108},{16,112},{20,116},{24,120},{28,124... | collective-permute-start | bytes 73736 | tf_op jit(solution)/shard_map/ppermute | solution.py:524
  59.8 2.3 %collective-permute-start.18 = (bf16[256,256]{1,0:T(8,128)(2,1)S(1)}, bf16[256,256]{1,0:T(8,128)(2,1)S(1)}, u32[]{:S(2)}, u32[]{:S(2)}) collective-permute-start(bf16[256,256]{1,0:T(8,128)(2,1)S(1)} %add_convert_fusion.3.refs_1_), channel_id=1, source_target_pairs={{0,3},{1,0},{2,1},{3,2},{4,7},{5,4},{6,5},{7,6},{8,11},{9,8},{10,9... | collective-permute-start | bytes 393224 | tf_op jit(solution)/shard_map/ppermute | solution.py:528
  63.5 2.0 %collective-permute-start.24 = (f32[48,128]{1,0:T(8,128)S(1)}, f32[48,128]{1,0:T(8,128)S(1)}, u32[]{:S(2)}, u32[]{:S(2)}) collective-permute-start(f32[48,128]{1,0:T(8,128)S(1)} %add_add_fusion.3.refs_2_), channel_id=1, source_target_pairs={{0,24},{4,28},{8,0},{12,4},{16,8},{20,12},{24,16},{28,20},{32,56},... | collective-permute-start | bytes 73736 | tf_op jit(solution)/shard_map/ppermute | solution.py:520
  66.8 2.8 %queries_keys_again.1 = (bf16[256,1024]{1,0:T(8,128)(2,1)S(1)}, bf16[256,1024]{1,0:T(8,128)(2,1)S(1)}, f32[256,1024]{1,0:T(8,128)S(1)}, bf16[256,1024]{1,0:T(8,1...) custom-call(s32[5]{0:T(128)S(1)} %stack.38.refs_0_.at_ref, bf16[1024,256]{1,0:T(8,128)(2,1)} %refs_1_.7, ...), custom_call_target="tpu_custom_call" | custom-call | flops 500000000 | bytes 3000000 | tf_op jit(solution)/shard_map/queries_keys_again/pallas_call | solution.py:106
  70.3 2.8 %back_query.1 = (f32[256,1024]{1,0:T(8,128)S(1)}, f32[256,256]{1,0:T(8,128)S(1)}) custom-call(s32[5]{0:T(128)S(1)} %stack.38.refs_0_.at_ref, bf16[256,256]{1,0:T(8,128)(2,1)S(1)} %add_convert_fusion.3.refs_1_, bf16[256,256]{1,0:T(8,128)(2,1)S(1)} %collective-permute-done.16.refs_2_, bf16[256,256]{1,0:T(8,128)(2,1)S(1)} %collective-permute-done.17.refs_3_, ...), custom_call_target="tpu_custom_call" | custom-call | flops 2000000000 | bytes 5000000 | tf_op jit(solution)/shard_map/back_query/pallas_call | solution.py:106
  73.8 4.5 %collective-permute-start.25 = (f32[48,128]{1,0:T(8,128)S(1)}, f32[48,128]{1,0:T(8,128)S(1)}, u32[]{:S(2)}, u32[]{:S(2)}) collective-permute-start(f32[48,128]{1,0:T(8,128)S(1)} %add_add_fusion.2.refs_1_), channel_id=1, source_target_pairs={{0,4},{4,0},{8,12},{12,8},{16,20},{20,16},{24,28},{28,24},{32,36},... | collective-permute-start | bytes 73736 | tf_op jit(solution)/shard_map/ppermute | solution.py:516
  78.3 2.1 %collective-permute-start.35 = (bf16[144,256]{1,0:T(8,128)(2,1)S(1)}, bf16[144,256]{1,0:T(8,128)(2,1)S(1)}, u32[]{:S(2)}, u32[]{:S(2)}) collective-permute-start(bf16[144,256]{1,0:T(8,128)(2,1)S(1)} %experts_sum.1.refs_6_), channel_id=1, source_target_pairs={{0,96},{4,100},{8,104},{12,108},{16,112},{20,116},{24,120},{28,124... | collective-permute-start | bytes 221192 | tf_op jit(solution)/shard_map/ppermute | solution.py:524
  85.1 2.2 %collective-permute-done.33 = bf16[144,256]{1,0:T(8,128)(2,1)S(1)} collective-permute-done((bf16[144,256]{1,0:T(8,128)(2,1)S(1)}, bf16[144,256]{1,0:T(8,128)(2,1)S(1)}, u32[]{:S(2)}, u32[]{:S(2)}) %collective-permute-start.33) | collective-permute-done | bytes 73760 | tf_op jit(solution)/shard_map/ppermute | solution.py:524
  91.0 2.6 %collective-permute-done.29 = bf16[128,512]{1,0:T(8,128)(2,1)S(1)} collective-permute-done((bf16[128,512]{1,0:T(8,128)(2,1)S(1)}, bf16[128,512]{1,0:T(8,128)(2,1)S(1)}, u32[]{:S(2)}, u32[]{:S(2)}) %collective-permute-start.29) | collective-permute-done | bytes 131104 | tf_op jit(solution)/shard_map/ppermute | solution.py:524
  95.2 3.7 %collective-permute-start.39 = (bf16[4,144,256]{2,1,0:T(8,128)(2,1)S(1)}, bf16[4,144,256]{2,1,0:T(8,128)(2,1)S(1)}, u32[]{:S(2)}, u32[]{:S(2)}) collective-permute-start(bf16[4,144,256]{2,1,0:T(8,128)(2,1)S(1)} %pad_maximum_fusion.refs_0_.refs_3_), channel_id=1, source_target_pairs={{0,4},{4,0},{8,12},{12,8},{16,20},{20,16},{24,28},{28,24},{32,36},... | collective-permute-start | bytes 884744 | tf_op jit(solution)/shard_map/ppermute | solution.py:516
  99.0 1.9 %grad_x.1 = bf16[1024,256]{1,0:T(8,128)(2,1)} custom-call(s32[5]{0:T(128)S(1)} %stack.38.refs_0_.at_ref, f32[256,1024]{1,0:T(8,128)S(1)} %get-tuple-element.102.refs_1_, bf16[256,1024]{1,0:T(8,128)(2,1)S(1)} %get-tuple-element.111.refs_2_, bf16[256,1024]{1,0:T(8,128)(2,1)S(1)} %get-tuple-element.112.refs_3_, bf16[256,256]{1,0:T(8,128)(2,1)S(1)} %copy-done, ...), custom_call_target="tpu_custom_call" | custom-call | flops 300000000 | bytes 3000000 | tf_op jit(solution)/shard_map/grad_x/pallas_call | solution.py:106
  100.8 2.2 %collective-permute-start.41 = (bf16[4,144,256]{2,1,0:T(8,128)(2,1)S(1)}, bf16[4,144,256]{2,1,0:T(8,128)(2,1)S(1)}, u32[]{:S(2)}, u32[]{:S(2)}) collective-permute-start(bf16[4,144,256]{2,1,0:T(8,128)(2,1)S(1)} %collective-permute-done.37.refs_2_.refs_5_), channel_id=1, source_target_pairs={{0,4},{4,0},{8,12},{12,8},{16,20},{20,16},{24,28},{28,24},{32,36},... | collective-permute-start | bytes 884744 | tf_op jit(solution)/shard_map/ppermute | solution.py:516
  103.0 1.9 %collective-permute-done.36.refs_1_.refs_4_ = bf16[4,144,256]{2,1,0:T(8,128)(2,1)S(1)} collective-permute-done((bf16[4,144,256]{2,1,0:T(8,128)(2,1)S(1)}, bf16[4,144,256]{2,1,0:T(8,128)(2,1)S(1)}, u32[]{:S(2)}, u32[]{:S(2)}) %collective-permute-start.36) | collective-permute-done | bytes 294944 | tf_op jit(solution)/shard_map/ppermute | solution.py:520
  107.6 3.1 %place_experts.1 = (f32[2,256,1024]{2,1,0:T(8,128)}, f32[2,1024,256]{2,1,0:T(8,128)}) custom-call(s32[5]{0:T(128)S(1)} %stack.38.refs_0_.at_ref, bf16[4,144,256]{2,1,0:T(8,128)(2,1)S(1)} %pad_maximum_fusion.refs_0_.refs_3_, bf16[4,144,256]{2,1,0:T(8,128)(2,1)S(1)} %collective-permute-done.36.refs_1_.refs_4_, ...), custom_call_target="tpu_custom_call" | custom-call | flops 1000000 | bytes 7000000 | tf_op jit(solution)/shard_map/place_experts/pallas_call | solution.py:464
  112.2 3.3 %collective-permute-done.30 = bf16[128,512]{1,0:T(8,128)(2,1)S(1)} collective-permute-done((bf16[128,512]{1,0:T(8,128)(2,1)S(1)}, bf16[128,512]{1,0:T(8,128)(2,1)S(1)}, u32[]{:S(2)}, u32[]{:S(2)}) %collective-permute-start.30) | collective-permute-done | bytes 131104 | tf_op jit(solution)/shard_map/ppermute | solution.py:520
  (124 shorter events, 41.3 us)
Async XLA Ops:
  0.7 12.7 %collective-permute-start.4 = (bf16[1024,256]{1,0:T(8,128)(2,1)}, bf16[1024,256]{1,0:T(8,128)(2,1)}, u32[]{:S(2)}, u32[]{:S(2)}) collective-permute-start(bf16[1024,256]{1,0:T(8,128)(2,1)} %refs_1_.7), channel_id=1, source_target_pairs={{0,4},{4,0},{8,12},{12,8},{16,20},{20,16},{24,28},{28,24},{32,36},... | collective-permute-start | bytes 1572872 | tf_op jit(solution)/shard_map/ppermute | solution.py:516
  2.2 19.0 %collective-permute-start.9 = (bf16[1024,256]{1,0:T(8,128)(2,1)}, bf16[1024,256]{1,0:T(8,128)(2,1)}, u32[]{:S(2)}, u32[]{:S(2)}) collective-permute-start(bf16[1024,256]{1,0:T(8,128)(2,1)} %refs_1_.6), channel_id=1, source_target_pairs={{0,4},{4,0},{8,12},{12,8},{16,20},{20,16},{24,28},{28,24},{32,36},... | collective-permute-start | bytes 1572872 | tf_op jit(solution)/shard_map/ppermute | solution.py:516
  7.2 9.4 %collective-permute-start.3 = (f32[80,128]{1,0:T(8,128)S(1)}, f32[80,128]{1,0:T(8,128)S(1)}, u32[]{:S(2)}, u32[]{:S(2)}) collective-permute-start(f32[80,128]{1,0:T(8,128)S(1)} %add.105), channel_id=1, source_target_pairs={{0,24},{4,28},{8,0},{12,4},{16,8},{20,12},{24,16},{28,20},{32,56},... | collective-permute-start | bytes 122888 | tf_op jit(solution)/shard_map/ppermute | solution.py:520
  9.8 6.8 %collective-permute-start.2 = (f32[80,128]{1,0:T(8,128)S(1)}, f32[80,128]{1,0:T(8,128)S(1)}, u32[]{:S(2)}, u32[]{:S(2)}) collective-permute-start(f32[80,128]{1,0:T(8,128)S(1)} %add.105), channel_id=1, source_target_pairs={{0,16},{4,20},{8,24},{12,28},{16,0},{20,4},{24,8},{28,12},{32,48},... | collective-permute-start | bytes 122888 | tf_op jit(solution)/shard_map/ppermute | solution.py:520
  13.4 12.1 %collective-permute-start.10 = (bf16[256,128]{1,0:T(8,128)(2,1)S(1)}, bf16[256,128]{1,0:T(8,128)(2,1)S(1)}, u32[]{:S(2)}, u32[]{:S(2)}) collective-permute-start(bf16[256,128]{1,0:T(8,128)(2,1)S(1)} %get-tuple-element.82), channel_id=1, source_target_pairs={{0,4},{4,0},{8,12},{12,8},{16,20},{20,16},{24,28},{28,24},{32,36},... | collective-permute-start | bytes 196616 | tf_op jit(solution)/shard_map/ppermute | solution.py:516
  16.7 7.2 %collective-permute-start.8 = (f32[80,128]{1,0:T(8,128)S(1)}, f32[80,128]{1,0:T(8,128)S(1)}, u32[]{:S(2)}, u32[]{:S(2)}) collective-permute-start(f32[80,128]{1,0:T(8,128)S(1)} %add_add_fusion.1), channel_id=1, source_target_pairs={{0,96},{4,100},{8,104},{12,108},{16,112},{20,116},{24,120},{28,124... | collective-permute-start | bytes 122888 | tf_op jit(solution)/shard_map/ppermute | solution.py:524
  36.8 7.1 %collective-permute-start.11 = (bf16[256,1024]{1,0:T(8,128)(2,1)S(1)}, bf16[256,1024]{1,0:T(8,128)(2,1)S(1)}, u32[]{:S(2)}, u32[]{:S(2)}) collective-permute-start(bf16[256,1024]{1,0:T(8,128)(2,1)S(1)} %get-tuple-element.89), channel_id=1, source_target_pairs={{0,4},{4,0},{8,12},{12,8},{16,20},{20,16},{24,28},{28,24},{32,36},... | collective-permute-start | bytes 1572872 | tf_op jit(solution)/shard_map/ppermute | solution.py:516
  38.0 28.1 %all-to-all-start = ((bf16[16,144,256]{2,1,0:T(8,128)(2,1)}), bf16[16,144,256]{2,1,0:T(8,128)(2,1)S(1)}, u32[]{:S(2)}, u32[]{:S(2)}) async-start(bf16[16,144,256]{2,1,0:T(8,128)(2,1)} %get-tuple-element.98), calls=%async_computation | async-start | bytes 2359296 | tf_op jit(solution)/shard_map/all_to_all | solution.py:539
  46.0 9.8 %collective-permute-start.14 = (bf16[304,256]{1,0:T(8,128)(2,1)S(1)}, bf16[304,256]{1,0:T(8,128)(2,1)S(1)}, u32[]{:S(2)}, u32[]{:S(2)}) collective-permute-start(bf16[304,256]{1,0:T(8,128)(2,1)S(1)} %get-tuple-element.94), channel_id=1, source_target_pairs={{0,2},{1,3},{2,0},{3,1},{4,6},{5,7},{6,4},{7,5},{8,10},{9,11},{10,... | collective-permute-start | bytes 466952 | tf_op jit(solution)/shard_map/ppermute | solution.py:528
  48.7 7.2 %collective-permute-start.15 = (bf16[304,256]{1,0:T(8,128)(2,1)S(1)}, bf16[304,256]{1,0:T(8,128)(2,1)S(1)}, u32[]{:S(2)}, u32[]{:S(2)}) collective-permute-start(bf16[304,256]{1,0:T(8,128)(2,1)S(1)} %get-tuple-element.95), channel_id=1, source_target_pairs={{0,3},{1,0},{2,1},{3,2},{4,7},{5,4},{6,5},{7,6},{8,11},{9,8},{10,9... | collective-permute-start | bytes 466952 | tf_op jit(solution)/shard_map/ppermute | solution.py:528
  59.8 9.8 %collective-permute-start.18 = (bf16[256,256]{1,0:T(8,128)(2,1)S(1)}, bf16[256,256]{1,0:T(8,128)(2,1)S(1)}, u32[]{:S(2)}, u32[]{:S(2)}) collective-permute-start(bf16[256,256]{1,0:T(8,128)(2,1)S(1)} %add_convert_fusion.3.refs_1_), channel_id=1, source_target_pairs={{0,3},{1,0},{2,1},{3,2},{4,7},{5,4},{6,5},{7,6},{8,11},{9,8},{10,9... | collective-permute-start | bytes 393224 | tf_op jit(solution)/shard_map/ppermute | solution.py:528
  62.1 8.2 %collective-permute-start.17 = (bf16[256,256]{1,0:T(8,128)(2,1)S(1)}, bf16[256,256]{1,0:T(8,128)(2,1)S(1)}, u32[]{:S(2)}, u32[]{:S(2)}) collective-permute-start(bf16[256,256]{1,0:T(8,128)(2,1)S(1)} %add_convert_fusion.3.refs_1_), channel_id=1, source_target_pairs={{0,2},{1,3},{2,0},{3,1},{4,6},{5,7},{6,4},{7,5},{8,10},{9,11},{10,... | collective-permute-start | bytes 393224 | tf_op jit(solution)/shard_map/ppermute | solution.py:528
  62.6 7.7 %collective-permute-start.16 = (bf16[256,256]{1,0:T(8,128)(2,1)S(1)}, bf16[256,256]{1,0:T(8,128)(2,1)S(1)}, u32[]{:S(2)}, u32[]{:S(2)}) collective-permute-start(bf16[256,256]{1,0:T(8,128)(2,1)S(1)} %add_convert_fusion.3.refs_1_), channel_id=1, source_target_pairs={{0,1},{1,2},{2,3},{3,0},{4,5},{5,6},{6,7},{7,4},{8,9},{9,10},{10,1... | collective-permute-start | bytes 393224 | tf_op jit(solution)/shard_map/ppermute | solution.py:528
  63.5 9.6 %collective-permute-start.24 = (f32[48,128]{1,0:T(8,128)S(1)}, f32[48,128]{1,0:T(8,128)S(1)}, u32[]{:S(2)}, u32[]{:S(2)}) collective-permute-start(f32[48,128]{1,0:T(8,128)S(1)} %add_add_fusion.3.refs_2_), channel_id=1, source_target_pairs={{0,24},{4,28},{8,0},{12,4},{16,8},{20,12},{24,16},{28,20},{32,56},... | collective-permute-start | bytes 73736 | tf_op jit(solution)/shard_map/ppermute | solution.py:520
  65.5 7.6 %collective-permute-start.23 = (f32[48,128]{1,0:T(8,128)S(1)}, f32[48,128]{1,0:T(8,128)S(1)}, u32[]{:S(2)}, u32[]{:S(2)}) collective-permute-start(f32[48,128]{1,0:T(8,128)S(1)} %add_add_fusion.3.refs_2_), channel_id=1, source_target_pairs={{0,16},{4,20},{8,24},{12,28},{16,0},{20,4},{24,8},{28,12},{32,48},... | collective-permute-start | bytes 73736 | tf_op jit(solution)/shard_map/ppermute | solution.py:520
  73.8 7.7 %collective-permute-start.25 = (f32[48,128]{1,0:T(8,128)S(1)}, f32[48,128]{1,0:T(8,128)S(1)}, u32[]{:S(2)}, u32[]{:S(2)}) collective-permute-start(f32[48,128]{1,0:T(8,128)S(1)} %add_add_fusion.2.refs_1_), channel_id=1, source_target_pairs={{0,4},{4,0},{8,12},{12,8},{16,20},{20,16},{24,28},{28,24},{32,36},... | collective-permute-start | bytes 73736 | tf_op jit(solution)/shard_map/ppermute | solution.py:516
  87.3 11.7 %collective-permute-start.38 = (bf16[4,144,256]{2,1,0:T(8,128)(2,1)S(1)}, bf16[4,144,256]{2,1,0:T(8,128)(2,1)S(1)}, u32[]{:S(2)}, u32[]{:S(2)}) collective-permute-start(bf16[4,144,256]{2,1,0:T(8,128)(2,1)S(1)} %pad_maximum_fusion.refs_0_.refs_3_), channel_id=1, source_target_pairs={{0,24},{4,28},{8,0},{12,4},{16,8},{20,12},{24,16},{28,20},{32,56},... | collective-permute-start | bytes 884744 | tf_op jit(solution)/shard_map/ppermute | solution.py:520
  88.1 12.7 %collective-permute-start.37 = (bf16[4,144,256]{2,1,0:T(8,128)(2,1)S(1)}, bf16[4,144,256]{2,1,0:T(8,128)(2,1)S(1)}, u32[]{:S(2)}, u32[]{:S(2)}) collective-permute-start(bf16[4,144,256]{2,1,0:T(8,128)(2,1)S(1)} %pad_maximum_fusion.refs_0_.refs_3_), channel_id=1, source_target_pairs={{0,16},{4,20},{8,24},{12,28},{16,0},{20,4},{24,8},{28,12},{32,48},... | collective-permute-start | bytes 884744 | tf_op jit(solution)/shard_map/ppermute | solution.py:520
  89.3 15.6 %collective-permute-start.36 = (bf16[4,144,256]{2,1,0:T(8,128)(2,1)S(1)}, bf16[4,144,256]{2,1,0:T(8,128)(2,1)S(1)}, u32[]{:S(2)}, u32[]{:S(2)}) collective-permute-start(bf16[4,144,256]{2,1,0:T(8,128)(2,1)S(1)} %pad_maximum_fusion.refs_0_.refs_3_), channel_id=1, source_target_pairs={{0,8},{4,12},{8,16},{12,20},{16,24},{20,28},{24,0},{28,4},{32,40},... | collective-permute-start | bytes 884744 | tf_op jit(solution)/shard_map/ppermute | solution.py:520
  93.6 7.2 %collective-permute-start.27 = (bf16[128,512]{1,0:T(8,128)(2,1)S(1)}, bf16[128,512]{1,0:T(8,128)(2,1)S(1)}, u32[]{:S(2)}, u32[]{:S(2)}) collective-permute-start(bf16[128,512]{1,0:T(8,128)(2,1)S(1)} %add_convert_fusion.2), channel_id=1, source_target_pairs={{0,32},{4,36},{8,40},{12,44},{16,48},{20,52},{24,56},{28,60},{32,6... | collective-permute-start | bytes 393224 | tf_op jit(solution)/shard_map/ppermute | solution.py:524
  95.2 10.6 %collective-permute-start.39 = (bf16[4,144,256]{2,1,0:T(8,128)(2,1)S(1)}, bf16[4,144,256]{2,1,0:T(8,128)(2,1)S(1)}, u32[]{:S(2)}, u32[]{:S(2)}) collective-permute-start(bf16[4,144,256]{2,1,0:T(8,128)(2,1)S(1)} %pad_maximum_fusion.refs_0_.refs_3_), channel_id=1, source_target_pairs={{0,4},{4,0},{8,12},{12,8},{16,20},{20,16},{24,28},{28,24},{32,36},... | collective-permute-start | bytes 884744 | tf_op jit(solution)/shard_map/ppermute | solution.py:516
  98.9 8.1 %collective-permute-start.42 = (bf16[4,144,256]{2,1,0:T(8,128)(2,1)S(1)}, bf16[4,144,256]{2,1,0:T(8,128)(2,1)S(1)}, u32[]{:S(2)}, u32[]{:S(2)}) collective-permute-start(bf16[4,144,256]{2,1,0:T(8,128)(2,1)S(1)} %collective-permute-done.38.refs_3_.refs_6_), channel_id=1, source_target_pairs={{0,4},{4,0},{8,12},{12,8},{16,20},{20,16},{24,28},{28,24},{32,36},... | collective-permute-start | bytes 884744 | tf_op jit(solution)/shard_map/ppermute | solution.py:516
  105.4 6.8 %collective-permute-start.32 = (bf16[128,512]{1,0:T(8,128)(2,1)S(1)}, bf16[128,512]{1,0:T(8,128)(2,1)S(1)}, u32[]{:S(2)}, u32[]{:S(2)}) collective-permute-start(bf16[128,512]{1,0:T(8,128)(2,1)S(1)} %add_convert_fusion.1), channel_id=1, source_target_pairs={{0,24},{4,28},{8,0},{12,4},{16,8},{20,12},{24,16},{28,20},{32,56},... | collective-permute-start | bytes 393224 | tf_op jit(solution)/shard_map/ppermute | solution.py:520
  107.0 8.5 %collective-permute-start.30 = (bf16[128,512]{1,0:T(8,128)(2,1)S(1)}, bf16[128,512]{1,0:T(8,128)(2,1)S(1)}, u32[]{:S(2)}, u32[]{:S(2)}) collective-permute-start(bf16[128,512]{1,0:T(8,128)(2,1)S(1)} %add_convert_fusion.1), channel_id=1, source_target_pairs={{0,8},{4,12},{8,16},{12,20},{16,24},{20,28},{24,0},{28,4},{32,40},... | collective-permute-start | bytes 393224 | tf_op jit(solution)/shard_map/ppermute | solution.py:520
  (36 other events, 294.5 us)

commit v5 on v4

--- a/solution.py
+++ b/solution.py
@@ -13,7 +13,7 @@
 FH = 1024
 N1 = 1024
 N2 = 2048
-TB = 1024
+TB = N1
 HC = 1024
 LIMIT = 36
 F32 = jnp.float32
@@ -200,22 +200,19 @@
     )(at, tokens, keep_row, wq, wk, wv)
 
 
-def query_kernel(at_ref, tok_ref, oth_ref, wq_ref, tokt_ref, q_ref):
-    wqt = flip(wq_ref[...]).astype(BF)
-    for half, ref in enumerate((tok_ref, oth_ref)):
-        tokt = flip(ref[...]).astype(BF)
-        cols = slice(N1 * half, N1 * half + N1)
-        tokt_ref[:, cols] = tokt
-        pre = mm(wqt, tokt)
-        q_ref[:, cols] = jnp.where(pre > 0, pre + 1.0, jnp.exp(jnp.minimum(pre, 0.0))).astype(BF)
-
-
-def query_call(at, tokens, tokens_o, wq):
-    out = (struct((D, N2), BF), struct((D, N2), BF))
-    return call(query_kernel, out, 4e8, 3e6, "queries")(at, tokens, tokens_o, wq)
-
-
-def gate_kernel(at_ref, ck_ref, cko_ref, wgeo_ref, bgeo_ref, wroute_ref, r_ref, g_ref):
+def query_kernel(at_ref, tok_ref, wq_ref, tokt_ref, q_ref):
+    tokt = flip(tok_ref[...]).astype(BF)
+    tokt_ref[...] = tokt
+    pre = mm(flip(wq_ref[...]).astype(BF), tokt)
+    q_ref[...] = jnp.where(pre > 0, pre + 1.0, jnp.exp(jnp.minimum(pre, 0.0))).astype(BF)
+
+
+def query_call(at, tokens, wq, name):
+    out = (struct((D, N1), BF), struct((D, N1), BF))
+    return call(query_kernel, out, 2e8, 2e6, name, fetch=2)(at, tokens, wq)
+
+
+def gate_kernel(at_ref, wgeo_ref, bgeo_ref, wroute_ref, ck_ref, cko_ref, r_ref, g_ref):
     geo = [column_of(wgeo_ref[k : k + 1, :]) for k in range(3)]
     bias = column_of(bgeo_ref[...])
     for half, ref in enumerate((ck_ref, cko_ref)):
@@ -225,16 +222,14 @@
             pre = pre + geo[k] * ref[k : k + 1, :]
         r = jnp.tanh(pre)
         r_ref[:, cols] = r
-        logit = lax.dot_general(
-            wroute_ref[...], r, (((0,), (0,)), ((), ())), precision=lax.Precision.HIGHEST, preferred_element_type=F32
-        )
+        logit = jnp.dot(wroute_ref[...], r, precision=lax.Precision.HIGHEST, preferred_element_type=F32)
         expo = jnp.exp(logit)
         g_ref[:, cols] = expo / jnp.sum(expo, axis=0, keepdims=True)
 
 
-def gate_call(at, ck, ck_o, wgeo, bgeo, wroute):
+def gate_call(at, wgeo, bgeo, wroute, ck, ck_o):
     out = (struct((64, N2), F32), struct((8, N2), F32))
-    return call(gate_kernel, out, 1e8, 1e6, "gate")(at, ck, ck_o, wgeo, bgeo, wroute)
+    return call(gate_kernel, out, 1e8, 1e6, "gate", fetch=3)(at, wgeo, bgeo, wroute, ck, ck_o)
 
 
 def own_gate(at_ref, gates):
@@ -252,13 +247,13 @@
         gate = keep * own_gate(at_ref, g_ref[:, cols])[0]
         df_ref[:, cols] = (flip(cot) * gate).astype(BF)
         for j in range(0, FH, 256):
-            back_ref[j : j + 256, cols] = (mm_nt(wout_ref[core, j : j + 256, :], cot) * gate).astype(BF)
+            back_ref[j : j + 256, cols] = mm_nt(wout_ref[core, j : j + 256, :], cot) * gate
     wint_ref[...] = flip(win_ref[core]).astype(BF)
 
 
 def back_call(at, cot, cot_o, ck, ck_o, g, w_in, w_out):
-    out = (struct((D, N1), BF), struct((D, N2), BF), struct((FH, N2), BF), struct((FH, D), BF))
-    return call(back_kernel, out, 11e8, 8e6, "cotangent_back")(at, cot, cot_o, ck, ck_o, g, w_in, w_out)
+    out = (struct((D, N1), BF), struct((D, N2), BF), struct((FH, N2), F32), struct((FH, D), BF))
+    return call(back_kernel, out, 11e8, 8e6, "cotangent_back", limit=12)(at, cot, cot_o, ck, ck_o, g, w_in, w_out)
 
 
 GELU_A = 0.7978845608028654
@@ -266,7 +261,7 @@
 
 
 def expert_kernel(
-    at_ref, msg_ref, m_ref, mo_ref, tokt_ref, q_ref, dy_ref, df_ref, back_ref, g_ref, r_ref, win_ref, wint_ref,
+    at_ref, msg_ref, m_ref, mo_ref, tokt_ref, tokto_ref, q_ref, qo_ref, dy_ref, df_ref, back_ref, g_ref, r_ref, win_ref, wint_ref,
     own_ref, oth_ref, kvt_ref, ks_ref, keep_msg, send_msg, pieces_ref,
     gw1, gw2, dkv, route,
 ):
@@ -282,11 +277,12 @@
 
     def step(i, first):
         cols = slice(TB * i, TB * i + TB)
-        q = q_ref[:, cols]
+        q = (q_ref if i == 0 else qo_ref)[...]
+        tokt = (tokt_ref if i == 0 else tokto_ref)[...]
         both = mm(sums, q)
         rden = 1.0 / (both[2 * D : 3 * D] + both[3 * D :])
         attn = (both[:D] + both[D : 2 * D]) * rden
-        mid = (tokt_ref[:, cols].astype(F32) + attn).astype(BF)
+        mid = (tokt.astype(F32) + attn).astype(BF)
         df = df_ref[:, cols]
         dmid = dy_ref[:, cols].astype(F32) if TB * i < N1 else jnp.zeros((D, TB), F32)
         stat = jnp.zeros((1, TB), F32)
@@ -297,9 +293,9 @@
             half = 0.5 + 0.5 * jnp.tanh(u * (GELU_A + GELU_B * u2))
             act = u * half
             slope = half + act * (1.0 - half) * (2.0 * GELU_A + 6.0 * GELU_B * u2)
-            back = back_ref[rows, cols].astype(F32)
-            stat = stat + jnp.sum(act * back, axis=0, keepdims=True)
+            back = back_ref[rows, cols]
             act = act.astype(BF)
+            stat = stat + jnp.sum(act.astype(F32) * back, axis=0, keepdims=True)
             du = (back * slope).astype(BF)
             dw2, dw1 = mm_nt(act, df), mm_nt(du, mid)
             gw2[rows, :] = dw2 if first else gw2[rows, :] + dw2
@@ -344,7 +340,7 @@
     keep_msg[...], send_msg[...] = ordered(core, *halves)
 
 
-def expert_call(at, msg, m, m_o, tokt, q, dy, df, back, g, r, w_in, wint):
+def expert_call(at, msg, m, m_o, tokt, tokt_o, q, q_o, dy, df, back, g, r, w_in, wint):
     return call(
         expert_kernel,
         (
@@ -354,20 +350,20 @@
         6e9, 12e6, "expert",
         [pltpu.VMEM((FH, D), F32)] * 2 + [pltpu.VMEM((2 * D + 32, D), F32), pltpu.VMEM((8, 64), F32)],
         limit=LIMIT,
-    )(at, msg, m, m_o, tokt, q, dy, df, back, g, r, w_in, wint)
+    )(at, msg, m, m_o, tokt, tokt_o, q, q_o, dy, df, back, g, r, w_in, wint)
 
 
 def dmid_kernel(at_ref, own_ref, oth_ref, msg_ref, msgo_ref, *out_refs):
     hi, lo = split2(msg_ref[...] + msgo_ref[...])
     for d, ref in enumerate(out_refs):
         cols = pl.ds(pl.multiple_of(lax.rem(at_ref[2] + d, 4) * 256, 256), 256)
-        ref[0:256, :] = (own_ref[:, cols] + oth_ref[:, cols].astype(F32)).astype(BF)
-        ref[256:304, 0:128] = hi
-        ref[256:304, 128:256] = lo
+        ref[0:256, :] = (own_ref[:, cols] + oth_ref[:, cols].astype(F32)).astype(ref.dtype)
+        ref[256:304, 0:128] = hi.astype(ref.dtype)
+        ref[256:304, 128:256] = lo.astype(ref.dtype)
 
 
 def dmid_call(at, own, oth, msg, msg_o):
-    return call(dmid_kernel, (struct((304, 256), BF),) * 4, 1e6, 2e6, "dmid_pieces")(at, own, oth, msg, msg_o)
+    return call(dmid_kernel, (struct((304, 256), F32),) + (struct((304, 256), BF),) * 3, 1e6, 2e6, "dmid_pieces")(at, own, oth, msg, msg_o)
 
 
 def back_query_kernel(
@@ -386,22 +382,24 @@
     mask = head_mask(D, D)
     ksh, ksl = split2(jnp.where(mask, ks, 0.0))
     kch, kcl = split2(jnp.where(mask, column_of(ks), 0.0))
-    num = mm(kvth, q) + mm(kvtl, q)
-    rden = 1.0 / (mm(ksh, q) + mm(ksl, q))
-    attn = num * rden
+    both = mm(jnp.concatenate([kvth, kvtl, ksh, ksl], axis=0), q)
+    rden = 1.0 / (both[2 * D : 3 * D] + both[3 * D :])
+    attn = (both[:D] + both[D : 2 * D]) * rden
     dnum = dmid * rden
     nh, nl = split2(dnum)
     zh, zl = split2(dnum * attn)
-    dq = (mm(kvh, nh) - mm(kch, zh)) + (mm(kvl, nh) - mm(kcl, zh)) + (mm(kvh, nl) - mm(kch, zl))
+    left = jnp.concatenate([kvh, -kch], axis=1)
+    both = mm(jnp.concatenate([left, jnp.concatenate([kvl, -kcl], axis=1)], axis=0), jnp.concatenate([nh, zh], axis=0))
+    dq = both[:D] + both[D:] + mm(left, jnp.concatenate([nl, zl], axis=0))
     wq = wq_ref[...]
     dqp = (dq * qslope_ref[...]).astype(BF)
     gx_ref[...] = dmid + mm(wq, dqp)
     gq_ref[...] = mm_nt(tokt, dqp)
 
 
-def back_query_call(at, dm, kvt, ks, tokt, q, qslope, wq):
+def back_query_call(at, dm, kvt, ks, tokt, q, qslope, wq, after):
     out = (struct((D, N1), F32), struct((D, D), F32))
-    return call(back_query_kernel, out, 2e9, 5e6, "back_query", [pltpu.VMEM((D, N1), F32)])(
+    return call(back_query_kernel, out, 2e9, 5e6, "back_query", [pltpu.VMEM((D, N1), F32)], after)(
         at, *dm, kvt, ks, tokt, q, qslope, wq
     )
 
@@ -491,12 +489,12 @@
     gv_ref[...] = mm(m, hi) + mm(m, lo)
     sums = halves[0][40:48, 0:64]
     at_row = lax.broadcasted_iota(jnp.int32, sums.shape, 0)
-    cols = [column_of(jnp.sum(jnp.where(at_row == 2 * y + e, sums, 0.0), axis=0, keepdims=True)) for e in range(2)]
-    route_ref[...] = jnp.concatenate(cols, axis=1)
+    for e in range(2):
+        route_ref[e : e + 1, :] = jnp.sum(jnp.where(at_row == 2 * y + e, sums, 0.0), axis=0, keepdims=True)
 
 
 def place_m_call(at, msg, msg_o, pieces):
-    out = (struct((D, D), F32), struct((64, 2), F32))
+    out = (struct((D, D), F32), struct((2, 64), F32))
     return call(place_m_kernel, out, 1e8, 1e6, "grad_wv", [pltpu.VMEM((2, D, 128), BF)])(at, msg, msg_o, *pieces)
 
 
@@ -550,15 +548,16 @@
     tokens_o, cot_o = swap_core(tokens), swap_core(cotangent)
     ck, msg, m, m_away = keys_call(at, tokens, keep[None, :], coords, w_key, w_value)
     ck_o, m_o = swap_core(ck), swap_core(m_away)
-    tokt, q = query_call(at, tokens, tokens_o, w_query)
-    r, g = gate_call(at, ck, ck_o, w_geo, b_geo[None, :], w_route)
+    tokt, q = query_call(at, tokens, w_query, "queries")
+    tokt_o, q_o = query_call(at, tokens_o, w_query, "queries_other")
+    r, g = gate_call(at, w_geo, b_geo[None, :], w_route.T, ck, ck_o)
     dy, df, back, wint = back_call(at, cotangent, cot_o, ck, ck_o, g, w_in, w_out)
 
     msg = add([msg, swap_core(msg)], (), F32)
     msg = add([msg] + star(msg, to_x), (q, g), F32)
-    msg = add([msg] + star(msg, to_z), (back,), F32)
+    msg = add([msg] + star(msg, to_z), (back, q_o), F32)
     own, oth, kvt, ks, msg2, msg2_away, pieces = expert_call(
-        at, msg, m, m_o, tokt, q, dy, df, back, g, r, w_in, wint
+        at, msg, m, m_o, tokt, tokt_o, q, q_o, dy, df, back, g, r, w_in, wint
     )
 
     pieces = exchange(pieces)
@@ -566,14 +565,14 @@
     p0, p1, p2, p3 = dmid_call(at, own, swap_core(oth), msg2, swap_core(msg2_away))
     arrived = [p0, to_y(p1, 1), to_y(p2, 2), to_y(p3, 3)]
     msg2 = add([p[256:, :128] for p in arrived] + [p[256:, 128:] for p in arrived], (), F32)
-    dm = add([p[:256] for p in arrived])
+    dm = add([p[:256] for p in arrived], (), BF)
     dm = [dm] + star(dm, to_y)
     msg2 = msg2_z = add([msg2] + star(msg2, to_z), (), F32)
 
     pieces = chips_call(at, pieces, (msg2_z,))
 
     tokt, q, qslope, km, v, slope = again_call(at, tokens, keep[None, :], w_query, w_key, w_value, (pieces,))
-    gx, gq = back_query_call(at, dm, kvt, ks, tokt, q, qslope, w_query)
+    gx, gq = back_query_call(at, dm, kvt, ks, tokt, q, qslope, w_query, ())
     msg2 = add([msg2] + star(msg2, to_x), (gq,), F32)
     msg2_o = swap_core(msg2)
     dk, dv, part, away = back_keys_call(at, msg2, msg2_o, km, v, slope, tokt, gq)
@@ -589,7 +588,7 @@
     part = add([part] + star(part, to_z), (grad_x,))
     part = add([part] + star(part, to_x), (grad_w_in, grad_wv))
     grad_wq, grad_wk = place_proj_call(at, part, swap_core(part))
-    return (grad_x, grad_wq, grad_wk, grad_wv, grad_w_in, grad_w_out, grad_route)
+    return (grad_x, grad_wq, grad_wk, grad_wv, grad_w_in, grad_w_out, grad_route.T)
 
 
 def solution(mesh):

time: 119 us -> 118 us (level)
  local copies, waits for them, and re-layouts: 4.21 us -> 0.82 us
  Pallas kernels: 35.6 us -> 38.2 us
    unnamed x32 -> x18, local copies, waits for them, and re-layouts: 4.13 us -> 0.74 us
    pallas_call x13 -> x14, Pallas kernels: 32.5 us -> 35.1 us  [run(): pl.pallas_call(body, in_specs=[pl.BlockSpec(memory_space=pltpu.SMEM)] + [...]
    ppermute x14, waiting for transfers between devices: 1.29 us -> 2.7 us  [swap_core(): return lax.ppermute(v, 'pts', [(i, i ^ 1) for i in range(32)])]
    ppermute x12, waiting for transfers between devices: 9.73 us -> 8.5 us  [to_z(): return lax.ppermute(v, 'pts', [(i, (i + 8 * d) % 32) for i in range(32)])]
  transfers between devices with their start and end apart: 45 -> 45, of which waited for: 15 -> 13; matrix products, arithmetic and copies ran while one was open for 1% -> 0% of each run, Pallas kernels for 20% -> 22%
where the time goes in v5:
time: 118 us
  starting transfers between devices  54.6 us (46%)
  Pallas kernels  38.2 us (32%)
  waiting for transfers between devices  23.2 us (20%)
    pallas_call x14, Pallas kernels, run(): pl.pallas_call(body, in_specs=[pl.BlockSpec(memory_space=pltpu.SMEM)] + [...  35.1 us
    ppermute x14, starting transfers between devices, swap_core(): return lax.ppermute(v, 'pts', [(i, i ^ 1) for i in range(32)])  17.3 us
    ppermute x12, starting transfers between devices, to_z(): return lax.ppermute(v, 'pts', [(i, (i + 8 * d) % 32) for i in range(32)])  13.2 us
    ppermute x12, starting transfers between devices, to_x(): lax.ppermute(v, 'pts', [(i, i & ~6 | i + 2 * d & 6) for i in range(32)])  10.9 us
    ppermute x12, waiting for transfers between devices, to_z(): return lax.ppermute(v, 'pts', [(i, (i + 8 * d) % 32) for i in range(32)])  8.5 us
    ppermute x6, starting transfers between devices, to_y(): return lax.ppermute(v, 'exp', [(i, (i + d) % 4) for i in range(4)])  8.2 us
    ppermute x6, waiting for transfers between devices, to_y(): return lax.ppermute(v, 'exp', [(i, (i + d) % 4) for i in range(4)])  6.15 us
    ppermute x12, waiting for transfers between devices, to_x(): lax.ppermute(v, 'pts', [(i, i & ~6 | i + 2 * d & 6) for i in range(32)])  5.8 us
  transfers between devices with their start and end apart: 45, of which 13 were waited for; matrix products, arithmetic and copies ran while one was open for 0% of the time, Pallas kernels for 22%

profile of v5, /device:TPU:1, one launch (start us, length us, event | category | flops | bytes accessed | tf_op | source)
XLA Modules:
  0.0 118.0 jit_solution(6122450552747509007)
XLA Ops:
  2.3 2.9 %keys.1 = (f32[4,1024]{1,0:T(4,128)S(1)}, f32[80,128]{1,0:T(8,128)S(1)}, bf16[256,128]{1,0:T(8,128)(2,1)S(1)}, bf16[256,128]{1,0:T(8,128)(2,1)S(1)}) custom-call(s32[5]{0:T(128)S(1)} %stack.38.refs_0_.at_ref, bf16[1024,256]{1,0:T(8,128)(2,1)} %refs_1_.9, s32[1,1024]{1,0:T(1,128)} %bitcast.18, f32[3,1024]{1,0:T(4,128)} %refs_3_.2, bf16[256,256]{1,0:T(8,128)(2,1)} %refs_4_.5, ...), custom_call_target="tpu_custom_call" | custom-call | flops 400000000 | bytes 3000000 | tf_op jit(solution)/shard_map/keys/pallas_call | solution.py:106
  6.6 2.6 %collective-permute-start.3 = (f32[80,128]{1,0:T(8,128)S(1)}, f32[80,128]{1,0:T(8,128)S(1)}, u32[]{:S(2)}, u32[]{:S(2)}) collective-permute-start(f32[80,128]{1,0:T(8,128)S(1)} %add.105), channel_id=1, source_target_pairs={{0,24},{4,28},{8,0},{12,4},{16,8},{20,12},{24,16},{28,20},{32,56},... | collective-permute-start | bytes 122888 | tf_op jit(solution)/shard_map/ppermute | solution.py:518
  10.3 2.1 %queries.1 = (bf16[256,1024]{1,0:T(8,128)(2,1)S(1)}, bf16[256,1024]{1,0:T(8,128)(2,1)S(1)}) custom-call(s32[5]{0:T(128)S(1)} %stack.38.refs_0_.at_ref, bf16[1024,256]{1,0:T(8,128)(2,1)} %refs_1_.9, bf16[256,256]{1,0:T(8,128)(2,1)} %refs_10_.1), custom_call_target="tpu_custom_call" | custom-call | flops 200000000 | bytes 2000000 | tf_op jit(solution)/shard_map/queries/pallas_call | solution.py:106
  12.5 1.8 %gate.1 = (f32[64,2048]{1,0:T(8,128)S(1)}, f32[8,2048]{1,0:T(8,128)S(1)}) custom-call(s32[5]{0:T(128)S(1)} %stack.38.refs_0_.at_ref, f32[3,64]{1,0:T(4,128)} %refs_1_.7, f32[1,64]{1,0:T(1,128)} %bitcast.21, f32[8,64]{1,0:T(8,128)} %bitcast.17, f32[4,1024]{1,0:T(4,128)S(1)} %get-tuple-element.72.refs_4_.refs_3_, ...), custom_call_target="tpu_custom_call" | custom-call | flops 100000000 | bytes 1000000 | tf_op jit(solution)/shard_map/gate/pallas_call | solution.py:106
  15.6 3.8 %collective-permute-start.7 = (f32[80,128]{1,0:T(8,128)S(1)}, f32[80,128]{1,0:T(8,128)S(1)}, u32[]{:S(2)}, u32[]{:S(2)}) collective-permute-start(f32[80,128]{1,0:T(8,128)S(1)} %add_add_fusion.1), channel_id=1, source_target_pairs={{0,96},{4,100},{8,104},{12,108},{16,112},{20,116},{24,120},{28,124... | collective-permute-start | bytes 122888 | tf_op jit(solution)/shard_map/ppermute | solution.py:522
  20.1 2.1 %cotangent_back.1 = (bf16[256,1024]{1,0:T(8,128)(2,1)S(1)}, bf16[256,2048]{1,0:T(8,128)(2,1)S(1)}, f32[1024,2048]{1,0:T(8,128)S(1)}, bf16[1024,256]{1,0:T(8,128)(2,1)S(1)}) custom-call(s32[5]{0:T(128)S(1)} %stack.38.refs_0_.at_ref, bf16[1024,256]{1,0:T(8,128)(2,1)S(1)} %copy-done.5, bf16[1024,256]{1,0:T(8,128)(2,1)S(1)} %collective-permute-done.8.refs_2_, ...), custom_call_target="tpu_custom_call" | custom-call | flops 1100000000 | bytes 8000000 | tf_op jit(solution)/shard_map/cotangent_back/pallas_call | solution.py:106
  22.2 2.2 %queries_other.1 = (bf16[256,1024]{1,0:T(8,128)(2,1)S(1)}, bf16[256,1024]{1,0:T(8,128)(2,1)S(1)}) custom-call(s32[5]{0:T(128)S(1)} %stack.38.refs_0_.at_ref, bf16[1024,256]{1,0:T(8,128)(2,1)} %collective-permute-done.9.refs_1_, bf16[256,256]{1,0:T(8,128)(2,1)} %refs_10_.1), custom_call_target="tpu_custom_call" | custom-call | flops 200000000 | bytes 2000000 | tf_op jit(solution)/shard_map/queries_other/pallas_call | solution.py:106
  24.5 10.9 %expert.1 = (f32[256,1024]{1,0:T(8,128)S(1)}, bf16[256,1024]{1,0:T(8,128)(2,1)S(1)}, f32[256,256]{1,0:T(8,128)S(1)}, f32[8,256]{1,0:T(8,128)S(1)}, f32[48,128]{1...) custom-call(s32[5]{0:T(128)S(1)} %stack.38.refs_0_.at_ref, f32[80,128]{1,0:T(8,128)S(1)} %add_add_fusion.refs_1_, ...), custom_call_target="tpu_custom_call" | custom-call | flops 6000000000 | bytes 12000000 | tf_op jit(solution)/shard_map/expert/pallas_call | solution.py:106
  37.3 4.9 %all-to-all-start = ((bf16[16,144,256]{2,1,0:T(8,128)(2,1)}), bf16[16,144,256]{2,1,0:T(8,128)(2,1)S(1)}, u32[]{:S(2)}, u32[]{:S(2)}) async-start(bf16[16,144,256]{2,1,0:T(8,128)(2,1)} %get-tuple-element.102), calls=%async_computation | async-start | bytes 2359296 | tf_op jit(solution)/shard_map/all_to_all | solution.py:537
  45.7 2.6 %collective-permute-start.14 = (bf16[304,256]{1,0:T(8,128)(2,1)S(1)}, bf16[304,256]{1,0:T(8,128)(2,1)S(1)}, u32[]{:S(2)}, u32[]{:S(2)}) collective-permute-start(bf16[304,256]{1,0:T(8,128)(2,1)S(1)} %get-tuple-element.98), channel_id=1, source_target_pairs={{0,2},{1,3},{2,0},{3,1},{4,6},{5,7},{6,4},{7,5},{8,10},{9,11},{10,... | collective-permute-start | bytes 466952 | tf_op jit(solution)/shard_map/ppermute | solution.py:526
  51.1 4.5 %collective-permute-done.14 = bf16[304,256]{1,0:T(8,128)(2,1)S(1)} collective-permute-done((bf16[304,256]{1,0:T(8,128)(2,1)S(1)}, bf16[304,256]{1,0:T(8,128)(2,1)S(1)}, u32[]{:S(2)}, u32[]{:S(2)}) %collective-permute-start.14) | collective-permute-done | bytes 155680 | tf_op jit(solution)/shard_map/ppermute | solution.py:526
  55.5 2.7 %collective-permute-start.21 = (f32[48,128]{1,0:T(8,128)S(1)}, f32[48,128]{1,0:T(8,128)S(1)}, u32[]{:S(2)}, u32[]{:S(2)}) collective-permute-start(f32[48,128]{1,0:T(8,128)S(1)} %convert_add_fusion), channel_id=1, source_target_pairs={{0,96},{4,100},{8,104},{12,108},{16,112},{20,116},{24,120},{28,124... | collective-permute-start | bytes 73736 | tf_op jit(solution)/shard_map/ppermute | solution.py:522
  59.5 2.3 %collective-permute-start.18 = (bf16[256,256]{1,0:T(8,128)(2,1)S(1)}, bf16[256,256]{1,0:T(8,128)(2,1)S(1)}, u32[]{:S(2)}, u32[]{:S(2)}) collective-permute-start(bf16[256,256]{1,0:T(8,128)(2,1)S(1)} %add_convert_fusion.3.refs_1_), channel_id=1, source_target_pairs={{0,3},{1,0},{2,1},{3,2},{4,7},{5,4},{6,5},{7,6},{8,11},{9,8},{10,9... | collective-permute-start | bytes 393224 | tf_op jit(solution)/shard_map/ppermute | solution.py:526
  66.5 2.8 %queries_keys_again.1 = (bf16[256,1024]{1,0:T(8,128)(2,1)S(1)}, bf16[256,1024]{1,0:T(8,128)(2,1)S(1)}, f32[256,1024]{1,0:T(8,128)S(1)}, bf16[256,1024]{1,0:T(8,1...) custom-call(s32[5]{0:T(128)S(1)} %stack.38.refs_0_.at_ref, bf16[1024,256]{1,0:T(8,128)(2,1)} %refs_1_.9, ...), custom_call_target="tpu_custom_call" | custom-call | flops 500000000 | bytes 3000000 | tf_op jit(solution)/shard_map/queries_keys_again/pallas_call | solution.py:106
  70.0 2.6 %back_query.1 = (f32[256,1024]{1,0:T(8,128)S(1)}, f32[256,256]{1,0:T(8,128)S(1)}) custom-call(s32[5]{0:T(128)S(1)} %stack.38.refs_0_.at_ref, bf16[256,256]{1,0:T(8,128)(2,1)S(1)} %add_convert_fusion.3.refs_1_, bf16[256,256]{1,0:T(8,128)(2,1)S(1)} %collective-permute-done.16.refs_2_, bf16[256,256]{1,0:T(8,128)(2,1)S(1)} %collective-permute-done.17.refs_3_, ...), custom_call_target="tpu_custom_call" | custom-call | flops 2000000000 | bytes 5000000 | tf_op jit(solution)/shard_map/back_query/pallas_call | solution.py:106
  73.3 4.6 %collective-permute-start.25 = (f32[48,128]{1,0:T(8,128)S(1)}, f32[48,128]{1,0:T(8,128)S(1)}, u32[]{:S(2)}, u32[]{:S(2)}) collective-permute-start(f32[48,128]{1,0:T(8,128)S(1)} %add_add_fusion.2.refs_1_), channel_id=1, source_target_pairs={{0,4},{4,0},{8,12},{12,8},{16,20},{20,16},{24,28},{28,24},{32,36},... | collective-permute-start | bytes 73736 | tf_op jit(solution)/shard_map/ppermute | solution.py:514
  77.9 2.1 %collective-permute-start.35 = (bf16[144,256]{1,0:T(8,128)(2,1)S(1)}, bf16[144,256]{1,0:T(8,128)(2,1)S(1)}, u32[]{:S(2)}, u32[]{:S(2)}) collective-permute-start(bf16[144,256]{1,0:T(8,128)(2,1)S(1)} %experts_sum.1.refs_6_), channel_id=1, source_target_pairs={{0,96},{4,100},{8,104},{12,108},{16,112},{20,116},{24,120},{28,124... | collective-permute-start | bytes 221192 | tf_op jit(solution)/shard_map/ppermute | solution.py:522
  84.7 2.2 %collective-permute-done.33 = bf16[144,256]{1,0:T(8,128)(2,1)S(1)} collective-permute-done((bf16[144,256]{1,0:T(8,128)(2,1)S(1)}, bf16[144,256]{1,0:T(8,128)(2,1)S(1)}, u32[]{:S(2)}, u32[]{:S(2)}) %collective-permute-start.33) | collective-permute-done | bytes 73760 | tf_op jit(solution)/shard_map/ppermute | solution.py:522
  90.7 2.6 %collective-permute-done.29 = bf16[128,512]{1,0:T(8,128)(2,1)S(1)} collective-permute-done((bf16[128,512]{1,0:T(8,128)(2,1)S(1)}, bf16[128,512]{1,0:T(8,128)(2,1)S(1)}, u32[]{:S(2)}, u32[]{:S(2)}) %collective-permute-start.29) | collective-permute-done | bytes 131104 | tf_op jit(solution)/shard_map/ppermute | solution.py:522
  94.9 3.7 %collective-permute-start.39 = (bf16[4,144,256]{2,1,0:T(8,128)(2,1)S(1)}, bf16[4,144,256]{2,1,0:T(8,128)(2,1)S(1)}, u32[]{:S(2)}, u32[]{:S(2)}) collective-permute-start(bf16[4,144,256]{2,1,0:T(8,128)(2,1)S(1)} %pad_maximum_fusion.refs_0_.refs_3_), channel_id=1, source_target_pairs={{0,4},{4,0},{8,12},{12,8},{16,20},{20,16},{24,28},{28,24},{32,36},... | collective-permute-start | bytes 884744 | tf_op jit(solution)/shard_map/ppermute | solution.py:514
  98.6 1.9 %grad_x.1 = bf16[1024,256]{1,0:T(8,128)(2,1)} custom-call(s32[5]{0:T(128)S(1)} %stack.38.refs_0_.at_ref, f32[256,1024]{1,0:T(8,128)S(1)} %get-tuple-element.106.refs_1_, bf16[256,1024]{1,0:T(8,128)(2,1)S(1)} %get-tuple-element.115.refs_2_, bf16[256,1024]{1,0:T(8,128)(2,1)S(1)} %get-tuple-element.116.refs_3_, bf16[256,256]{1,0:T(8,128)(2,1)S(1)} %copy-done, ...), custom_call_target="tpu_custom_call" | custom-call | flops 300000000 | bytes 3000000 | tf_op jit(solution)/shard_map/grad_x/pallas_call | solution.py:106
  100.5 2.2 %collective-permute-start.41 = (bf16[4,144,256]{2,1,0:T(8,128)(2,1)S(1)}, bf16[4,144,256]{2,1,0:T(8,128)(2,1)S(1)}, u32[]{:S(2)}, u32[]{:S(2)}) collective-permute-start(bf16[4,144,256]{2,1,0:T(8,128)(2,1)S(1)} %collective-permute-done.37.refs_2_.refs_5_), channel_id=1, source_target_pairs={{0,4},{4,0},{8,12},{12,8},{16,20},{20,16},{24,28},{28,24},{32,36},... | collective-permute-start | bytes 884744 | tf_op jit(solution)/shard_map/ppermute | solution.py:514
  107.0 3.1 %place_experts.1 = (f32[2,256,1024]{2,1,0:T(8,128)}, f32[2,1024,256]{2,1,0:T(8,128)}) custom-call(s32[5]{0:T(128)S(1)} %stack.38.refs_0_.at_ref, bf16[4,144,256]{2,1,0:T(8,128)(2,1)S(1)} %pad_maximum_fusion.refs_0_.refs_3_, bf16[4,144,256]{2,1,0:T(8,128)(2,1)S(1)} %collective-permute-done.36.refs_1_.refs_4_, ...), custom_call_target="tpu_custom_call" | custom-call | flops 1000000 | bytes 7000000 | tf_op jit(solution)/shard_map/place_experts/pallas_call | solution.py:462
  111.6 3.4 %collective-permute-done.30 = bf16[128,512]{1,0:T(8,128)(2,1)S(1)} collective-permute-done((bf16[128,512]{1,0:T(8,128)(2,1)S(1)}, bf16[128,512]{1,0:T(8,128)(2,1)S(1)}, u32[]{:S(2)}, u32[]{:S(2)}) %collective-permute-start.30) | collective-permute-done | bytes 131104 | tf_op jit(solution)/shard_map/ppermute | solution.py:518
  (111 shorter events, 40.8 us)
Async XLA Ops:
  0.7 18.8 %collective-permute-start.8 = (bf16[1024,256]{1,0:T(8,128)(2,1)}, bf16[1024,256]{1,0:T(8,128)(2,1)S(1)}, u32[]{:S(2)}, u32[]{:S(2)}) collective-permute-start(bf16[1024,256]{1,0:T(8,128)(2,1)} %refs_1_.8), channel_id=1, source_target_pairs={{0,4},{4,0},{8,12},{12,8},{16,20},{20,16},{24,28},{28,24},{32,36},... | collective-permute-start | bytes 1572872 | tf_op jit(solution)/shard_map/ppermute | solution.py:514
  2.2 20.1 %collective-permute-start.9 = (bf16[1024,256]{1,0:T(8,128)(2,1)}, bf16[1024,256]{1,0:T(8,128)(2,1)}, u32[]{:S(2)}, u32[]{:S(2)}) collective-permute-start(bf16[1024,256]{1,0:T(8,128)(2,1)} %refs_1_.9), channel_id=1, source_target_pairs={{0,4},{4,0},{8,12},{12,8},{16,20},{20,16},{24,28},{28,24},{32,36},... | collective-permute-start | bytes 1572872 | tf_op jit(solution)/shard_map/ppermute | solution.py:514
  6.6 7.7 %collective-permute-start.3 = (f32[80,128]{1,0:T(8,128)S(1)}, f32[80,128]{1,0:T(8,128)S(1)}, u32[]{:S(2)}, u32[]{:S(2)}) collective-permute-start(f32[80,128]{1,0:T(8,128)S(1)} %add.105), channel_id=1, source_target_pairs={{0,24},{4,28},{8,0},{12,4},{16,8},{20,12},{24,16},{28,20},{32,56},... | collective-permute-start | bytes 122888 | tf_op jit(solution)/shard_map/ppermute | solution.py:518
  14.3 10.2 %collective-permute-start.10 = (bf16[256,128]{1,0:T(8,128)(2,1)S(1)}, bf16[256,128]{1,0:T(8,128)(2,1)S(1)}, u32[]{:S(2)}, u32[]{:S(2)}) collective-permute-start(bf16[256,128]{1,0:T(8,128)(2,1)S(1)} %get-tuple-element.85), channel_id=1, source_target_pairs={{0,4},{4,0},{8,12},{12,8},{16,20},{20,16},{24,28},{28,24},{32,36},... | collective-permute-start | bytes 196616 | tf_op jit(solution)/shard_map/ppermute | solution.py:514
  15.6 8.8 %collective-permute-start.7 = (f32[80,128]{1,0:T(8,128)S(1)}, f32[80,128]{1,0:T(8,128)S(1)}, u32[]{:S(2)}, u32[]{:S(2)}) collective-permute-start(f32[80,128]{1,0:T(8,128)S(1)} %add_add_fusion.1), channel_id=1, source_target_pairs={{0,96},{4,100},{8,104},{12,108},{16,112},{20,116},{24,120},{28,124... | collective-permute-start | bytes 122888 | tf_op jit(solution)/shard_map/ppermute | solution.py:522
  36.1 7.3 %collective-permute-start.11 = (bf16[256,1024]{1,0:T(8,128)(2,1)S(1)}, bf16[256,1024]{1,0:T(8,128)(2,1)S(1)}, u32[]{:S(2)}, u32[]{:S(2)}) collective-permute-start(bf16[256,1024]{1,0:T(8,128)(2,1)S(1)} %get-tuple-element.93), channel_id=1, source_target_pairs={{0,4},{4,0},{8,12},{12,8},{16,20},{20,16},{24,28},{28,24},{32,36},... | collective-permute-start | bytes 1572872 | tf_op jit(solution)/shard_map/ppermute | solution.py:514
  37.3 28.5 %all-to-all-start = ((bf16[16,144,256]{2,1,0:T(8,128)(2,1)}), bf16[16,144,256]{2,1,0:T(8,128)(2,1)S(1)}, u32[]{:S(2)}, u32[]{:S(2)}) async-start(bf16[16,144,256]{2,1,0:T(8,128)(2,1)} %get-tuple-element.102), calls=%async_computation | async-start | bytes 2359296 | tf_op jit(solution)/shard_map/all_to_all | solution.py:537
  44.1 7.0 %collective-permute-start.13 = (bf16[304,256]{1,0:T(8,128)(2,1)S(1)}, bf16[304,256]{1,0:T(8,128)(2,1)S(1)}, u32[]{:S(2)}, u32[]{:S(2)}) collective-permute-start(bf16[304,256]{1,0:T(8,128)(2,1)S(1)} %get-tuple-element.97), channel_id=1, source_target_pairs={{0,1},{1,2},{2,3},{3,0},{4,5},{5,6},{6,7},{7,4},{8,9},{9,10},{10,1... | collective-permute-start | bytes 466952 | tf_op jit(solution)/shard_map/ppermute | solution.py:526
  45.7 9.8 %collective-permute-start.14 = (bf16[304,256]{1,0:T(8,128)(2,1)S(1)}, bf16[304,256]{1,0:T(8,128)(2,1)S(1)}, u32[]{:S(2)}, u32[]{:S(2)}) collective-permute-start(bf16[304,256]{1,0:T(8,128)(2,1)S(1)} %get-tuple-element.98), channel_id=1, source_target_pairs={{0,2},{1,3},{2,0},{3,1},{4,6},{5,7},{6,4},{7,5},{8,10},{9,11},{10,... | collective-permute-start | bytes 466952 | tf_op jit(solution)/shard_map/ppermute | solution.py:526
  48.3 7.2 %collective-permute-start.15 = (bf16[304,256]{1,0:T(8,128)(2,1)S(1)}, bf16[304,256]{1,0:T(8,128)(2,1)S(1)}, u32[]{:S(2)}, u32[]{:S(2)}) collective-permute-start(bf16[304,256]{1,0:T(8,128)(2,1)S(1)} %get-tuple-element.99), channel_id=1, source_target_pairs={{0,3},{1,0},{2,1},{3,2},{4,7},{5,4},{6,5},{7,6},{8,11},{9,8},{10,9... | collective-permute-start | bytes 466952 | tf_op jit(solution)/shard_map/ppermute | solution.py:526
  59.5 9.8 %collective-permute-start.18 = (bf16[256,256]{1,0:T(8,128)(2,1)S(1)}, bf16[256,256]{1,0:T(8,128)(2,1)S(1)}, u32[]{:S(2)}, u32[]{:S(2)}) collective-permute-start(bf16[256,256]{1,0:T(8,128)(2,1)S(1)} %add_convert_fusion.3.refs_1_), channel_id=1, source_target_pairs={{0,3},{1,0},{2,1},{3,2},{4,7},{5,4},{6,5},{7,6},{8,11},{9,8},{10,9... | collective-permute-start | bytes 393224 | tf_op jit(solution)/shard_map/ppermute | solution.py:526
  61.7 8.2 %collective-permute-start.17 = (bf16[256,256]{1,0:T(8,128)(2,1)S(1)}, bf16[256,256]{1,0:T(8,128)(2,1)S(1)}, u32[]{:S(2)}, u32[]{:S(2)}) collective-permute-start(bf16[256,256]{1,0:T(8,128)(2,1)S(1)} %add_convert_fusion.3.refs_1_), channel_id=1, source_target_pairs={{0,2},{1,3},{2,0},{3,1},{4,6},{5,7},{6,4},{7,5},{8,10},{9,11},{10,... | collective-permute-start | bytes 393224 | tf_op jit(solution)/shard_map/ppermute | solution.py:526
  62.3 7.7 %collective-permute-start.16 = (bf16[256,256]{1,0:T(8,128)(2,1)S(1)}, bf16[256,256]{1,0:T(8,128)(2,1)S(1)}, u32[]{:S(2)}, u32[]{:S(2)}) collective-permute-start(bf16[256,256]{1,0:T(8,128)(2,1)S(1)} %add_convert_fusion.3.refs_1_), channel_id=1, source_target_pairs={{0,1},{1,2},{2,3},{3,0},{4,5},{5,6},{6,7},{7,4},{8,9},{9,10},{10,1... | collective-permute-start | bytes 393224 | tf_op jit(solution)/shard_map/ppermute | solution.py:526
  63.4 9.1 %collective-permute-start.24 = (f32[48,128]{1,0:T(8,128)S(1)}, f32[48,128]{1,0:T(8,128)S(1)}, u32[]{:S(2)}, u32[]{:S(2)}) collective-permute-start(f32[48,128]{1,0:T(8,128)S(1)} %add_add_fusion.3.refs_2_), channel_id=1, source_target_pairs={{0,24},{4,28},{8,0},{12,4},{16,8},{20,12},{24,16},{28,20},{32,56},... | collective-permute-start | bytes 73736 | tf_op jit(solution)/shard_map/ppermute | solution.py:518
  65.2 7.3 %collective-permute-start.23 = (f32[48,128]{1,0:T(8,128)S(1)}, f32[48,128]{1,0:T(8,128)S(1)}, u32[]{:S(2)}, u32[]{:S(2)}) collective-permute-start(f32[48,128]{1,0:T(8,128)S(1)} %add_add_fusion.3.refs_2_), channel_id=1, source_target_pairs={{0,16},{4,20},{8,24},{12,28},{16,0},{20,4},{24,8},{28,12},{32,48},... | collective-permute-start | bytes 73736 | tf_op jit(solution)/shard_map/ppermute | solution.py:518
  73.3 7.9 %collective-permute-start.25 = (f32[48,128]{1,0:T(8,128)S(1)}, f32[48,128]{1,0:T(8,128)S(1)}, u32[]{:S(2)}, u32[]{:S(2)}) collective-permute-start(f32[48,128]{1,0:T(8,128)S(1)} %add_add_fusion.2.refs_1_), channel_id=1, source_target_pairs={{0,4},{4,0},{8,12},{12,8},{16,20},{20,16},{24,28},{28,24},{32,36},... | collective-permute-start | bytes 73736 | tf_op jit(solution)/shard_map/ppermute | solution.py:514
  86.9 11.7 %collective-permute-start.38 = (bf16[4,144,256]{2,1,0:T(8,128)(2,1)S(1)}, bf16[4,144,256]{2,1,0:T(8,128)(2,1)S(1)}, u32[]{:S(2)}, u32[]{:S(2)}) collective-permute-start(bf16[4,144,256]{2,1,0:T(8,128)(2,1)S(1)} %pad_maximum_fusion.refs_0_.refs_3_), channel_id=1, source_target_pairs={{0,24},{4,28},{8,0},{12,4},{16,8},{20,12},{24,16},{28,20},{32,56},... | collective-permute-start | bytes 884744 | tf_op jit(solution)/shard_map/ppermute | solution.py:518
  87.5 12.9 %collective-permute-start.37 = (bf16[4,144,256]{2,1,0:T(8,128)(2,1)S(1)}, bf16[4,144,256]{2,1,0:T(8,128)(2,1)S(1)}, u32[]{:S(2)}, u32[]{:S(2)}) collective-permute-start(bf16[4,144,256]{2,1,0:T(8,128)(2,1)S(1)} %pad_maximum_fusion.refs_0_.refs_3_), channel_id=1, source_target_pairs={{0,16},{4,20},{8,24},{12,28},{16,0},{20,4},{24,8},{28,12},{32,48},... | collective-permute-start | bytes 884744 | tf_op jit(solution)/shard_map/ppermute | solution.py:518
  88.7 15.6 %collective-permute-start.36 = (bf16[4,144,256]{2,1,0:T(8,128)(2,1)S(1)}, bf16[4,144,256]{2,1,0:T(8,128)(2,1)S(1)}, u32[]{:S(2)}, u32[]{:S(2)}) collective-permute-start(bf16[4,144,256]{2,1,0:T(8,128)(2,1)S(1)} %pad_maximum_fusion.refs_0_.refs_3_), channel_id=1, source_target_pairs={{0,8},{4,12},{8,16},{12,20},{16,24},{20,28},{24,0},{28,4},{32,40},... | collective-permute-start | bytes 884744 | tf_op jit(solution)/shard_map/ppermute | solution.py:518
  93.3 7.2 %collective-permute-start.27 = (bf16[128,512]{1,0:T(8,128)(2,1)S(1)}, bf16[128,512]{1,0:T(8,128)(2,1)S(1)}, u32[]{:S(2)}, u32[]{:S(2)}) collective-permute-start(bf16[128,512]{1,0:T(8,128)(2,1)S(1)} %add_convert_fusion.2), channel_id=1, source_target_pairs={{0,32},{4,36},{8,40},{12,44},{16,48},{20,52},{24,56},{28,60},{32,6... | collective-permute-start | bytes 393224 | tf_op jit(solution)/shard_map/ppermute | solution.py:522
  94.9 10.4 %collective-permute-start.39 = (bf16[4,144,256]{2,1,0:T(8,128)(2,1)S(1)}, bf16[4,144,256]{2,1,0:T(8,128)(2,1)S(1)}, u32[]{:S(2)}, u32[]{:S(2)}) collective-permute-start(bf16[4,144,256]{2,1,0:T(8,128)(2,1)S(1)} %pad_maximum_fusion.refs_0_.refs_3_), channel_id=1, source_target_pairs={{0,4},{4,0},{8,12},{12,8},{16,20},{20,16},{24,28},{28,24},{32,36},... | collective-permute-start | bytes 884744 | tf_op jit(solution)/shard_map/ppermute | solution.py:514
  98.6 7.9 %collective-permute-start.42 = (bf16[4,144,256]{2,1,0:T(8,128)(2,1)S(1)}, bf16[4,144,256]{2,1,0:T(8,128)(2,1)S(1)}, u32[]{:S(2)}, u32[]{:S(2)}) collective-permute-start(bf16[4,144,256]{2,1,0:T(8,128)(2,1)S(1)} %collective-permute-done.38.refs_3_.refs_6_), channel_id=1, source_target_pairs={{0,4},{4,0},{8,12},{12,8},{16,20},{20,16},{24,28},{28,24},{32,36},... | collective-permute-start | bytes 884744 | tf_op jit(solution)/shard_map/ppermute | solution.py:514
  104.9 6.8 %collective-permute-start.32 = (bf16[128,512]{1,0:T(8,128)(2,1)S(1)}, bf16[128,512]{1,0:T(8,128)(2,1)S(1)}, u32[]{:S(2)}, u32[]{:S(2)}) collective-permute-start(bf16[128,512]{1,0:T(8,128)(2,1)S(1)} %add_convert_fusion.1), channel_id=1, source_target_pairs={{0,24},{4,28},{8,0},{12,4},{16,8},{20,12},{24,16},{28,20},{32,56},... | collective-permute-start | bytes 393224 | tf_op jit(solution)/shard_map/ppermute | solution.py:518
  106.4 8.6 %collective-permute-start.30 = (bf16[128,512]{1,0:T(8,128)(2,1)S(1)}, bf16[128,512]{1,0:T(8,128)(2,1)S(1)}, u32[]{:S(2)}, u32[]{:S(2)}) collective-permute-start(bf16[128,512]{1,0:T(8,128)(2,1)S(1)} %add_convert_fusion.1), channel_id=1, source_target_pairs={{0,8},{4,12},{8,16},{12,20},{16,24},{20,28},{24,0},{28,4},{32,40},... | collective-permute-start | bytes 393224 | tf_op jit(solution)/shard_map/ppermute | solution.py:518
  (30 other events, 230.1 us)

commit v6 on v5

--- a/solution.py
+++ b/solution.py
@@ -137,12 +137,13 @@
     total = every_ref[0].astype(F32)
     for k in range(1, 16):
         total = total + every_ref[k].astype(F32)
-    out_ref[...] = total.astype(out_ref.dtype)
+    total = total.astype(out_ref.dtype)
+    for k in range(16):
+        out_ref[k] = total
 
 
 def chips_call(at, every, after=()):
-    out = struct(every.shape[1:], every.dtype)
-    return call(chips_kernel, (out,), 1e6, 1e6, "experts_sum", after=after)(at, every)[0]
+    return call(chips_kernel, (struct(every.shape, every.dtype),), 1e6, 1e6, "experts_sum", after=after)(at, every)[0]
 
 
 def keys_values(tokt, keep, wk, wv):
@@ -153,9 +154,14 @@
     return km, val, keep * jnp.where(kpre > 0, 1.0, low)
 
 
-def keys_kernel(at_ref, tok_ref, keep_ref, coords_ref, wk_ref, wv_ref, ck_ref, msg_ref, keep_m, send_m, km_buf):
+def keys_kernel(
+    at_ref, tok_ref, keep_ref, coords_ref, wk_ref, wv_ref, wq_ref,
+    ck_ref, msg_ref, keep_m, send_m, tokt_ref, wqt_ref, km_buf,
+):
     core = at_ref[0]
     tokt = flip(tok_ref[...]).astype(BF)
+    tokt_ref[...] = tokt
+    wqt_ref[...] = flip(wq_ref[...]).astype(BF)
     keep = keep_ref[...].astype(F32)
     ck_ref[0:3, :] = coords_ref[...]
     ck_ref[3:4, :] = keep
@@ -171,12 +177,15 @@
         ref[...] = mm_nt(tokt, km_buf[rows, :]).astype(BF)
 
 
-def keys_call(at, tokens, keep_row, coords, wk, wv):
+def keys_call(at, tokens, keep_row, coords, wk, wv, wq):
     return call(
         keys_kernel,
-        (struct((4, N1), F32), struct((80, 128), F32), struct((D, 128), BF), struct((D, 128), BF)),
-        4e8, 3e6, "keys", [pltpu.VMEM((D, N1), BF)], fetch=5,
-    )(at, tokens, keep_row, coords, wk, wv)
+        (
+            struct((4, N1), F32), struct((80, 128), F32), struct((D, 128), BF), struct((D, 128), BF),
+            struct((D, N1), BF), struct((D, D), BF),
+        ),
+        4e8, 3e6, "keys", [pltpu.VMEM((D, N1), BF)], fetch=6,
+    )(at, tokens, keep_row, coords, wk, wv, wq)
 
 
 def again_kernel(at_ref, tok_ref, keep_ref, wq_ref, wk_ref, wv_ref, tokt_ref, q_ref, qslope_ref, km_ref, v_ref, slope_ref):
@@ -200,16 +209,28 @@
     )(at, tokens, keep_row, wq, wk, wv)
 
 
-def query_kernel(at_ref, tok_ref, wq_ref, tokt_ref, q_ref):
+def query_of(tokt, wqt):
+    pre = mm(wqt, tokt)
+    return jnp.where(pre > 0, pre + 1.0, jnp.exp(jnp.minimum(pre, 0.0))).astype(BF)
+
+
+def query_kernel(at_ref, tokt_ref, wqt_ref, q_ref):
+    q_ref[...] = query_of(tokt_ref[...], wqt_ref[...])
+
+
+def query_other_kernel(at_ref, tok_ref, wqt_ref, tokt_ref, q_ref):
     tokt = flip(tok_ref[...]).astype(BF)
     tokt_ref[...] = tokt
-    pre = mm(flip(wq_ref[...]).astype(BF), tokt)
-    q_ref[...] = jnp.where(pre > 0, pre + 1.0, jnp.exp(jnp.minimum(pre, 0.0))).astype(BF)
-
-
-def query_call(at, tokens, wq, name):
+    q_ref[...] = query_of(tokt, wqt_ref[...])
+
+
+def query_call(at, tokt, wqt):
+    return call(query_kernel, (struct((D, N1), BF),), 2e8, 2e6, "queries")(at, tokt, wqt)[0]
+
+
+def query_other_call(at, tokens, wqt):
     out = (struct((D, N1), BF), struct((D, N1), BF))
-    return call(query_kernel, out, 2e8, 2e6, name, fetch=2)(at, tokens, wq)
+    return call(query_other_kernel, out, 2e8, 2e6, "queries_other")(at, tokens, wqt)
 
 
 def gate_kernel(at_ref, wgeo_ref, bgeo_ref, wroute_ref, ck_ref, cko_ref, r_ref, g_ref):
@@ -221,14 +242,14 @@
         for k in range(3):
             pre = pre + geo[k] * ref[k : k + 1, :]
         r = jnp.tanh(pre)
-        r_ref[:, cols] = r
+        r_ref[0:64, cols], r_ref[64:128, cols] = split2(r)
         logit = jnp.dot(wroute_ref[...], r, precision=lax.Precision.HIGHEST, preferred_element_type=F32)
         expo = jnp.exp(logit)
         g_ref[:, cols] = expo / jnp.sum(expo, axis=0, keepdims=True)
 
 
 def gate_call(at, wgeo, bgeo, wroute, ck, ck_o):
-    out = (struct((64, N2), F32), struct((8, N2), F32))
+    out = (struct((128, N2), BF), struct((8, N2), F32))
     return call(gate_kernel, out, 1e8, 1e6, "gate", fetch=3)(at, wgeo, bgeo, wroute, ck, ck_o)
 
 
@@ -308,9 +329,9 @@
         dden = -jnp.sum((dnum * attn).reshape(8, HD, TB), axis=1)
         lhs = jnp.concatenate([*split2(dnum), *split2(jnp.concatenate([dden, dden], axis=0))], axis=0)
         dkv_part = mm_nt(lhs, q)
-        route_part = lax.dot_general(
-            turn, r_ref[:, cols], (((1,), (1,)), ((), ())), precision=lax.Precision.HIGHEST, preferred_element_type=F32
-        )
+        hi, lo = split2(jnp.concatenate([turn, turn], axis=0))
+        both = mm_nt(jnp.concatenate([hi, lo], axis=0), r_ref[:, cols])
+        route_part = both[0:8, 0:64] + (both[0:8, 64:128] + both[16:24, 0:64])
         dkv[...] = dkv_part if first else dkv[...] + dkv_part
         route[...] = route_part if first else route[...] + route_part
         for k in range(TB // 512):
@@ -437,55 +458,44 @@
     return call(grad_x_kernel, (struct((N1, D), BF),), 3e8, 3e6, "grad_x")(at, gx, dk, dv, wk, wv)[0]
 
 
-def origin(at_ref, dx, dz):
-    return lax.rem(at_ref[4] + 4 - dz, 4) * 4 + lax.rem(at_ref[3] + 4 - dx, 4)
-
-
-def place_kernel(at_ref, *refs):
-    ins, (gin_ref, gout_ref, buf) = refs[:8], refs[8:]
-
-    def put(side):
-        for dx in range(4):
-            for dz in range(4):
-                rows = pl.ds(pl.multiple_of(origin(at_ref, dx, dz) * 64, 64), 64)
-                buf[rows, :] = ins[4 * side + dx][dz, 0:64, :].astype(F32)
-                gout_ref[0, rows, :] = ins[4 * side + dx][dz, 64:128, :].astype(F32)
-        for j in range(0, FH, 256):
-            gin_ref[0, :, j : j + 256] = buf[j : j + 256, :].T
-
-    for side in range(2):
-        pl.when(pl.program_id(0) == side)(lambda side=side: put(side))
-
-
-def place_call(at, pieces):
-    expert = lambda i, at: (jnp.where(i == 0, at[0], 1 - at[0]), 0, 0)
+def place_kernel(at_ref, own_ref, oth_ref, gin_ref, gout_ref):
+    def put(ref, part):
+        cols = slice(128 * part, 128 * part + 128)
+        gin_ref[0] = jnp.concatenate([ref[k, 0:64, cols].astype(F32) for k in range(16)], axis=0).T
+        for k in range(8):
+            gout_ref[0, 64 * k : 64 * k + 64, :] = ref[8 * part + k, 64:128, :].astype(F32)
+
+    step = pl.program_id(0)
+    for s in range(4):
+        pl.when(step == s)(lambda s=s: put(own_ref if s < 2 else oth_ref, s % 2))
+
+
+def place_call(at, own, oth):
+    expert = lambda i, at: jnp.where(i < 2, at[0], 1 - at[0])
+    out = pl.BlockSpec((1, 128, FH), lambda i, at: (expert(i, at), lax.rem(i, 2), 0))
+    out2 = pl.BlockSpec((1, 512, D), lambda i, at: (expert(i, at), lax.rem(i, 2), 0))
     return pl.pallas_call(
         place_kernel,
         grid_spec=pltpu.PrefetchScalarGridSpec(
             num_scalar_prefetch=1,
-            grid=(2,),
-            in_specs=[pl.BlockSpec(memory_space=pltpu.VMEM)] * 8,
-            out_specs=[pl.BlockSpec((1, D, FH), expert), pl.BlockSpec((1, FH, D), expert)],
-            scratch_shapes=[pltpu.VMEM((FH, D), F32)],
+            grid=(4,),
+            in_specs=[pl.BlockSpec(memory_space=pltpu.VMEM)] * 2,
+            out_specs=[out, out2],
         ),
         out_shape=(struct((2, D, FH), F32), struct((2, FH, D), F32)),
-        compiler_params=pltpu.CompilerParams(vmem_limit_bytes=16 * 1024 * 1024),
+        compiler_params=pltpu.CompilerParams(vmem_limit_bytes=32 * 1024 * 1024),
         cost_estimate=pl.CostEstimate(flops=1000000, bytes_accessed=7000000, transcendentals=0),
         name="place_experts",
-    )(at, *pieces)
-
-
-def place_m_kernel(at_ref, msg_ref, msgo_ref, *refs):
-    ins, (gv_ref, route_ref, buf) = refs[:8], refs[8:]
+    )(at, own, oth)
+
+
+def place_m_kernel(at_ref, msg_ref, msgo_ref, own_ref, oth_ref, gv_ref, route_ref):
     core, y = at_ref[0], at_ref[2]
     halves = ordered(core, msg_ref[...], msgo_ref[...])
     hi, lo = split2(heads_of(halves).T)
-    for side in range(2):
-        for dx in range(4):
-            for dz in range(4):
-                rows = pl.ds(pl.multiple_of(origin(at_ref, dx, dz) * 16, 16), 16)
-                buf[side, rows, :] = ins[4 * side + dx][dz, 128:144, 0:128]
-    m = jnp.concatenate(ordered(core, buf[0], buf[1]), axis=1)
+    own = jnp.concatenate([own_ref[k, 128:144, 0:128].astype(F32) for k in range(16)], axis=0)
+    oth = jnp.concatenate([oth_ref[k, 128:144, 0:128].astype(F32) for k in range(16)], axis=0)
+    m = jnp.concatenate(ordered(core, own, oth), axis=1).astype(BF)
     gv_ref[...] = mm(m, hi) + mm(m, lo)
     sums = halves[0][40:48, 0:64]
     at_row = lax.broadcasted_iota(jnp.int32, sums.shape, 0)
@@ -493,9 +503,9 @@
         route_ref[e : e + 1, :] = jnp.sum(jnp.where(at_row == 2 * y + e, sums, 0.0), axis=0, keepdims=True)
 
 
-def place_m_call(at, msg, msg_o, pieces):
+def place_m_call(at, msg, msg_o, own, oth):
     out = (struct((D, D), F32), struct((2, 64), F32))
-    return call(place_m_kernel, out, 1e8, 1e6, "grad_wv", [pltpu.VMEM((2, D, 128), BF)])(at, msg, msg_o, *pieces)
+    return call(place_m_kernel, out, 1e8, 1e6, "grad_wv")(at, msg, msg_o, own, oth)
 
 
 def place_proj_kernel(at_ref, own_ref, oth_ref, gq_ref, gk_ref):
@@ -543,13 +553,13 @@
     pts = lax.axis_index("pts")
     y = lax.axis_index("exp")
     core = pts % 2
-    at = jnp.stack([core, 2 * y + core, y, (pts // 2) % 4, pts // 8]).astype(jnp.int32)
+    at = jnp.stack([core, 2 * y + core, y]).astype(jnp.int32)
 
     tokens_o, cot_o = swap_core(tokens), swap_core(cotangent)
-    ck, msg, m, m_away = keys_call(at, tokens, keep[None, :], coords, w_key, w_value)
+    ck, msg, m, m_away, tokt, wqt = keys_call(at, tokens, keep[None, :], coords, w_key, w_value, w_query)
     ck_o, m_o = swap_core(ck), swap_core(m_away)
-    tokt, q = query_call(at, tokens, w_query, "queries")
-    tokt_o, q_o = query_call(at, tokens_o, w_query, "queries_other")
+    q = query_call(at, tokt, wqt)
+    tokt_o, q_o = query_other_call(at, tokens_o, wqt)
     r, g = gate_call(at, w_geo, b_geo[None, :], w_route.T, ck, ck_o)
     dy, df, back, wint = back_call(at, cotangent, cot_o, ck, ck_o, g, w_in, w_out)
 
@@ -570,22 +580,23 @@
     msg2 = msg2_z = add([msg2] + star(msg2, to_z), (), F32)
 
     pieces = chips_call(at, pieces, (msg2_z,))
-
+    around = star(msg2, to_x)
+    pieces, *around = lax.optimization_barrier((pieces, *around))
     tokt, q, qslope, km, v, slope = again_call(at, tokens, keep[None, :], w_query, w_key, w_value, (pieces,))
+    pieces = exchange(pieces)
+
     gx, gq = back_query_call(at, dm, kvt, ks, tokt, q, qslope, w_query, ())
-    msg2 = add([msg2] + star(msg2, to_x), (gq,), F32)
+    msg2 = add([msg2] + around, (), F32)
     msg2_o = swap_core(msg2)
     dk, dv, part, away = back_keys_call(at, msg2, msg2_o, km, v, slope, tokt, gq)
-
-    pieces = jnp.stack([pieces] + star(pieces, to_z))
-    pieces = [pieces] + star(pieces, to_x)
-    pieces = pieces + [swap_core(piece) for piece in pieces]
     grad_x = grad_x_call(at, gx, dk, dv, w_key, w_value)
-    grad_w_in, grad_w_out = place_call(at, pieces)
-    grad_wv, grad_route = place_m_call(at, msg2, msg2_o, pieces)
 
     part = add([part, swap_core(away)])
     part = add([part] + star(part, to_z), (grad_x,))
+    pieces, _ = lax.optimization_barrier((pieces, part))
+    pieces_o = swap_core(pieces)
+    grad_w_in, grad_w_out = place_call(at, pieces, pieces_o)
+    grad_wv, grad_route = place_m_call(at, msg2, msg2_o, pieces, pieces_o)
     part = add([part] + star(part, to_x), (grad_w_in, grad_wv))
     grad_wq, grad_wk = place_proj_call(at, part, swap_core(part))
     return (grad_x, grad_wq, grad_wk, grad_wv, grad_w_in, grad_w_out, grad_route.T)

time: 118 us -> 117 us (level)
  starting transfers between devices: 54.6 us -> 52.1 us
  waiting for transfers between devices: 23.2 us -> 25.2 us
  Pallas kernels: 38.2 us -> 36.9 us
    ppermute x14 -> x11, starting transfers between devices: 17.3 us -> 12.6 us  [swap_core(): return lax.ppermute(v, 'pts', [(i, i ^ 1) for i in range(32)])]
    all_to_all x1 -> x2, starting transfers between devices: 4.85 us -> 8.37 us  [exchange(): return lax.all_to_all(v, 'pts', 0, 0, axis_index_groups=CHIPS)]
    ppermute x12 -> x9, waiting for transfers between devices: 8.5 us -> 11.2 us  [to_z(): return lax.ppermute(v, 'pts', [(i, (i + 8 * d) % 32) for i in range(32)])]
    ppermute x12 -> x9, waiting for transfers between devices: 5.8 us -> 3.85 us  [to_x(): lax.ppermute(v, 'pts', [(i, i & ~6 | i + 2 * d & 6) for i in range(32)])]
    pallas_call x14, Pallas kernels: 35.1 us -> 33.7 us  [run(): pl.pallas_call(body, in_specs=[pl.BlockSpec(memory_space=pltpu.SMEM)] + [...]
    ppermute x14 -> x11, waiting for transfers between devices: 2.7 us -> 4.02 us  [swap_core(): return lax.ppermute(v, 'pts', [(i, i ^ 1) for i in range(32)])]
    ppermute x12 -> x9, starting transfers between devices: 13.2 us -> 12.5 us  [to_z(): return lax.ppermute(v, 'pts', [(i, (i + 8 * d) % 32) for i in range(32)])]
    ppermute x12 -> x9, starting transfers between devices: 10.9 us -> 10.3 us  [to_x(): lax.ppermute(v, 'pts', [(i, i & ~6 | i + 2 * d & 6) for i in range(32)])]
  transfers between devices with their start and end apart: 45 -> 37, of which waited for: 13 -> 14; matrix products, arithmetic and copies ran while one was open for 0% -> 0% of each run, Pallas kernels for 22% -> 21%
where the time goes in v6:
time: 117 us; the launch traced here: 116 us
  starting transfers between devices  52.1 us (45%)
  Pallas kernels  36.9 us (32%)
  waiting for transfers between devices  25.2 us (22%)
    pallas_call x14, Pallas kernels, run(): pl.pallas_call(body, in_specs=[pl.BlockSpec(memory_space=pltpu.SMEM)] + [...  33.7 us
    ppermute x11, starting transfers between devices, swap_core(): return lax.ppermute(v, 'pts', [(i, i ^ 1) for i in range(32)])  12.6 us
    ppermute x9, starting transfers between devices, to_z(): return lax.ppermute(v, 'pts', [(i, (i + 8 * d) % 32) for i in range(32)])  12.5 us
    ppermute x9, waiting for transfers between devices, to_z(): return lax.ppermute(v, 'pts', [(i, (i + 8 * d) % 32) for i in range(32)])  11.2 us
    ppermute x9, starting transfers between devices, to_x(): lax.ppermute(v, 'pts', [(i, i & ~6 | i + 2 * d & 6) for i in range(32)])  10.3 us
    ppermute x6, starting transfers between devices, to_y(): return lax.ppermute(v, 'exp', [(i, (i + d) % 4) for i in range(4)])  8.44 us
    all_to_all x2, starting transfers between devices, exchange(): return lax.all_to_all(v, 'pts', 0, 0, axis_index_groups=CHIPS)  8.37 us
    ppermute x6, waiting for transfers between devices, to_y(): return lax.ppermute(v, 'exp', [(i, (i + d) % 4) for i in range(4)])  6.15 us
  transfers between devices with their start and end apart: 37, of which 14 were waited for; matrix products, arithmetic and copies ran while one was open for 0% of the time, Pallas kernels for 21%

profile of v6, /device:TPU:1, one launch (start us, length us, event | category | flops | bytes accessed | tf_op | source)
XLA Modules:
  0.0 116.3 jit_solution(7489624107889616592)
XLA Ops:
  2.3 3.0 %keys.1 = (f32[4,1024]{1,0:T(4,128)S(1)}, f32[80,128]{1,0:T(8,128)S(1)}, bf16[256,128]{1,0:T(8,128)(2,1)S(1)}, bf16[256,128]{1,0:T(8,128)(2,1)S(1)}, bf16[256,10...) custom-call(s32[3]{0:T(128)S(1)} %pad_add_fusion.refs_0_.at_ref, bf16[1024,256]{1,0:T(8,128)(2,1)} %refs_1_.7, ...), custom_call_target="tpu_custom_call" | custom-call | flops 400000000 | bytes 3000000 | tf_op jit(solution)/shard_map/keys/pallas_call | solution.py:106
  6.7 2.6 %collective-permute-start.3 = (f32[80,128]{1,0:T(8,128)S(1)}, f32[80,128]{1,0:T(8,128)S(1)}, u32[]{:S(2)}, u32[]{:S(2)}) collective-permute-start(f32[80,128]{1,0:T(8,128)S(1)} %add.99), channel_id=1, source_target_pairs={{0,24},{4,28},{8,0},{12,4},{16,8},{20,12},{24,16},{28,20},{32,56},... | collective-permute-start | bytes 122888 | tf_op jit(solution)/shard_map/ppermute | solution.py:528
  11.3 1.9 %gate.1 = (bf16[128,2048]{1,0:T(8,128)(2,1)S(1)}, f32[8,2048]{1,0:T(8,128)S(1)}) custom-call(s32[3]{0:T(128)S(1)} %pad_add_fusion.refs_0_.at_ref, f32[3,64]{1,0:T(4,128)} %refs_1_.5, f32[1,64]{1,0:T(1,128)} %bitcast.11, f32[8,64]{1,0:T(8,128)} %bitcast.9, f32[4,1024]{1,0:T(4,128)S(1)} %get-tuple-element.74.refs_4_.refs_3_, ...), custom_call_target="tpu_custom_call" | custom-call | flops 100000000 | bytes 1000000 | tf_op jit(solution)/shard_map/gate/pallas_call | solution.py:106
  14.5 3.8 %collective-permute-start.7 = (f32[80,128]{1,0:T(8,128)S(1)}, f32[80,128]{1,0:T(8,128)S(1)}, u32[]{:S(2)}, u32[]{:S(2)}) collective-permute-start(f32[80,128]{1,0:T(8,128)S(1)} %add_add_fusion.1), channel_id=1, source_target_pairs={{0,96},{4,100},{8,104},{12,108},{16,112},{20,116},{24,120},{28,124... | collective-permute-start | bytes 122888 | tf_op jit(solution)/shard_map/ppermute | solution.py:532
  19.1 2.1 %cotangent_back.1 = (bf16[256,1024]{1,0:T(8,128)(2,1)S(1)}, bf16[256,2048]{1,0:T(8,128)(2,1)S(1)}, f32[1024,2048]{1,0:T(8,128)S(1)}, bf16[1024,256]{1,0:T(8,128)(2,1)S(1)}) custom-call(s32[3]{0:T(128)S(1)} %pad_add_fusion.refs_0_.at_ref, bf16[1024,256]{1,0:T(8,128)(2,1)S(1)} %copy-done.5, bf16[1024,256]{1,0:T(8,128)(2,1)S(1)} %collective-permute-done.8.refs_2_, ...), custom_call_target="tpu_custom_call" | custom-call | flops 1100000000 | bytes 8000000 | tf_op jit(solution)/shard_map/cotangent_back/pallas_call | solution.py:106
  22.9 10.6 %expert.1 = (f32[256,1024]{1,0:T(8,128)S(1)}, bf16[256,1024]{1,0:T(8,128)(2,1)S(1)}, f32[256,256]{1,0:T(8,128)S(1)}, f32[8,256]{1,0:T(8,128)S(1)}, f32[48,128]{1...) custom-call(s32[3]{0:T(128)S(1)} %pad_add_fusion.refs_0_.at_ref, ...), custom_call_target="tpu_custom_call" | custom-call | flops 6000000000 | bytes 12000000 | tf_op jit(solution)/shard_map/expert/pallas_call | solution.py:106
  34.2 2.8 %collective-permute-start.11 = (bf16[256,1024]{1,0:T(8,128)(2,1)S(1)}, bf16[256,1024]{1,0:T(8,128)(2,1)S(1)}, u32[]{:S(2)}, u32[]{:S(2)}) collective-permute-start(bf16[256,1024]{1,0:T(8,128)(2,1)S(1)} %get-tuple-element.94), channel_id=1, source_target_pairs={{0,4},{4,0},{8,12},{12,8},{16,20},{20,16},{24,28},{28,24},{32,36},... | collective-permute-start | bytes 1572872 | tf_op jit(solution)/shard_map/ppermute | solution.py:524
  37.0 3.9 %all-to-all-start = ((bf16[16,144,256]{2,1,0:T(8,128)(2,1)}), bf16[16,144,256]{2,1,0:T(8,128)(2,1)S(1)}, u32[]{:S(2)}, u32[]{:S(2)}) async-start(bf16[16,144,256]{2,1,0:T(8,128)(2,1)} %get-tuple-element.103), calls=%async_computation | async-start | bytes 2359296 | tf_op jit(solution)/shard_map/all_to_all | solution.py:547
  44.3 2.6 %collective-permute-start.14 = (bf16[304,256]{1,0:T(8,128)(2,1)S(1)}, bf16[304,256]{1,0:T(8,128)(2,1)S(1)}, u32[]{:S(2)}, u32[]{:S(2)}) collective-permute-start(bf16[304,256]{1,0:T(8,128)(2,1)S(1)} %get-tuple-element.99), channel_id=1, source_target_pairs={{0,2},{1,3},{2,0},{3,1},{4,6},{5,7},{6,4},{7,5},{8,10},{9,11},{10,... | collective-permute-start | bytes 466952 | tf_op jit(solution)/shard_map/ppermute | solution.py:536
  49.6 4.4 %collective-permute-done.14 = bf16[304,256]{1,0:T(8,128)(2,1)S(1)} collective-permute-done((bf16[304,256]{1,0:T(8,128)(2,1)S(1)}, bf16[304,256]{1,0:T(8,128)(2,1)S(1)}, u32[]{:S(2)}, u32[]{:S(2)}) %collective-permute-start.14) | collective-permute-done | bytes 155680 | tf_op jit(solution)/shard_map/ppermute | solution.py:536
  54.1 2.7 %collective-permute-start.21 = (f32[48,128]{1,0:T(8,128)S(1)}, f32[48,128]{1,0:T(8,128)S(1)}, u32[]{:S(2)}, u32[]{:S(2)}) collective-permute-start(f32[48,128]{1,0:T(8,128)S(1)} %convert_add_fusion), channel_id=1, source_target_pairs={{0,96},{4,100},{8,104},{12,108},{16,112},{20,116},{24,120},{28,124... | collective-permute-start | bytes 73736 | tf_op jit(solution)/shard_map/ppermute | solution.py:532
  58.0 3.5 %collective-permute-done.20 = f32[48,128]{1,0:T(8,128)S(1)} collective-permute-done((f32[48,128]{1,0:T(8,128)S(1)}, f32[48,128]{1,0:T(8,128)S(1)}, u32[]{:S(2)}, u32[]{:S(2)}) %collective-permute-start.20) | collective-permute-done | bytes 24608 | tf_op jit(solution)/shard_map/ppermute | solution.py:532
  61.8 2.0 %collective-permute-start.24 = (f32[48,128]{1,0:T(8,128)S(1)}, f32[48,128]{1,0:T(8,128)S(1)}, u32[]{:S(2)}, u32[]{:S(2)}) collective-permute-start(f32[48,128]{1,0:T(8,128)S(1)} %add_add_fusion.3.refs_2_), channel_id=1, source_target_pairs={{0,24},{4,28},{8,0},{12,4},{16,8},{20,12},{24,16},{28,20},{32,56},... | collective-permute-start | bytes 73736 | tf_op jit(solution)/shard_map/ppermute | solution.py:528
  65.0 2.7 %collective-permute-start.18 = (bf16[256,256]{1,0:T(8,128)(2,1)S(1)}, bf16[256,256]{1,0:T(8,128)(2,1)S(1)}, u32[]{:S(2)}, u32[]{:S(2)}) collective-permute-start(bf16[256,256]{1,0:T(8,128)(2,1)S(1)} %add_convert_fusion.3.refs_1_), channel_id=1, source_target_pairs={{0,3},{1,0},{2,1},{3,2},{4,7},{5,4},{6,5},{7,6},{8,11},{9,8},{10,9... | collective-permute-start | bytes 393224 | tf_op jit(solution)/shard_map/ppermute | solution.py:536
  70.1 4.4 %all-to-all-start.1 = ((bf16[16,144,256]{2,1,0:T(8,128)(2,1)}), bf16[16,144,256]{2,1,0:T(8,128)(2,1)S(1)}, u32[]{:S(2)}, u32[]{:S(2)}) async-start(bf16[16,144,256]{2,1,0:T(8,128)(2,1)} %experts_sum.1.refs_6_), calls=%async_computation.1 | async-start | bytes 2359296 | tf_op jit(solution)/shard_map/all_to_all | solution.py:547
  74.6 4.7 %collective-permute-start.25 = (f32[48,128]{1,0:T(8,128)S(1)}, f32[48,128]{1,0:T(8,128)S(1)}, u32[]{:S(2)}, u32[]{:S(2)}) collective-permute-start(f32[48,128]{1,0:T(8,128)S(1)} %add_add_fusion.2.refs_1_), channel_id=1, source_target_pairs={{0,4},{4,0},{8,12},{12,8},{16,20},{20,16},{24,28},{28,24},{32,36},... | collective-permute-start | bytes 73736 | tf_op jit(solution)/shard_map/ppermute | solution.py:524
  79.3 2.8 %queries_keys_again.1 = (bf16[256,1024]{1,0:T(8,128)(2,1)S(1)}, bf16[256,1024]{1,0:T(8,128)(2,1)S(1)}, f32[256,1024]{1,0:T(8,128)S(1)}, bf16[256,1024]{1,0:T(8,1...) custom-call(s32[3]{0:T(128)S(1)} %pad_add_fusion.refs_0_.at_ref, bf16[1024,256]{1,0:T(8,128)(2,1)} %refs_1_.7, ...), custom_call_target="tpu_custom_call" | custom-call | flops 500000000 | bytes 3000000 | tf_op jit(solution)/shard_map/queries_keys_again/pallas_call | solution.py:106
  82.2 2.5 %back_query.1 = (f32[256,1024]{1,0:T(8,128)S(1)}, f32[256,256]{1,0:T(8,128)S(1)}) custom-call(s32[3]{0:T(128)S(1)} %pad_add_fusion.refs_0_.at_ref, bf16[256,256]{1,0:T(8,128)(2,1)S(1)} %add_convert_fusion.3.refs_1_, bf16[256,256]{1,0:T(8,128)(2,1)S(1)} %collective-permute-done.16.refs_2_, bf16[256,256]{1,0:T(8,128)(2,1)S(1)} %collective-permute-done.17.refs_3_, ...), custom_call_target="tpu_custom_call" | custom-call | flops 2000000000 | bytes 5000000 | tf_op jit(solution)/shard_map/back_query/pallas_call | solution.py:106
  87.8 2.9 %collective-permute-start.29 = (bf16[128,512]{1,0:T(8,128)(2,1)S(1)}, bf16[128,512]{1,0:T(8,128)(2,1)S(1)}, u32[]{:S(2)}, u32[]{:S(2)}) collective-permute-start(bf16[128,512]{1,0:T(8,128)(2,1)S(1)} %add_convert_fusion.2), channel_id=1, source_target_pairs={{0,96},{4,100},{8,104},{12,108},{16,112},{20,116},{24,120},{28,124... | collective-permute-start | bytes 393224 | tf_op jit(solution)/shard_map/ppermute | solution.py:532
  94.0 3.1 %collective-permute-done.28 = bf16[128,512]{1,0:T(8,128)(2,1)S(1)} collective-permute-done((bf16[128,512]{1,0:T(8,128)(2,1)S(1)}, bf16[128,512]{1,0:T(8,128)(2,1)S(1)}, u32[]{:S(2)}, u32[]{:S(2)}) %collective-permute-start.28) | collective-permute-done | bytes 131104 | tf_op jit(solution)/shard_map/ppermute | solution.py:532
  97.2 3.4 %collective-permute-done.27 = bf16[128,512]{1,0:T(8,128)(2,1)S(1)} collective-permute-done((bf16[128,512]{1,0:T(8,128)(2,1)S(1)}, bf16[128,512]{1,0:T(8,128)(2,1)S(1)}, u32[]{:S(2)}, u32[]{:S(2)}) %collective-permute-start.27) | collective-permute-done | bytes 131104 | tf_op jit(solution)/shard_map/ppermute | solution.py:532
  101.2 2.3 %collective-permute-start.32 = (bf16[128,512]{1,0:T(8,128)(2,1)S(1)}, bf16[128,512]{1,0:T(8,128)(2,1)S(1)}, u32[]{:S(2)}, u32[]{:S(2)}) collective-permute-start(bf16[128,512]{1,0:T(8,128)(2,1)S(1)} %add_convert_fusion.1), channel_id=1, source_target_pairs={{0,24},{4,28},{8,0},{12,4},{16,8},{20,12},{24,16},{28,20},{32,56},... | collective-permute-start | bytes 393224 | tf_op jit(solution)/shard_map/ppermute | solution.py:528
  104.7 3.2 %place_experts.1 = (f32[2,256,1024]{2,1,0:T(8,128)}, f32[2,1024,256]{2,1,0:T(8,128)}) custom-call(s32[3]{0:T(128)S(1)} %pad_add_fusion.refs_0_.at_ref, bf16[16,144,256]{2,1,0:T(8,128)(2,1)S(1)} %all-to-all-done.1.own_ref.refs_3_, bf16[16,144,256]{2,1,0:T(8,128)(2,1)S(1)} %collective-permute-done.33.oth_ref.refs_4_), custom_call_target="tpu_custom_call" | custom-call | flops 1000000 | bytes 7000000 | tf_op jit(solution)/shard_map/place_experts/pallas_call | solution.py:477
  109.8 3.5 %collective-permute-done.30 = bf16[128,512]{1,0:T(8,128)(2,1)S(1)} collective-permute-done((bf16[128,512]{1,0:T(8,128)(2,1)S(1)}, bf16[128,512]{1,0:T(8,128)(2,1)S(1)}, u32[]{:S(2)}, u32[]{:S(2)}) %collective-permute-start.30) | collective-permute-done | bytes 131104 | tf_op jit(solution)/shard_map/ppermute | solution.py:528
  (92 shorter events, 33.8 us)
Async XLA Ops:
  0.6 17.7 %collective-permute-start.8 = (bf16[1024,256]{1,0:T(8,128)(2,1)}, bf16[1024,256]{1,0:T(8,128)(2,1)S(1)}, u32[]{:S(2)}, u32[]{:S(2)}) collective-permute-start(bf16[1024,256]{1,0:T(8,128)(2,1)} %refs_1_.6), channel_id=1, source_target_pairs={{0,4},{4,0},{8,12},{12,8},{16,20},{20,16},{24,28},{28,24},{32,36},... | collective-permute-start | bytes 1572872 | tf_op jit(solution)/shard_map/ppermute | solution.py:524
  2.1 19.1 %collective-permute-start.9 = (bf16[1024,256]{1,0:T(8,128)(2,1)}, bf16[1024,256]{1,0:T(8,128)(2,1)S(1)}, u32[]{:S(2)}, u32[]{:S(2)}) collective-permute-start(bf16[1024,256]{1,0:T(8,128)(2,1)} %refs_1_.7), channel_id=1, source_target_pairs={{0,4},{4,0},{8,12},{12,8},{16,20},{20,16},{24,28},{28,24},{32,36},... | collective-permute-start | bytes 1572872 | tf_op jit(solution)/shard_map/ppermute | solution.py:524
  6.7 6.6 %collective-permute-start.3 = (f32[80,128]{1,0:T(8,128)S(1)}, f32[80,128]{1,0:T(8,128)S(1)}, u32[]{:S(2)}, u32[]{:S(2)}) collective-permute-start(f32[80,128]{1,0:T(8,128)S(1)} %add.99), channel_id=1, source_target_pairs={{0,24},{4,28},{8,0},{12,4},{16,8},{20,12},{24,16},{28,20},{32,56},... | collective-permute-start | bytes 122888 | tf_op jit(solution)/shard_map/ppermute | solution.py:528
  13.2 9.6 %collective-permute-start.10 = (bf16[256,128]{1,0:T(8,128)(2,1)S(1)}, bf16[256,128]{1,0:T(8,128)(2,1)S(1)}, u32[]{:S(2)}, u32[]{:S(2)}) collective-permute-start(bf16[256,128]{1,0:T(8,128)(2,1)S(1)} %get-tuple-element.87), channel_id=1, source_target_pairs={{0,4},{4,0},{8,12},{12,8},{16,20},{20,16},{24,28},{28,24},{32,36},... | collective-permute-start | bytes 196616 | tf_op jit(solution)/shard_map/ppermute | solution.py:524
  14.5 7.7 %collective-permute-start.7 = (f32[80,128]{1,0:T(8,128)S(1)}, f32[80,128]{1,0:T(8,128)S(1)}, u32[]{:S(2)}, u32[]{:S(2)}) collective-permute-start(f32[80,128]{1,0:T(8,128)S(1)} %add_add_fusion.1), channel_id=1, source_target_pairs={{0,96},{4,100},{8,104},{12,108},{16,112},{20,116},{24,120},{28,124... | collective-permute-start | bytes 122888 | tf_op jit(solution)/shard_map/ppermute | solution.py:532
  34.2 8.0 %collective-permute-start.11 = (bf16[256,1024]{1,0:T(8,128)(2,1)S(1)}, bf16[256,1024]{1,0:T(8,128)(2,1)S(1)}, u32[]{:S(2)}, u32[]{:S(2)}) collective-permute-start(bf16[256,1024]{1,0:T(8,128)(2,1)S(1)} %get-tuple-element.94), channel_id=1, source_target_pairs={{0,4},{4,0},{8,12},{12,8},{16,20},{20,16},{24,28},{28,24},{32,36},... | collective-permute-start | bytes 1572872 | tf_op jit(solution)/shard_map/ppermute | solution.py:524
  37.0 31.2 %all-to-all-start = ((bf16[16,144,256]{2,1,0:T(8,128)(2,1)}), bf16[16,144,256]{2,1,0:T(8,128)(2,1)S(1)}, u32[]{:S(2)}, u32[]{:S(2)}) async-start(bf16[16,144,256]{2,1,0:T(8,128)(2,1)} %get-tuple-element.103), calls=%async_computation | async-start | bytes 2359296 | tf_op jit(solution)/shard_map/all_to_all | solution.py:547
  42.9 6.7 %collective-permute-start.13 = (bf16[304,256]{1,0:T(8,128)(2,1)S(1)}, bf16[304,256]{1,0:T(8,128)(2,1)S(1)}, u32[]{:S(2)}, u32[]{:S(2)}) collective-permute-start(bf16[304,256]{1,0:T(8,128)(2,1)S(1)} %get-tuple-element.98), channel_id=1, source_target_pairs={{0,1},{1,2},{2,3},{3,0},{4,5},{5,6},{6,7},{7,4},{8,9},{9,10},{10,1... | collective-permute-start | bytes 466952 | tf_op jit(solution)/shard_map/ppermute | solution.py:536
  44.3 9.8 %collective-permute-start.14 = (bf16[304,256]{1,0:T(8,128)(2,1)S(1)}, bf16[304,256]{1,0:T(8,128)(2,1)S(1)}, u32[]{:S(2)}, u32[]{:S(2)}) collective-permute-start(bf16[304,256]{1,0:T(8,128)(2,1)S(1)} %get-tuple-element.99), channel_id=1, source_target_pairs={{0,2},{1,3},{2,0},{3,1},{4,6},{5,7},{6,4},{7,5},{8,10},{9,11},{10,... | collective-permute-start | bytes 466952 | tf_op jit(solution)/shard_map/ppermute | solution.py:536
  46.9 7.2 %collective-permute-start.15 = (bf16[304,256]{1,0:T(8,128)(2,1)S(1)}, bf16[304,256]{1,0:T(8,128)(2,1)S(1)}, u32[]{:S(2)}, u32[]{:S(2)}) collective-permute-start(bf16[304,256]{1,0:T(8,128)(2,1)S(1)} %get-tuple-element.100), channel_id=1, source_target_pairs={{0,3},{1,0},{2,1},{3,2},{4,7},{5,4},{6,5},{7,6},{8,11},{9,8},{10,9... | collective-permute-start | bytes 466952 | tf_op jit(solution)/shard_map/ppermute | solution.py:536
  61.8 8.2 %collective-permute-start.24 = (f32[48,128]{1,0:T(8,128)S(1)}, f32[48,128]{1,0:T(8,128)S(1)}, u32[]{:S(2)}, u32[]{:S(2)}) collective-permute-start(f32[48,128]{1,0:T(8,128)S(1)} %add_add_fusion.3.refs_2_), channel_id=1, source_target_pairs={{0,24},{4,28},{8,0},{12,4},{16,8},{20,12},{24,16},{28,20},{32,56},... | collective-permute-start | bytes 73736 | tf_op jit(solution)/shard_map/ppermute | solution.py:528
  63.8 6.3 %collective-permute-start.23 = (f32[48,128]{1,0:T(8,128)S(1)}, f32[48,128]{1,0:T(8,128)S(1)}, u32[]{:S(2)}, u32[]{:S(2)}) collective-permute-start(f32[48,128]{1,0:T(8,128)S(1)} %add_add_fusion.3.refs_2_), channel_id=1, source_target_pairs={{0,16},{4,20},{8,24},{12,28},{16,0},{20,4},{24,8},{28,12},{32,48},... | collective-permute-start | bytes 73736 | tf_op jit(solution)/shard_map/ppermute | solution.py:528
  64.3 5.8 %collective-permute-start.22 = (f32[48,128]{1,0:T(8,128)S(1)}, f32[48,128]{1,0:T(8,128)S(1)}, u32[]{:S(2)}, u32[]{:S(2)}) collective-permute-start(f32[48,128]{1,0:T(8,128)S(1)} %add_add_fusion.3.refs_2_), channel_id=1, source_target_pairs={{0,8},{4,12},{8,16},{12,20},{16,24},{20,28},{24,0},{28,4},{32,40},... | collective-permute-start | bytes 73736 | tf_op jit(solution)/shard_map/ppermute | solution.py:528
  65.0 17.1 %collective-permute-start.18 = (bf16[256,256]{1,0:T(8,128)(2,1)S(1)}, bf16[256,256]{1,0:T(8,128)(2,1)S(1)}, u32[]{:S(2)}, u32[]{:S(2)}) collective-permute-start(bf16[256,256]{1,0:T(8,128)(2,1)S(1)} %add_convert_fusion.3.refs_1_), channel_id=1, source_target_pairs={{0,3},{1,0},{2,1},{3,2},{4,7},{5,4},{6,5},{7,6},{8,11},{9,8},{10,9... | collective-permute-start | bytes 393224 | tf_op jit(solution)/shard_map/ppermute | solution.py:536
  67.7 14.4 %collective-permute-start.17 = (bf16[256,256]{1,0:T(8,128)(2,1)S(1)}, bf16[256,256]{1,0:T(8,128)(2,1)S(1)}, u32[]{:S(2)}, u32[]{:S(2)}) collective-permute-start(bf16[256,256]{1,0:T(8,128)(2,1)S(1)} %add_convert_fusion.3.refs_1_), channel_id=1, source_target_pairs={{0,2},{1,3},{2,0},{3,1},{4,6},{5,7},{6,4},{7,5},{8,10},{9,11},{10,... | collective-permute-start | bytes 393224 | tf_op jit(solution)/shard_map/ppermute | solution.py:536
  69.9 12.2 %collective-permute-start.16 = (bf16[256,256]{1,0:T(8,128)(2,1)S(1)}, bf16[256,256]{1,0:T(8,128)(2,1)S(1)}, u32[]{:S(2)}, u32[]{:S(2)}) collective-permute-start(bf16[256,256]{1,0:T(8,128)(2,1)S(1)} %add_convert_fusion.3.refs_1_), channel_id=1, source_target_pairs={{0,1},{1,2},{2,3},{3,0},{4,5},{5,6},{6,7},{7,4},{8,9},{9,10},{10,1... | collective-permute-start | bytes 393224 | tf_op jit(solution)/shard_map/ppermute | solution.py:536
  70.1 30.6 %all-to-all-start.1 = ((bf16[16,144,256]{2,1,0:T(8,128)(2,1)}), bf16[16,144,256]{2,1,0:T(8,128)(2,1)S(1)}, u32[]{:S(2)}, u32[]{:S(2)}) async-start(bf16[16,144,256]{2,1,0:T(8,128)(2,1)} %experts_sum.1.refs_6_), calls=%async_computation.1 | async-start | bytes 2359296 | tf_op jit(solution)/shard_map/all_to_all | solution.py:547
  74.6 10.1 %collective-permute-start.25 = (f32[48,128]{1,0:T(8,128)S(1)}, f32[48,128]{1,0:T(8,128)S(1)}, u32[]{:S(2)}, u32[]{:S(2)}) collective-permute-start(f32[48,128]{1,0:T(8,128)S(1)} %add_add_fusion.2.refs_1_), channel_id=1, source_target_pairs={{0,4},{4,0},{8,12},{12,8},{16,20},{20,16},{24,28},{28,24},{32,36},... | collective-permute-start | bytes 73736 | tf_op jit(solution)/shard_map/ppermute | solution.py:524
  87.8 6.2 %collective-permute-start.29 = (bf16[128,512]{1,0:T(8,128)(2,1)S(1)}, bf16[128,512]{1,0:T(8,128)(2,1)S(1)}, u32[]{:S(2)}, u32[]{:S(2)}) collective-permute-start(bf16[128,512]{1,0:T(8,128)(2,1)S(1)} %add_convert_fusion.2), channel_id=1, source_target_pairs={{0,96},{4,100},{8,104},{12,108},{16,112},{20,116},{24,120},{28,124... | collective-permute-start | bytes 393224 | tf_op jit(solution)/shard_map/ppermute | solution.py:532
  90.7 6.4 %collective-permute-start.28 = (bf16[128,512]{1,0:T(8,128)(2,1)S(1)}, bf16[128,512]{1,0:T(8,128)(2,1)S(1)}, u32[]{:S(2)}, u32[]{:S(2)}) collective-permute-start(bf16[128,512]{1,0:T(8,128)(2,1)S(1)} %add_convert_fusion.2), channel_id=1, source_target_pairs={{0,64},{4,68},{8,72},{12,76},{16,80},{20,84},{24,88},{28,92},{32,9... | collective-permute-start | bytes 393224 | tf_op jit(solution)/shard_map/ppermute | solution.py:532
  91.3 9.3 %collective-permute-start.27 = (bf16[128,512]{1,0:T(8,128)(2,1)S(1)}, bf16[128,512]{1,0:T(8,128)(2,1)S(1)}, u32[]{:S(2)}, u32[]{:S(2)}) collective-permute-start(bf16[128,512]{1,0:T(8,128)(2,1)S(1)} %add_convert_fusion.2), channel_id=1, source_target_pairs={{0,32},{4,36},{8,40},{12,44},{16,48},{20,52},{24,56},{28,60},{32,6... | collective-permute-start | bytes 393224 | tf_op jit(solution)/shard_map/ppermute | solution.py:532
  101.2 8.2 %collective-permute-start.32 = (bf16[128,512]{1,0:T(8,128)(2,1)S(1)}, bf16[128,512]{1,0:T(8,128)(2,1)S(1)}, u32[]{:S(2)}, u32[]{:S(2)}) collective-permute-start(bf16[128,512]{1,0:T(8,128)(2,1)S(1)} %add_convert_fusion.1), channel_id=1, source_target_pairs={{0,24},{4,28},{8,0},{12,4},{16,8},{20,12},{24,16},{28,20},{32,56},... | collective-permute-start | bytes 393224 | tf_op jit(solution)/shard_map/ppermute | solution.py:528
  103.5 6.3 %collective-permute-start.31 = (bf16[128,512]{1,0:T(8,128)(2,1)S(1)}, bf16[128,512]{1,0:T(8,128)(2,1)S(1)}, u32[]{:S(2)}, u32[]{:S(2)}) collective-permute-start(bf16[128,512]{1,0:T(8,128)(2,1)S(1)} %add_convert_fusion.1), channel_id=1, source_target_pairs={{0,16},{4,20},{8,24},{12,28},{16,0},{20,4},{24,8},{28,12},{32,48},... | collective-permute-start | bytes 393224 | tf_op jit(solution)/shard_map/ppermute | solution.py:528
  104.1 9.2 %collective-permute-start.30 = (bf16[128,512]{1,0:T(8,128)(2,1)S(1)}, bf16[128,512]{1,0:T(8,128)(2,1)S(1)}, u32[]{:S(2)}, u32[]{:S(2)}) collective-permute-start(bf16[128,512]{1,0:T(8,128)(2,1)S(1)} %add_convert_fusion.1), channel_id=1, source_target_pairs={{0,8},{4,12},{8,16},{12,20},{16,24},{20,28},{24,0},{28,4},{32,40},... | collective-permute-start | bytes 393224 | tf_op jit(solution)/shard_map/ppermute | solution.py:528
  (21 other events, 120.1 us)

commit v7 on v6

--- a/solution.py
+++ b/solution.py
@@ -581,7 +581,7 @@
 
     pieces = chips_call(at, pieces, (msg2_z,))
     around = star(msg2, to_x)
-    pieces, *around = lax.optimization_barrier((pieces, *around))
+    pieces, *dm = lax.optimization_barrier((pieces, *dm))
     tokt, q, qslope, km, v, slope = again_call(at, tokens, keep[None, :], w_query, w_key, w_value, (pieces,))
     pieces = exchange(pieces)
 

time: 117 us -> 115 us (0.983)
  starting transfers between devices: 52.1 us -> 50.9 us
    ppermute x9, waiting for transfers between devices: 11.2 us -> 8.44 us  [to_z(): return lax.ppermute(v, 'pts', [(i, (i + 8 * d) % 32) for i in range(32)])]
    ppermute x11, starting transfers between devices: 12.6 us -> 9.88 us  [swap_core(): return lax.ppermute(v, 'pts', [(i, i ^ 1) for i in range(32)])]
    ppermute x6, waiting for transfers between devices: 6.15 us -> 8.11 us  [to_y(): return lax.ppermute(v, 'exp', [(i, (i + d) % 4) for i in range(4)])]
    all_to_all x2, starting transfers between devices: 8.37 us -> 9.82 us  [exchange(): return lax.all_to_all(v, 'pts', 0, 0, axis_index_groups=CHIPS)]
  transfers between devices with their start and end apart: 37 -> 37, of which waited for: 14 -> 14; matrix products, arithmetic and copies ran while one was open for 0% -> 0% of each run, Pallas kernels for 21% -> 22%
where the time goes in v7:
time: 115 us; the launch traced here: 114 us
  starting transfers between devices  50.9 us (44%)
  Pallas kernels  36.8 us (32%)
  waiting for transfers between devices  24.4 us (21%)
    pallas_call x14, Pallas kernels, run(): pl.pallas_call(body, in_specs=[pl.BlockSpec(memory_space=pltpu.SMEM)] + [...  33.7 us
    ppermute x9, starting transfers between devices, to_z(): return lax.ppermute(v, 'pts', [(i, (i + 8 * d) % 32) for i in range(32)])  12.5 us
    ppermute x9, starting transfers between devices, to_x(): lax.ppermute(v, 'pts', [(i, i & ~6 | i + 2 * d & 6) for i in range(32)])  10.3 us
    ppermute x11, starting transfers between devices, swap_core(): return lax.ppermute(v, 'pts', [(i, i ^ 1) for i in range(32)])  9.88 us
    all_to_all x2, starting transfers between devices, exchange(): return lax.all_to_all(v, 'pts', 0, 0, axis_index_groups=CHIPS)  9.82 us
    ppermute x9, waiting for transfers between devices, to_z(): return lax.ppermute(v, 'pts', [(i, (i + 8 * d) % 32) for i in range(32)])  8.44 us
    ppermute x6, starting transfers between devices, to_y(): return lax.ppermute(v, 'exp', [(i, (i + d) % 4) for i in range(4)])  8.44 us
    ppermute x6, waiting for transfers between devices, to_y(): return lax.ppermute(v, 'exp', [(i, (i + d) % 4) for i in range(4)])  8.11 us
  transfers between devices with their start and end apart: 37, of which 14 were waited for; matrix products, arithmetic and copies ran while one was open for 0% of the time, Pallas kernels for 22%

profile of v7, /device:TPU:1, one launch (start us, length us, event | category | flops | bytes accessed | tf_op | source)
XLA Modules:
  0.0 114.2 jit_solution(15643988387669801612)
XLA Ops:
  2.3 3.0 %keys.1 = (f32[4,1024]{1,0:T(4,128)S(1)}, f32[80,128]{1,0:T(8,128)S(1)}, bf16[256,128]{1,0:T(8,128)(2,1)S(1)}, bf16[256,128]{1,0:T(8,128)(2,1)S(1)}, bf16[256,10...) custom-call(s32[3]{0:T(128)S(1)} %pad_add_fusion.refs_0_.at_ref, bf16[1024,256]{1,0:T(8,128)(2,1)} %refs_1_.7, ...), custom_call_target="tpu_custom_call" | custom-call | flops 400000000 | bytes 3000000 | tf_op jit(solution)/shard_map/keys/pallas_call | solution.py:106
  6.7 2.6 %collective-permute-start.3 = (f32[80,128]{1,0:T(8,128)S(1)}, f32[80,128]{1,0:T(8,128)S(1)}, u32[]{:S(2)}, u32[]{:S(2)}) collective-permute-start(f32[80,128]{1,0:T(8,128)S(1)} %add.99), channel_id=1, source_target_pairs={{0,24},{4,28},{8,0},{12,4},{16,8},{20,12},{24,16},{28,20},{32,56},... | collective-permute-start | bytes 122888 | tf_op jit(solution)/shard_map/ppermute | solution.py:528
  11.3 1.9 %gate.1 = (bf16[128,2048]{1,0:T(8,128)(2,1)S(1)}, f32[8,2048]{1,0:T(8,128)S(1)}) custom-call(s32[3]{0:T(128)S(1)} %pad_add_fusion.refs_0_.at_ref, f32[3,64]{1,0:T(4,128)} %refs_1_.5, f32[1,64]{1,0:T(1,128)} %bitcast.11, f32[8,64]{1,0:T(8,128)} %bitcast.9, f32[4,1024]{1,0:T(4,128)S(1)} %get-tuple-element.75.refs_4_.refs_3_, ...), custom_call_target="tpu_custom_call" | custom-call | flops 100000000 | bytes 1000000 | tf_op jit(solution)/shard_map/gate/pallas_call | solution.py:106
  14.5 3.8 %collective-permute-start.7 = (f32[80,128]{1,0:T(8,128)S(1)}, f32[80,128]{1,0:T(8,128)S(1)}, u32[]{:S(2)}, u32[]{:S(2)}) collective-permute-start(f32[80,128]{1,0:T(8,128)S(1)} %add_add_fusion.1), channel_id=1, source_target_pairs={{0,96},{4,100},{8,104},{12,108},{16,112},{20,116},{24,120},{28,124... | collective-permute-start | bytes 122888 | tf_op jit(solution)/shard_map/ppermute | solution.py:532
  19.1 2.1 %cotangent_back.1 = (bf16[256,1024]{1,0:T(8,128)(2,1)S(1)}, bf16[256,2048]{1,0:T(8,128)(2,1)S(1)}, f32[1024,2048]{1,0:T(8,128)S(1)}, bf16[1024,256]{1,0:T(8,128)(2,1)S(1)}) custom-call(s32[3]{0:T(128)S(1)} %pad_add_fusion.refs_0_.at_ref, bf16[1024,256]{1,0:T(8,128)(2,1)S(1)} %copy-done.5, bf16[1024,256]{1,0:T(8,128)(2,1)S(1)} %collective-permute-done.8.refs_2_, ...), custom_call_target="tpu_custom_call" | custom-call | flops 1100000000 | bytes 8000000 | tf_op jit(solution)/shard_map/cotangent_back/pallas_call | solution.py:106
  22.9 10.6 %expert.1 = (f32[256,1024]{1,0:T(8,128)S(1)}, bf16[256,1024]{1,0:T(8,128)(2,1)S(1)}, f32[256,256]{1,0:T(8,128)S(1)}, f32[8,256]{1,0:T(8,128)S(1)}, f32[48,128]{1...) custom-call(s32[3]{0:T(128)S(1)} %pad_add_fusion.refs_0_.at_ref, ...), custom_call_target="tpu_custom_call" | custom-call | flops 6000000000 | bytes 12000000 | tf_op jit(solution)/shard_map/expert/pallas_call | solution.py:106
  34.2 2.8 %collective-permute-start.11 = (bf16[256,1024]{1,0:T(8,128)(2,1)S(1)}, bf16[256,1024]{1,0:T(8,128)(2,1)S(1)}, u32[]{:S(2)}, u32[]{:S(2)}) collective-permute-start(bf16[256,1024]{1,0:T(8,128)(2,1)S(1)} %get-tuple-element.96), channel_id=1, source_target_pairs={{0,4},{4,0},{8,12},{12,8},{16,20},{20,16},{24,28},{28,24},{32,36},... | collective-permute-start | bytes 1572872 | tf_op jit(solution)/shard_map/ppermute | solution.py:524
  37.0 3.9 %all-to-all-start = ((bf16[16,144,256]{2,1,0:T(8,128)(2,1)}), bf16[16,144,256]{2,1,0:T(8,128)(2,1)S(1)}, u32[]{:S(2)}, u32[]{:S(2)}) async-start(bf16[16,144,256]{2,1,0:T(8,128)(2,1)} %get-tuple-element.94), calls=%async_computation | async-start | bytes 2359296 | tf_op jit(solution)/shard_map/all_to_all | solution.py:547
  44.3 2.6 %collective-permute-start.14 = (bf16[304,256]{1,0:T(8,128)(2,1)S(1)}, bf16[304,256]{1,0:T(8,128)(2,1)S(1)}, u32[]{:S(2)}, u32[]{:S(2)}) collective-permute-start(bf16[304,256]{1,0:T(8,128)(2,1)S(1)} %get-tuple-element.101), channel_id=1, source_target_pairs={{0,2},{1,3},{2,0},{3,1},{4,6},{5,7},{6,4},{7,5},{8,10},{9,11},{10,... | collective-permute-start | bytes 466952 | tf_op jit(solution)/shard_map/ppermute | solution.py:536
  49.6 4.4 %collective-permute-done.14 = bf16[304,256]{1,0:T(8,128)(2,1)S(1)} collective-permute-done((bf16[304,256]{1,0:T(8,128)(2,1)S(1)}, bf16[304,256]{1,0:T(8,128)(2,1)S(1)}, u32[]{:S(2)}, u32[]{:S(2)}) %collective-permute-start.14) | collective-permute-done | bytes 155680 | tf_op jit(solution)/shard_map/ppermute | solution.py:536
  54.1 2.7 %collective-permute-start.18 = (f32[48,128]{1,0:T(8,128)S(1)}, f32[48,128]{1,0:T(8,128)S(1)}, u32[]{:S(2)}, u32[]{:S(2)}) collective-permute-start(f32[48,128]{1,0:T(8,128)S(1)} %convert_add_fusion), channel_id=1, source_target_pairs={{0,96},{4,100},{8,104},{12,108},{16,112},{20,116},{24,120},{28,124... | collective-permute-start | bytes 73736 | tf_op jit(solution)/shard_map/ppermute | solution.py:532
  58.0 2.7 %collective-permute-start.21 = (bf16[256,256]{1,0:T(8,128)(2,1)S(1)}, bf16[256,256]{1,0:T(8,128)(2,1)S(1)}, u32[]{:S(2)}, u32[]{:S(2)}) collective-permute-start(bf16[256,256]{1,0:T(8,128)(2,1)S(1)} %add_convert_fusion.3.refs_1_), channel_id=1, source_target_pairs={{0,3},{1,0},{2,1},{3,2},{4,7},{5,4},{6,5},{7,6},{8,11},{9,8},{10,9... | collective-permute-start | bytes 393224 | tf_op jit(solution)/shard_map/ppermute | solution.py:536
  61.8 2.2 %collective-permute-start.24 = (f32[48,128]{1,0:T(8,128)S(1)}, f32[48,128]{1,0:T(8,128)S(1)}, u32[]{:S(2)}, u32[]{:S(2)}) collective-permute-start(f32[48,128]{1,0:T(8,128)S(1)} %add_add_fusion.3.refs_2_), channel_id=1, source_target_pairs={{0,24},{4,28},{8,0},{12,4},{16,8},{20,12},{24,16},{28,20},{32,56},... | collective-permute-start | bytes 73736 | tf_op jit(solution)/shard_map/ppermute | solution.py:528
  67.3 2.0 %collective-permute-done.19.refs_2_ = bf16[256,256]{1,0:T(8,128)(2,1)S(1)} collective-permute-done((bf16[256,256]{1,0:T(8,128)(2,1)S(1)}, bf16[256,256]{1,0:T(8,128)(2,1)S(1)}, u32[]{:S(2)}, u32[]{:S(2)}) %collective-permute-start.19) | collective-permute-done | bytes 131104 | tf_op jit(solution)/shard_map/ppermute | solution.py:536
  69.3 5.9 %all-to-all-start.1 = ((bf16[16,144,256]{2,1,0:T(8,128)(2,1)}), bf16[16,144,256]{2,1,0:T(8,128)(2,1)S(1)}, u32[]{:S(2)}, u32[]{:S(2)}) async-start(bf16[16,144,256]{2,1,0:T(8,128)(2,1)} %experts_sum.1.refs_6_), calls=%async_computation.1 | async-start | bytes 2359296 | tf_op jit(solution)/shard_map/all_to_all | solution.py:547
  75.2 2.1 %collective-permute-start.25 = (f32[48,128]{1,0:T(8,128)S(1)}, f32[48,128]{1,0:T(8,128)S(1)}, u32[]{:S(2)}, u32[]{:S(2)}) collective-permute-start(f32[48,128]{1,0:T(8,128)S(1)} %add_add_fusion.2.refs_1_), channel_id=1, source_target_pairs={{0,4},{4,0},{8,12},{12,8},{16,20},{20,16},{24,28},{28,24},{32,36},... | collective-permute-start | bytes 73736 | tf_op jit(solution)/shard_map/ppermute | solution.py:524
  77.3 2.8 %queries_keys_again.1 = (bf16[256,1024]{1,0:T(8,128)(2,1)S(1)}, bf16[256,1024]{1,0:T(8,128)(2,1)S(1)}, f32[256,1024]{1,0:T(8,128)S(1)}, bf16[256,1024]{1,0:T(8,1...) custom-call(s32[3]{0:T(128)S(1)} %pad_add_fusion.refs_0_.at_ref, bf16[1024,256]{1,0:T(8,128)(2,1)} %refs_1_.7, ...), custom_call_target="tpu_custom_call" | custom-call | flops 500000000 | bytes 3000000 | tf_op jit(solution)/shard_map/queries_keys_again/pallas_call | solution.py:106
  80.1 2.5 %back_query.1 = (f32[256,1024]{1,0:T(8,128)S(1)}, f32[256,256]{1,0:T(8,128)S(1)}) custom-call(s32[3]{0:T(128)S(1)} %pad_add_fusion.refs_0_.at_ref, bf16[256,256]{1,0:T(8,128)(2,1)S(1)} %add_convert_fusion.3.refs_1_, bf16[256,256]{1,0:T(8,128)(2,1)S(1)} %collective-permute-done.19.refs_2_, bf16[256,256]{1,0:T(8,128)(2,1)S(1)} %collective-permute-done.20.refs_3_, ...), custom_call_target="tpu_custom_call" | custom-call | flops 2000000000 | bytes 5000000 | tf_op jit(solution)/shard_map/back_query/pallas_call | solution.py:106
  85.8 2.9 %collective-permute-start.29 = (bf16[128,512]{1,0:T(8,128)(2,1)S(1)}, bf16[128,512]{1,0:T(8,128)(2,1)S(1)}, u32[]{:S(2)}, u32[]{:S(2)}) collective-permute-start(bf16[128,512]{1,0:T(8,128)(2,1)S(1)} %add_convert_fusion.2), channel_id=1, source_target_pairs={{0,96},{4,100},{8,104},{12,108},{16,112},{20,116},{24,120},{28,124... | collective-permute-start | bytes 393224 | tf_op jit(solution)/shard_map/ppermute | solution.py:532
  89.9 1.8 %grad_x.1 = bf16[1024,256]{1,0:T(8,128)(2,1)} custom-call(s32[3]{0:T(128)S(1)} %pad_add_fusion.refs_0_.at_ref, f32[256,1024]{1,0:T(8,128)S(1)} %get-tuple-element.113.refs_1_, bf16[256,1024]{1,0:T(8,128)(2,1)S(1)} %get-tuple-element.118.refs_2_, bf16[256,1024]{1,0:T(8,128)(2,1)S(1)} %get-tuple-element.119.refs_3_, bf16[256,256]{1,0:T(8,128)(2,1)S(1)} %copy-done, ...), custom_call_target="tpu_custom_call" | custom-call | flops 300000000 | bytes 3000000 | tf_op jit(solution)/shard_map/grad_x/pallas_call | solution.py:106
  91.7 2.3 %collective-permute-done.29 = bf16[128,512]{1,0:T(8,128)(2,1)S(1)} collective-permute-done((bf16[128,512]{1,0:T(8,128)(2,1)S(1)}, bf16[128,512]{1,0:T(8,128)(2,1)S(1)}, u32[]{:S(2)}, u32[]{:S(2)}) %collective-permute-start.29) | collective-permute-done | bytes 131104 | tf_op jit(solution)/shard_map/ppermute | solution.py:532
  95.6 3.6 %collective-permute-done.27 = bf16[128,512]{1,0:T(8,128)(2,1)S(1)} collective-permute-done((bf16[128,512]{1,0:T(8,128)(2,1)S(1)}, bf16[128,512]{1,0:T(8,128)(2,1)S(1)}, u32[]{:S(2)}, u32[]{:S(2)}) %collective-permute-start.27) | collective-permute-done | bytes 131104 | tf_op jit(solution)/shard_map/ppermute | solution.py:532
  102.7 3.2 %place_experts.1 = (f32[2,256,1024]{2,1,0:T(8,128)}, f32[2,1024,256]{2,1,0:T(8,128)}) custom-call(s32[3]{0:T(128)S(1)} %pad_add_fusion.refs_0_.at_ref, bf16[16,144,256]{2,1,0:T(8,128)(2,1)S(1)} %all-to-all-done.1.own_ref.refs_3_, bf16[16,144,256]{2,1,0:T(8,128)(2,1)S(1)} %collective-permute-done.33.oth_ref.refs_4_), custom_call_target="tpu_custom_call" | custom-call | flops 1000000 | bytes 7000000 | tf_op jit(solution)/shard_map/place_experts/pallas_call | solution.py:477
  107.7 3.5 %collective-permute-done.30 = bf16[128,512]{1,0:T(8,128)(2,1)S(1)} collective-permute-done((bf16[128,512]{1,0:T(8,128)(2,1)S(1)}, bf16[128,512]{1,0:T(8,128)(2,1)S(1)}, u32[]{:S(2)}, u32[]{:S(2)}) %collective-permute-start.30) | collective-permute-done | bytes 131104 | tf_op jit(solution)/shard_map/ppermute | solution.py:528
  (92 shorter events, 35.4 us)
Async XLA Ops:
  0.6 17.7 %collective-permute-start.8 = (bf16[1024,256]{1,0:T(8,128)(2,1)}, bf16[1024,256]{1,0:T(8,128)(2,1)S(1)}, u32[]{:S(2)}, u32[]{:S(2)}) collective-permute-start(bf16[1024,256]{1,0:T(8,128)(2,1)} %refs_1_.6), channel_id=1, source_target_pairs={{0,4},{4,0},{8,12},{12,8},{16,20},{20,16},{24,28},{28,24},{32,36},... | collective-permute-start | bytes 1572872 | tf_op jit(solution)/shard_map/ppermute | solution.py:524
  2.1 19.1 %collective-permute-start.9 = (bf16[1024,256]{1,0:T(8,128)(2,1)}, bf16[1024,256]{1,0:T(8,128)(2,1)S(1)}, u32[]{:S(2)}, u32[]{:S(2)}) collective-permute-start(bf16[1024,256]{1,0:T(8,128)(2,1)} %refs_1_.7), channel_id=1, source_target_pairs={{0,4},{4,0},{8,12},{12,8},{16,20},{20,16},{24,28},{28,24},{32,36},... | collective-permute-start | bytes 1572872 | tf_op jit(solution)/shard_map/ppermute | solution.py:524
  6.7 6.6 %collective-permute-start.3 = (f32[80,128]{1,0:T(8,128)S(1)}, f32[80,128]{1,0:T(8,128)S(1)}, u32[]{:S(2)}, u32[]{:S(2)}) collective-permute-start(f32[80,128]{1,0:T(8,128)S(1)} %add.99), channel_id=1, source_target_pairs={{0,24},{4,28},{8,0},{12,4},{16,8},{20,12},{24,16},{28,20},{32,56},... | collective-permute-start | bytes 122888 | tf_op jit(solution)/shard_map/ppermute | solution.py:528
  13.2 9.6 %collective-permute-start.10 = (bf16[256,128]{1,0:T(8,128)(2,1)S(1)}, bf16[256,128]{1,0:T(8,128)(2,1)S(1)}, u32[]{:S(2)}, u32[]{:S(2)}) collective-permute-start(bf16[256,128]{1,0:T(8,128)(2,1)S(1)} %get-tuple-element.88), channel_id=1, source_target_pairs={{0,4},{4,0},{8,12},{12,8},{16,20},{20,16},{24,28},{28,24},{32,36},... | collective-permute-start | bytes 196616 | tf_op jit(solution)/shard_map/ppermute | solution.py:524
  14.5 7.7 %collective-permute-start.7 = (f32[80,128]{1,0:T(8,128)S(1)}, f32[80,128]{1,0:T(8,128)S(1)}, u32[]{:S(2)}, u32[]{:S(2)}) collective-permute-start(f32[80,128]{1,0:T(8,128)S(1)} %add_add_fusion.1), channel_id=1, source_target_pairs={{0,96},{4,100},{8,104},{12,108},{16,112},{20,116},{24,120},{28,124... | collective-permute-start | bytes 122888 | tf_op jit(solution)/shard_map/ppermute | solution.py:532
  34.2 8.0 %collective-permute-start.11 = (bf16[256,1024]{1,0:T(8,128)(2,1)S(1)}, bf16[256,1024]{1,0:T(8,128)(2,1)S(1)}, u32[]{:S(2)}, u32[]{:S(2)}) collective-permute-start(bf16[256,1024]{1,0:T(8,128)(2,1)S(1)} %get-tuple-element.96), channel_id=1, source_target_pairs={{0,4},{4,0},{8,12},{12,8},{16,20},{20,16},{24,28},{28,24},{32,36},... | collective-permute-start | bytes 1572872 | tf_op jit(solution)/shard_map/ppermute | solution.py:524
  37.0 28.6 %all-to-all-start = ((bf16[16,144,256]{2,1,0:T(8,128)(2,1)}), bf16[16,144,256]{2,1,0:T(8,128)(2,1)S(1)}, u32[]{:S(2)}, u32[]{:S(2)}) async-start(bf16[16,144,256]{2,1,0:T(8,128)(2,1)} %get-tuple-element.94), calls=%async_computation | async-start | bytes 2359296 | tf_op jit(solution)/shard_map/all_to_all | solution.py:547
  42.9 6.7 %collective-permute-start.13 = (bf16[304,256]{1,0:T(8,128)(2,1)S(1)}, bf16[304,256]{1,0:T(8,128)(2,1)S(1)}, u32[]{:S(2)}, u32[]{:S(2)}) collective-permute-start(bf16[304,256]{1,0:T(8,128)(2,1)S(1)} %get-tuple-element.100), channel_id=1, source_target_pairs={{0,1},{1,2},{2,3},{3,0},{4,5},{5,6},{6,7},{7,4},{8,9},{9,10},{10,1... | collective-permute-start | bytes 466952 | tf_op jit(solution)/shard_map/ppermute | solution.py:536
  44.3 9.8 %collective-permute-start.14 = (bf16[304,256]{1,0:T(8,128)(2,1)S(1)}, bf16[304,256]{1,0:T(8,128)(2,1)S(1)}, u32[]{:S(2)}, u32[]{:S(2)}) collective-permute-start(bf16[304,256]{1,0:T(8,128)(2,1)S(1)} %get-tuple-element.101), channel_id=1, source_target_pairs={{0,2},{1,3},{2,0},{3,1},{4,6},{5,7},{6,4},{7,5},{8,10},{9,11},{10,... | collective-permute-start | bytes 466952 | tf_op jit(solution)/shard_map/ppermute | solution.py:536
  46.9 7.2 %collective-permute-start.15 = (bf16[304,256]{1,0:T(8,128)(2,1)S(1)}, bf16[304,256]{1,0:T(8,128)(2,1)S(1)}, u32[]{:S(2)}, u32[]{:S(2)}) collective-permute-start(bf16[304,256]{1,0:T(8,128)(2,1)S(1)} %get-tuple-element.102), channel_id=1, source_target_pairs={{0,3},{1,0},{2,1},{3,2},{4,7},{5,4},{6,5},{7,6},{8,11},{9,8},{10,9... | collective-permute-start | bytes 466952 | tf_op jit(solution)/shard_map/ppermute | solution.py:536
  54.1 7.2 %collective-permute-start.18 = (f32[48,128]{1,0:T(8,128)S(1)}, f32[48,128]{1,0:T(8,128)S(1)}, u32[]{:S(2)}, u32[]{:S(2)}) collective-permute-start(f32[48,128]{1,0:T(8,128)S(1)} %convert_add_fusion), channel_id=1, source_target_pairs={{0,96},{4,100},{8,104},{12,108},{16,112},{20,116},{24,120},{28,124... | collective-permute-start | bytes 73736 | tf_op jit(solution)/shard_map/ppermute | solution.py:532
  58.0 6.5 %collective-permute-start.21 = (bf16[256,256]{1,0:T(8,128)(2,1)S(1)}, bf16[256,256]{1,0:T(8,128)(2,1)S(1)}, u32[]{:S(2)}, u32[]{:S(2)}) collective-permute-start(bf16[256,256]{1,0:T(8,128)(2,1)S(1)} %add_convert_fusion.3.refs_1_), channel_id=1, source_target_pairs={{0,3},{1,0},{2,1},{3,2},{4,7},{5,4},{6,5},{7,6},{8,11},{9,8},{10,9... | collective-permute-start | bytes 393224 | tf_op jit(solution)/shard_map/ppermute | solution.py:536
  60.8 6.5 %collective-permute-start.20 = (bf16[256,256]{1,0:T(8,128)(2,1)S(1)}, bf16[256,256]{1,0:T(8,128)(2,1)S(1)}, u32[]{:S(2)}, u32[]{:S(2)}) collective-permute-start(bf16[256,256]{1,0:T(8,128)(2,1)S(1)} %add_convert_fusion.3.refs_1_), channel_id=1, source_target_pairs={{0,2},{1,3},{2,0},{3,1},{4,6},{5,7},{6,4},{7,5},{8,10},{9,11},{10,... | collective-permute-start | bytes 393224 | tf_op jit(solution)/shard_map/ppermute | solution.py:536
  61.3 8.0 %collective-permute-start.19 = (bf16[256,256]{1,0:T(8,128)(2,1)S(1)}, bf16[256,256]{1,0:T(8,128)(2,1)S(1)}, u32[]{:S(2)}, u32[]{:S(2)}) collective-permute-start(bf16[256,256]{1,0:T(8,128)(2,1)S(1)} %add_convert_fusion.3.refs_1_), channel_id=1, source_target_pairs={{0,1},{1,2},{2,3},{3,0},{4,5},{5,6},{6,7},{7,4},{8,9},{9,10},{10,1... | collective-permute-start | bytes 393224 | tf_op jit(solution)/shard_map/ppermute | solution.py:536
  61.8 13.4 %collective-permute-start.24 = (f32[48,128]{1,0:T(8,128)S(1)}, f32[48,128]{1,0:T(8,128)S(1)}, u32[]{:S(2)}, u32[]{:S(2)}) collective-permute-start(f32[48,128]{1,0:T(8,128)S(1)} %add_add_fusion.3.refs_2_), channel_id=1, source_target_pairs={{0,24},{4,28},{8,0},{12,4},{16,8},{20,12},{24,16},{28,20},{32,56},... | collective-permute-start | bytes 73736 | tf_op jit(solution)/shard_map/ppermute | solution.py:528
  63.9 11.3 %collective-permute-start.23 = (f32[48,128]{1,0:T(8,128)S(1)}, f32[48,128]{1,0:T(8,128)S(1)}, u32[]{:S(2)}, u32[]{:S(2)}) collective-permute-start(f32[48,128]{1,0:T(8,128)S(1)} %add_add_fusion.3.refs_2_), channel_id=1, source_target_pairs={{0,16},{4,20},{8,24},{12,28},{16,0},{20,4},{24,8},{28,12},{32,48},... | collective-permute-start | bytes 73736 | tf_op jit(solution)/shard_map/ppermute | solution.py:528
  64.5 10.7 %collective-permute-start.22 = (f32[48,128]{1,0:T(8,128)S(1)}, f32[48,128]{1,0:T(8,128)S(1)}, u32[]{:S(2)}, u32[]{:S(2)}) collective-permute-start(f32[48,128]{1,0:T(8,128)S(1)} %add_add_fusion.3.refs_2_), channel_id=1, source_target_pairs={{0,8},{4,12},{8,16},{12,20},{16,24},{20,28},{24,0},{28,4},{32,40},... | collective-permute-start | bytes 73736 | tf_op jit(solution)/shard_map/ppermute | solution.py:528
  69.3 30.1 %all-to-all-start.1 = ((bf16[16,144,256]{2,1,0:T(8,128)(2,1)}), bf16[16,144,256]{2,1,0:T(8,128)(2,1)S(1)}, u32[]{:S(2)}, u32[]{:S(2)}) async-start(bf16[16,144,256]{2,1,0:T(8,128)(2,1)} %experts_sum.1.refs_6_), calls=%async_computation.1 | async-start | bytes 2359296 | tf_op jit(solution)/shard_map/all_to_all | solution.py:547
  75.2 7.4 %collective-permute-start.25 = (f32[48,128]{1,0:T(8,128)S(1)}, f32[48,128]{1,0:T(8,128)S(1)}, u32[]{:S(2)}, u32[]{:S(2)}) collective-permute-start(f32[48,128]{1,0:T(8,128)S(1)} %add_add_fusion.2.refs_1_), channel_id=1, source_target_pairs={{0,4},{4,0},{8,12},{12,8},{16,20},{20,16},{24,28},{28,24},{32,36},... | collective-permute-start | bytes 73736 | tf_op jit(solution)/shard_map/ppermute | solution.py:524
  85.8 8.2 %collective-permute-start.29 = (bf16[128,512]{1,0:T(8,128)(2,1)S(1)}, bf16[128,512]{1,0:T(8,128)(2,1)S(1)}, u32[]{:S(2)}, u32[]{:S(2)}) collective-permute-start(bf16[128,512]{1,0:T(8,128)(2,1)S(1)} %add_convert_fusion.2), channel_id=1, source_target_pairs={{0,96},{4,100},{8,104},{12,108},{16,112},{20,116},{24,120},{28,124... | collective-permute-start | bytes 393224 | tf_op jit(solution)/shard_map/ppermute | solution.py:532
  88.7 6.9 %collective-permute-start.28 = (bf16[128,512]{1,0:T(8,128)(2,1)S(1)}, bf16[128,512]{1,0:T(8,128)(2,1)S(1)}, u32[]{:S(2)}, u32[]{:S(2)}) collective-permute-start(bf16[128,512]{1,0:T(8,128)(2,1)S(1)} %add_convert_fusion.2), channel_id=1, source_target_pairs={{0,64},{4,68},{8,72},{12,76},{16,80},{20,84},{24,88},{28,92},{32,9... | collective-permute-start | bytes 393224 | tf_op jit(solution)/shard_map/ppermute | solution.py:532
  89.3 10.0 %collective-permute-start.27 = (bf16[128,512]{1,0:T(8,128)(2,1)S(1)}, bf16[128,512]{1,0:T(8,128)(2,1)S(1)}, u32[]{:S(2)}, u32[]{:S(2)}) collective-permute-start(bf16[128,512]{1,0:T(8,128)(2,1)S(1)} %add_convert_fusion.2), channel_id=1, source_target_pairs={{0,32},{4,36},{8,40},{12,44},{16,48},{20,52},{24,56},{28,60},{32,6... | collective-permute-start | bytes 393224 | tf_op jit(solution)/shard_map/ppermute | solution.py:532
  99.9 7.5 %collective-permute-start.32 = (bf16[128,512]{1,0:T(8,128)(2,1)S(1)}, bf16[128,512]{1,0:T(8,128)(2,1)S(1)}, u32[]{:S(2)}, u32[]{:S(2)}) collective-permute-start(bf16[128,512]{1,0:T(8,128)(2,1)S(1)} %add_convert_fusion.1), channel_id=1, source_target_pairs={{0,24},{4,28},{8,0},{12,4},{16,8},{20,12},{24,16},{28,20},{32,56},... | collective-permute-start | bytes 393224 | tf_op jit(solution)/shard_map/ppermute | solution.py:528
  102.7 8.6 %collective-permute-start.30 = (bf16[128,512]{1,0:T(8,128)(2,1)S(1)}, bf16[128,512]{1,0:T(8,128)(2,1)S(1)}, u32[]{:S(2)}, u32[]{:S(2)}) collective-permute-start(bf16[128,512]{1,0:T(8,128)(2,1)S(1)} %add_convert_fusion.1), channel_id=1, source_target_pairs={{0,8},{4,12},{8,16},{12,20},{16,24},{20,28},{24,0},{28,4},{32,40},... | collective-permute-start | bytes 393224 | tf_op jit(solution)/shard_map/ppermute | solution.py:528
  (21 other events, 116.5 us)
